TPU v7x, 128 devices: a whole 4x4x4 slice. The times are simulated.
128 devices in a mesh: ta: 16 (over x, y_lo, core), sa: 8 (over z, y_hi).
Axes of the slice: x: 4, y: 4 (y_hi: 2, y_lo: 2; y = y_hi * 2 + y_lo), z: 4, core: 2. Of those that a mesh axis runs over, the one named last changes fastest.
Arguments:
- null_vectors: bfloat16 [2, 24, 4, 3, 64, 32, 128], P(None, None, None, None, 'ta', 'sa'), may hold values from -0.15234375 to 0.15234375
- gauge_links: bfloat16 [2, 4, 3, 3, 64, 32, 128], P(None, None, None, None, 'ta', 'sa'), may hold values from -3.59375 to 3.59375
- coarse_in: float32 [16, 8, 8, 96], P('ta', 'sa'), may hold values from -6 to 6
Outputs:
- coarse_links: float32 [16, 8, 8, 5, 4608], P('ta', 'sa')
- coarse_out: float32 [16, 8, 8, 96], P('ta', 'sa')
All inputs are finite; a program needn't handle non-finite values.
Results may differ from a plain program's by a relative error of at most 0.0018.
Values may be sent and summed in bfloat16 or wider, within the bound.
No kernel may reach another device: no remote copies, remote signals or barrier semaphores. Data moves between devices by JAX's collectives and lax.ppermute only.
A program may use at most 256 MiB of HBM per device.

v0:
```python
import jax
import jax.numpy as jnp
from jax import lax
from jax.sharding import PartitionSpec as P

LAT_Y = 4
LAT_X = 32


gamma_rows = (
    ((2, 1.0, 0.0), (3, 1.0, 0.0), (0, 1.0, 0.0), (1, 1.0, 0.0)),
    ((2, 0.0, -1.0), (3, 0.0, 1.0), (0, 0.0, 1.0), (1, 0.0, -1.0)),
    ((3, -1.0, 0.0), (2, 1.0, 0.0), (1, 1.0, 0.0), (0, -1.0, 0.0)),
    ((3, 0.0, -1.0), (2, 0.0, -1.0), (1, 0.0, 1.0), (0, 0.0, 1.0)),
)
diag_shift = 1.0


def shifted_2(value, axis, steps):
    count = lax.axis_size(axis)
    pairs = [(source, (source + steps) % count) for source in range(count)]
    return lax.ppermute(value, axis, pairs)


def site_order(plane_size, width, depth):
    agg_cols = width // 4
    positions = jnp.arange(depth * plane_size, dtype=jnp.int32)
    local_count = depth * 16
    local = positions % local_count
    aggregate = positions // local_count
    agg_row = aggregate // agg_cols
    agg_col = aggregate % agg_cols
    outer_coord = local // 16
    row_inside = local // 4 % 4
    col_inside = local % 4
    return outer_coord * plane_size + (agg_row * 4 + row_inside) * width + agg_col * 4 + col_inside


def regroup(field, order, depth):
    leading = field.shape[:-3]
    plane_size = field.shape[-1]
    flat = field.reshape(leading + (depth * plane_size,))
    picked = jnp.take(flat, order, axis=-1)
    picked = picked.reshape(leading + (-1, depth * 16))
    return jnp.moveaxis(picked, -2, 0)


def color_agg(links, vectors):
    real_part = 0.0
    imag_part = 0.0
    for colour in range(3):
        link_r = links[:, 0, :, colour][:, None, None].astype(jnp.float32)
        link_i = links[:, 1, :, colour][:, None, None].astype(jnp.float32)
        vector_r = vectors[:, 0, :, :, colour][:, :, :, None].astype(jnp.float32)
        vector_i = vectors[:, 1, :, :, colour][:, :, :, None].astype(jnp.float32)
        real_part = real_part + link_r * vector_r - link_i * vector_i
        imag_part = imag_part + link_r * vector_i + link_i * vector_r
    return (real_part, imag_part)


def hop_agg(real_part, imag_part, direction):
    same_hop = jnp.stack([-0.5 * real_part, -0.5 * imag_part], axis=1).astype(jnp.bfloat16)
    rows_real = []
    rows_imag = []
    for spin in range(4):
        source, phase_r, phase_i = gamma_rows[direction][spin]
        rows_real.append(phase_r * real_part[:, :, source] - phase_i * imag_part[:, :, source])
        rows_imag.append(phase_r * imag_part[:, :, source] + phase_i * real_part[:, :, source])
    cross_hop = (
        0.5 * jnp.stack([jnp.stack(rows_real, 2), jnp.stack(rows_imag, 2)], axis=1)
    ).astype(jnp.bfloat16)
    return (same_hop, cross_hop)


def pair_product(left_side, right_side):
    return jnp.einsum(
        "arvsck,aqwsck->arvqw", left_side, right_side, preferred_element_type=jnp.float32
    )


def contract_agg(vectors, same_hop, cross_hop):
    vector_count = vectors.shape[2]
    hops = jnp.concatenate([same_hop, cross_hop], axis=2)
    row_blocks = []
    for chirality in range(2):
        spin_range = slice(2 * chirality, 2 * chirality + 2)
        product = pair_product(vectors[:, :, :, spin_range], hops[:, :, :, spin_range])
        real_part = product[..., 0, :, 0, :] + product[..., 1, :, 1, :]
        imag_part = product[..., 0, :, 1, :] - product[..., 1, :, 0, :]
        components = []
        for component in (real_part, imag_part):
            same_cols = component[..., :vector_count]
            cross_cols = component[..., vector_count:]
            if chirality == 0:
                components.append(jnp.concatenate([same_cols, cross_cols], axis=-1))
            else:
                components.append(jnp.concatenate([cross_cols, same_cols], axis=-1))
        row_blocks.append(jnp.stack(components, axis=-3))
    return jnp.concatenate(row_blocks, axis=-2)


def gram_agg(vectors):
    row_blocks = []
    for chirality in range(2):
        spin_range = slice(2 * chirality, 2 * chirality + 2)
        product = pair_product(vectors[:, :, :, spin_range], vectors[:, :, :, spin_range])
        real_part = product[..., 0, :, 0, :] + product[..., 1, :, 1, :]
        imag_part = product[..., 0, :, 1, :] - product[..., 1, :, 0, :]
        components = []
        for component in (real_part, imag_part):
            zero_block = jnp.zeros_like(component)
            if chirality == 0:
                components.append(jnp.concatenate([component, zero_block], axis=-1))
            else:
                components.append(jnp.concatenate([zero_block, component], axis=-1))
        row_blocks.append(jnp.stack(components, axis=-3))
    return jnp.concatenate(row_blocks, axis=-2)


def adjoint(blocks):
    vector_count = blocks.shape[-1] // 2
    chirality_sign = jnp.concatenate(
        [jnp.ones(vector_count, jnp.float32), -jnp.ones(vector_count, jnp.float32)]
    )
    outer_sign = chirality_sign[:, None] * chirality_sign[None, :]
    real_part = outer_sign * jnp.swapaxes(blocks[..., 0, :, :], -1, -2)
    imag_part = -outer_sign * jnp.swapaxes(blocks[..., 1, :, :], -1, -2)
    return jnp.stack([real_part, imag_part], axis=-3)


def direction_blocks(vec_agg, shifted_agg, link_agg, direction, weights):
    real_part, imag_part = color_agg(link_agg, shifted_agg)
    same_hop, cross_hop = hop_agg(real_part, imag_part, direction)
    results = []
    for weight in weights:
        operand = vec_agg * weight
        results.append(contract_agg(operand, same_hop, cross_hop))
    return results


def grid(blocks):
    return blocks.reshape((1, 1, LAT_Y // 4, LAT_X // 4) + blocks.shape[1:])


def matvec(blocks, coarse_vector):

    def times_vector(matrix, column):
        return jnp.einsum("...ij,...j->...i", matrix, column, precision=lax.Precision.HIGHEST)

    real_part = times_vector(blocks[..., 0, :, :], coarse_vector[..., 0, :]) - times_vector(
        blocks[..., 1, :, :], coarse_vector[..., 1, :]
    )
    imag_part = times_vector(blocks[..., 0, :, :], coarse_vector[..., 1, :]) + times_vector(
        blocks[..., 1, :, :], coarse_vector[..., 0, :]
    )
    return jnp.stack([real_part, imag_part], axis=-2)


def per_device(null_vectors, gauge_links, coarse_in):
    plane_size = null_vectors.shape[-1]
    full_order = site_order(plane_size, LAT_X, 16)
    vec_agg = regroup(null_vectors, full_order, 16)
    local = jnp.arange(256, dtype=jnp.int32)
    coords = (local // 64, local // 16 % 4, local // 4 % 4, local % 4)
    plane_index = jnp.arange(plane_size, dtype=jnp.int32)
    next_col = plane_index // LAT_X * LAT_X + (plane_index % LAT_X + 1) % LAT_X
    diagonal = diag_shift * gram_agg(vec_agg)
    first_t = lax.slice_in_dim(null_vectors, 0, 1, axis=4)
    first_z = lax.slice_in_dim(null_vectors, 0, 1, axis=5)
    face_t = shifted_2(first_t, "ta", -1)
    face_z = shifted_2(first_z, "sa", -1)
    ahead_t = jnp.concatenate([lax.slice_in_dim(null_vectors, 1, 4, axis=4), face_t], axis=4)
    ahead_z = jnp.concatenate([lax.slice_in_dim(null_vectors, 1, 4, axis=5), face_z], axis=5)
    link_t = None
    link_z = None
    forward = []
    for direction in range(4):
        if direction == 0:
            shifted = ahead_t
        elif direction == 1:
            shifted = ahead_z
        elif direction == 2:
            shifted = jnp.roll(null_vectors, -LAT_X, axis=-1)
        else:
            shifted = jnp.take(null_vectors, next_col, axis=-1)
        shifted_agg = regroup(shifted, full_order, 16)
        link_agg = regroup(gauge_links[:, direction], full_order, 16)
        boundary = coords[direction] == 3
        inner_weight = jnp.where(boundary, 0.0, 1.0).astype(jnp.bfloat16)
        outer_weight = jnp.where(boundary, 1.0, 0.0).astype(jnp.bfloat16)
        weights = (inner_weight, outer_weight)
        parts = direction_blocks(vec_agg, shifted_agg, link_agg, direction, weights)
        diagonal = diagonal + parts[0] + adjoint(parts[0])
        forward.append(grid(parts[1]))
    link_t = forward[0]
    link_z = forward[1]
    link_y = forward[2]
    link_x = forward[3]
    diagonal = grid(diagonal)
    coarse_blocks = jnp.stack([diagonal, link_t, link_z, link_y, link_x], axis=-4)
    reverse_y = adjoint(link_y)
    reverse_x = adjoint(link_x)
    reverse_t = adjoint(link_t)
    reverse_z = adjoint(link_z)
    coarse_vector = coarse_in.reshape(1, 1, LAT_Y // 4, LAT_X // 4, 2, -1)
    for step_number in range(2):
        result = matvec(diagonal, coarse_vector)
        ahead_coarse_t = shifted_2(coarse_vector, "ta", -1)
        result = result + matvec(link_t, ahead_coarse_t)
        result = result + shifted_2(matvec(reverse_t, coarse_vector), "ta", 1)
        ahead_coarse_z = shifted_2(coarse_vector, "sa", -1)
        result = result + matvec(link_z, ahead_coarse_z)
        result = result + shifted_2(matvec(reverse_z, coarse_vector), "sa", 1)
        result = result + matvec(link_y, jnp.roll(coarse_vector, -1, axis=2))
        result = result + jnp.roll(matvec(reverse_y, coarse_vector), 1, axis=2)
        result = result + matvec(link_x, jnp.roll(coarse_vector, -1, axis=3))
        result = result + jnp.roll(matvec(reverse_x, coarse_vector), 1, axis=3)
        coarse_vector = result
    block_size = coarse_blocks.shape[-3] * coarse_blocks.shape[-2] * coarse_blocks.shape[-1]
    return (
        coarse_blocks.reshape(1, 1, -1, 5, block_size),
        coarse_vector.reshape(1, 1, -1, coarse_in.shape[-1]),
    )


def solution(mesh):
    placed = (
        P(None, None, None, None, "ta", "sa", None),
        P(None, None, None, None, "ta", "sa", None),
        P("ta", "sa", None, None),
    )
    return jax.shard_map(
        per_device,
        mesh=mesh,
        in_specs=placed,
        out_specs=(P("ta", "sa", None, None, None), P("ta", "sa", None, None)),
        check_vma=False,
    )
```

profile of v0, /device:TPU:0, one launch (start us, length us, event | category | flops | bytes accessed | tf_op | source)
XLA Modules:
  0.0 842.8 jit_solution(7674111422610679741)
XLA Ops:
  2.0 6.8 collective-permute-start.4
  20.7 2.7 slice.1071
  23.5 15.9 %copy.474 = bf16[2,24,4,3,4,4,128]{1,4,3,2,5,0,6:T(4,128)(2,1)} copy(bf16[2,24,4,3,4,4,128]{6,5,4,3,2,1,0:T(4,128)(2,1)S(1)} %copy-done) | data formatting | bytes 4718592 | tf_op args[0]
  40.6 5.8 copy.797
  46.4 5.7 copy.793
  52.1 22.2 %gather_fusion.8 = bf16[2048,2,3,3]{3,1,2,0:T(2,128)(2,1)} fusion(bf16[2,3,3,2048]{2,0,3,1:T(2,128)(2,1)} %bitcast.1394, s32[2048]{0:T(1024)S(1)} %broadcast_clamp_fusion), kind=kCustom, calls=%fused_computation.8.clone | custom fusion | bytes 155648 | tf_op jit(solution)/shard_map/jit(_take)/gather | solution.py:43
  74.3 22.3 %gather_fusion.4 = bf16[2048,2,3,3]{3,1,2,0:T(2,128)(2,1)} fusion(bf16[2,3,3,2048]{2,0,3,1:T(2,128)(2,1)} %bitcast.1395, s32[2048]{0:T(1024)S(1)} %broadcast_clamp_fusion), kind=kCustom, calls=%fused_computation.6.clone | custom fusion | bytes 155648 | tf_op jit(solution)/shard_map/jit(_take)/gather | solution.py:43
  96.5 5.7 copy.791
  102.3 22.2 %gather_fusion.2 = bf16[2048,2,3,3]{3,1,2,0:T(2,128)(2,1)} fusion(bf16[2,3,3,2048]{2,0,3,1:T(2,128)(2,1)} %bitcast.1396, s32[2048]{0:T(1024)S(1)} %broadcast_clamp_fusion), kind=kCustom, calls=%fused_computation.1.clone | custom fusion | bytes 155648 | tf_op jit(solution)/shard_map/jit(_take)/gather | solution.py:43
  124.5 5.7 copy.795
  130.2 22.3 %gather_fusion.6 = bf16[2048,2,3,3]{3,1,2,0:T(2,128)(2,1)} fusion(bf16[2,3,3,2048]{2,0,3,1:T(2,128)(2,1)} %bitcast.1397, s32[2048]{0:T(1024)S(1)} %broadcast_clamp_fusion), kind=kCustom, calls=%fused_computation.7.clone | custom fusion | bytes 155648 | tf_op jit(solution)/shard_map/jit(_take)/gather | solution.py:43
  152.4 18.3 %broadcast_select_fusion.6 = (bf16[2048,2,3,3]{3,1,2,0:T(2,128)(2,1)}, bf16[2048,2,3,3]{3,1,2,0:T(2,128)(2,1)}, bf16[2048,2,3,3]{3,1,2,0:T(2,128)(2,1)}, bf16[2048,2,3,3]{3,1,2,0:T(2,128)(2,1)}) fusion(bf16[2048,2,3,3]{3,1,2,0:T(2,128)(2,1)} %gather_fusion.8, pred[2048]{0:T(1024)(128)(4,1)S(1)} %compare_and_fusion, bf16[2048,2,3,3]{3,1,2,0:T(2,128)(2,1)} %gather_fusion.4, ...), kind=kLoop, calls=%fused_computation.16 | loop fusion | flops 147456 | bytes 591872 | tf_op jit(solution)/shard_map/jit(_take)/select_n | solution.py:43
  170.8 4.7 copy.749
  175.5 4.7 copy.719
  180.1 4.7 copy.735
  184.8 4.7 copy.705
  190.9 19.2 %gather_fusion = bf16[128,2,24,4,3,4,4]{2,5,4,3,6,1,0:T(4,128)(2,1)} fusion(bf16[2,24,4,3,4,4,128]{1,4,3,2,5,0,6:T(4,128)(2,1)} %copy.474, s32[1024]{0:T(1024)S(1)} %pad_clamp_fusion), kind=kCustom, calls=%fused_computation.9 | custom fusion | bytes 4719104 | tf_op jit(solution)/shard_map/jit(_take)/gather | solution.py:185
  210.1 10.1 %copy.750 = bf16[2,24,4,3,4,4,128]{1,2,6,5,4,3,0:T(4,128)(2,1)S(1)} copy(bf16[2,24,4,3,4,4,128]{1,4,3,2,5,0,6:T(4,128)(2,1)} %bitcast.1383) | data formatting | bytes 4718592 | tf_op jit(solution)/shard_map/jit(_take)/gather | solution.py:185
  220.2 4.8 pad_maximum_fusion.8
  225.0 11.2 %broadcast_select_fusion.5 = bf16[2,24,4,3,2048]{1,2,4,3,0:T(4,128)(2,1)} fusion(bf16[2,24,4,3,2048]{1,2,4,3,0:T(4,128)(2,1)S(1)} %bitcast.1378, pred[2048]{0:T(1024)(128)(4,1)S(1)} %bitcast.1528), kind=kLoop, calls=%fused_computation.15 | loop fusion | flops 1179648 | bytes 4720640 | tf_op jit(solution)/shard_map/jit(_take)/select_n | solution.py:185
  240.6 2.9 slice.1030
  243.5 13.9 %copy.790 = bf16[2,24,4,3,4,4,128]{1,2,6,5,4,3,0:T(4,128)(2,1)} copy(bf16[2,24,4,3,4,4,128]{6,5,4,3,2,1,0:T(4,128)(2,1)S(1)} %copy-done) | data formatting | bytes 4718592 | tf_op jit(solution)/shard_map/reshape | solution.py:42
  270.9 19.2 %copy.796 = bf16[2,24,4,3,4,4,128]{1,2,6,5,4,3,0:T(4,128)(2,1)} copy(bf16[2,24,4,3,4,4,128]{6,5,4,3,2,1,0:T(4,128)(2,1)} %pad_maximum_fusion.8) | data formatting | bytes 4718592 | tf_op jit(solution)/shard_map/reshape | solution.py:42
  290.1 34.8 %gather_fusion.7 = bf16[2048,2,24,4,3]{2,3,4,1,0:T(4,128)(2,1)} fusion(bf16[2,24,4,3,2048]{1,2,4,3,0:T(4,128)(2,1)} %bitcast.1381, s32[2048]{0:T(1024)S(1)} %broadcast_clamp_fusion), kind=kCustom, calls=%fused_computation.4.clone | custom fusion | bytes 4726784 | tf_op jit(solution)/shard_map/jit(_take)/gather | solution.py:43
  324.8 34.7 %gather_fusion.1 = bf16[2048,2,24,4,3]{2,3,4,1,0:T(4,128)(2,1)} fusion(bf16[2,24,4,3,2048]{1,2,4,3,0:T(4,128)(2,1)} %bitcast.1379, s32[2048]{0:T(1024)S(1)} %broadcast_clamp_fusion), kind=kCustom, calls=%fused_computation.clone | custom fusion | bytes 4726784 | tf_op jit(solution)/shard_map/jit(_take)/gather | solution.py:43
  359.6 35.2 %gather_fusion.9 = bf16[2048,2,24,4,3]{2,3,4,1,0:T(4,128)(2,1)} fusion(bf16[2,24,4,3,2048]{1,2,4,3,0:T(4,128)(2,1)} %broadcast_select_fusion.5, s32[2048]{0:T(1024)S(1)} %broadcast_clamp_fusion), kind=kCustom, calls=%fused_computation.5.clone | custom fusion | bytes 4726784 | tf_op jit(solution)/shard_map/jit(_take)/gather | solution.py:43
  398.4 4.1 pad_maximum_fusion.7
  402.5 13.9 %copy.794 = bf16[2,24,4,3,4,4,128]{1,2,6,5,4,3,0:T(4,128)(2,1)} copy(bf16[2,24,4,3,4,4,128]{6,5,4,3,2,1,0:T(4,128)(2,1)S(1)} %pad_maximum_fusion.7) | data formatting | bytes 4718592 | tf_op jit(solution)/shard_map/reshape | solution.py:42
  416.4 34.8 %gather_fusion.5 = bf16[2048,2,24,4,3]{2,3,4,1,0:T(4,128)(2,1)} fusion(bf16[2,24,4,3,2048]{1,2,4,3,0:T(4,128)(2,1)} %bitcast.1382, s32[2048]{0:T(1024)S(1)} %broadcast_clamp_fusion), kind=kCustom, calls=%fused_computation.3.clone | custom fusion | bytes 4726784 | tf_op jit(solution)/shard_map/jit(_take)/gather | solution.py:43
  451.2 3.1 pad_maximum_fusion.6
  454.3 13.9 %copy.792 = bf16[2,24,4,3,4,4,128]{1,2,6,5,4,3,0:T(4,128)(2,1)} copy(bf16[2,24,4,3,4,4,128]{6,5,4,3,2,1,0:T(4,128)(2,1)S(1)} %pad_maximum_fusion.6) | data formatting | bytes 4718592 | tf_op jit(solution)/shard_map/reshape | solution.py:42
  468.2 34.8 %gather_fusion.3 = bf16[2048,2,24,4,3]{2,3,4,1,0:T(4,128)(2,1)} fusion(bf16[2,24,4,3,2048]{1,2,4,3,0:T(4,128)(2,1)} %bitcast.1380, s32[2048]{0:T(1024)S(1)} %broadcast_clamp_fusion), kind=kCustom, calls=%fused_computation.2.clone | custom fusion | bytes 4726784 | tf_op jit(solution)/shard_map/jit(_take)/gather | solution.py:43
  503.0 45.6 %broadcast_select_fusion = (bf16[2048,2,24,4,3]{2,3,4,1,0:T(4,128)(2,1)}, bf16[2048,2,24,4,3]{2,3,4,1,0:T(4,128)(2,1)}, bf16[2048,2,24,4,3]{2,3,4,1,0:T(4,128)(2...) fusion(bf16[2048,2,24,4,3]{2,3,4,1,0:T(4,128)(2,1)} %gather_fusion.9, ...), kind=kLoop, calls=%fused_computation.10 | loop fusion | flops 5898240 | bytes 23595008 | tf_op jit(solution)/shard_map/jit(_take)/select_n | solution.py:43
  548.6 16.6 %copy.330 = bf16[2,24,4,3,8,256]{5,1,2,3,0,4:T(8,128)(2,1)S(1)} copy(bf16[2,24,4,3,8,256]{1,2,3,0,5,4:T(4,128)(2,1)} %bitcast.1377) | data formatting | bytes 4718592 | tf_op jit(solution)/shard_map/reshape | solution.py:44
  569.8 12.6 %copy.751 = bf16[2,24,4,3,8,256]{5,4,1,3,2,0:T(8,128)(2,1)S(1)} copy(bf16[2,24,4,3,8,256]{1,2,3,0,5,4:T(4,128)(2,1)} %bitcast.1376) | data formatting | bytes 4718592 | tf_op jit(solution)/shard_map/reshape | solution.py:44
  584.6 3.1 multiply_convert_fusion.1
  587.8 3.2 multiply_subtract_fusion
  591.0 12.6 %copy.708 = bf16[2,24,4,3,8,256]{5,4,1,3,2,0:T(8,128)(2,1)S(1)} copy(bf16[2,24,4,3,8,256]{1,2,3,0,5,4:T(4,128)(2,1)} %bitcast.1375) | data formatting | bytes 4718592 | tf_op jit(solution)/shard_map/reshape | solution.py:44
  605.8 3.1 multiply_convert_fusion.5
  608.9 3.3 multiply_subtract_fusion.3
  612.2 13.1 %copy.722 = bf16[2,24,4,3,8,256]{5,4,1,3,2,0:T(8,128)(2,1)S(1)} copy(bf16[2,24,4,3,8,256]{1,2,3,0,5,4:T(4,128)(2,1)} %bitcast.1374) | data formatting | bytes 4718592 | tf_op jit(solution)/shard_map/reshape | solution.py:44
  627.5 2.9 fusion.4
  630.4 3.2 multiply_subtract_fusion.2
  633.6 12.6 %copy.738 = bf16[2,24,4,3,8,256]{5,4,1,3,2,0:T(8,128)(2,1)S(1)} copy(bf16[2,24,4,3,8,256]{1,2,3,0,5,4:T(4,128)(2,1)} %bitcast.1373) | data formatting | bytes 4718592 | tf_op jit(solution)/shard_map/reshape | solution.py:44
  648.5 2.9 multiply_convert_fusion.3
  827.0 4.2 collective-permute-start.8
  831.2 3.3 collective-permute-start.6
  838.3 3.5 collective-permute-done.9
  (566 shorter events, 228.5 us)
Async XLA Ops:
  2.0 807.9 %collective-permute-start.4 = (f32[1,1,1,8,2,48]{5,4,3,2,1,0:T(2,128)}, f32[1,1,1,8,2,48]{5,4,3,2,1,0:T(2,128)}, u32[]{:S(2)}, u32[]{:S(2)}) collective-permute-start(f32[1,1,1,8,2,48]{5,4,3,2,1,0:T(2,128)} %reshape.2347), channel_id=1, source_target_pairs={{0,7},{1,0},{2,1},{3,2},{4,3},{5,4},{6,5},{7,6},{8,15},{9,8},{10,9... | collective-permute-start | bytes 9224 | tf_op jit(solution)/shard_map/ppermute | solution.py:22
  8.7 793.6 %collective-permute-start.2 = (f32[1,1,1,8,2,48]{5,4,3,2,1,0:T(2,128)}, f32[1,1,1,8,2,48]{5,4,3,2,1,0:T(2,128)}, u32[]{:S(2)}, u32[]{:S(2)}) collective-permute-start(f32[1,1,1,8,2,48]{5,4,3,2,1,0:T(2,128)} %reshape.2347), channel_id=1, source_target_pairs={{0,120},{8,0},{16,8},{24,16},{32,24},{40,32},{48,40},{56,48},{64,5... | collective-permute-start | bytes 9224 | tf_op jit(solution)/shard_map/ppermute | solution.py:22
  12.8 7.9 copy-start
  12.9 438.4 %collective-permute-start = (bf16[2,24,4,3,1,4,128]{6,5,4,3,2,1,0:T(4,128)(2,1)}, bf16[2,24,4,3,1,4,128]{6,5,4,3,2,1,0:T(4,128)(2,1)S(1)}, u32[]{:S(2)}, u32[]{:S(2)}) collective-permute-start(bf16[2,24,4,3,1,4,128]{6,5,4,3,2,1,0:T(4,128)(2,1)} %slice.990), channel_id=1, source_target_pairs={{0,120},{8,0},{16,8},{24,16},{32,24},{40,32},{48,40},{56,48},{64,5... | collective-permute-start | bytes 1769480 | tf_op jit(solution)/shard_map/ppermute | solution.py:22
  17.5 378.9 %collective-permute-start.1 = (bf16[2,24,4,3,4,1,128]{6,1,5,4,3,2,0:T(8,128)(2,1)}, bf16[2,24,4,3,4,1,128]{6,1,5,4,3,2,0:T(8,128)(2,1)}, u32[]{:S(2)}, u32[]{:S(2)}) collective-permute-start(bf16[2,24,4,3,4,1,128]{6,1,5,4,3,2,0:T(8,128)(2,1)} %copy.801), channel_id=1, source_target_pairs={{0,7},{1,0},{2,1},{3,2},{4,3},{5,4},{6,5},{7,6},{8,15},{9,8},{10,9... | collective-permute-start | bytes 1769480 | tf_op jit(solution)/shard_map/ppermute | solution.py:22
  23.5 15.9 %copy-start.89 = (f32[48]{0:T(128)S(1)}, f32[48]{0:T(128)}, u32[]{:S(2)}) copy-start(f32[48]{0:T(128)} %constant.240.clone.1) | copy-start | bytes 580
  39.4 218.0 %copy-start.10 = (f32[48,48]{0,1:T(8,128)}, f32[48,48]{0,1:T(8,128)S(1)}, u32[]{:S(2)}) copy-start(f32[48,48]{0,1:T(8,128)S(1)} %get-tuple-element.275) | copy-start | bytes 27652
  39.4 218.7 %copy-start.12 = (f32[48,48]{0,1:T(8,128)}, f32[48,48]{0,1:T(8,128)S(1)}, u32[]{:S(2)}) copy-start(f32[48,48]{0,1:T(8,128)S(1)} %get-tuple-element.276) | copy-start | bytes 27652
  210.0 10.1 %copy-start.1 = (bf16[2,24,4,3,4,4,96]{6,5,4,3,2,1,0:T(4,128)(2,1)S(1)}, bf16[2,24,4,3,4,4,96]{6,5,4,3,2,1,0:T(4,128)(2,1)}, u32[]{:S(2)}) copy-start(bf16[2,24,4,3,4,4,96]{6,5,4,3,2,1,0:T(4,128)(2,1)} %slice.1071) | copy-start | bytes 5308420
  243.5 15.3 %copy-start.67 = (f32[8,3,256]{2,0,1:T(8,128)S(1)}, f32[8,3,256]{2,0,1:T(8,128)}, u32[]{:S(2)}) copy-start(f32[8,3,256]{2,0,1:T(8,128)} %get-tuple-element.240) | copy-start | bytes 73732
  243.5 15.3 %copy-start.66 = (f32[8,3,256]{2,0,1:T(8,128)S(1)}, f32[8,3,256]{2,0,1:T(8,128)}, u32[]{:S(2)}) copy-start(f32[8,3,256]{2,0,1:T(8,128)} %get-tuple-element.241) | copy-start | bytes 73732
  243.5 15.3 %copy-start.65 = (f32[8,3,256]{2,0,1:T(8,128)S(1)}, f32[8,3,256]{2,0,1:T(8,128)}, u32[]{:S(2)}) copy-start(f32[8,3,256]{2,0,1:T(8,128)} %get-tuple-element.242) | copy-start | bytes 73732
  243.5 15.4 %copy-start.64 = (f32[8,3,256]{2,0,1:T(8,128)S(1)}, f32[8,3,256]{2,0,1:T(8,128)}, u32[]{:S(2)}) copy-start(f32[8,3,256]{2,0,1:T(8,128)} %get-tuple-element.243) | copy-start | bytes 73732
  243.5 15.4 %copy-start.63 = (f32[8,3,256]{2,0,1:T(8,128)S(1)}, f32[8,3,256]{2,0,1:T(8,128)}, u32[]{:S(2)}) copy-start(f32[8,3,256]{2,0,1:T(8,128)} %get-tuple-element.244) | copy-start | bytes 73732
  565.2 4.6 copy-start.2
  671.9 13.4 %copy-start.7 = (f32[8,24,4,3,256]{4,1,2,3,0:T(8,128)S(1)}, f32[8,24,4,3,256]{4,1,2,3,0:T(8,128)}, u32[]{:S(2)}) copy-start(f32[8,24,4,3,256]{4,1,2,3,0:T(8,128)} %get-tuple-element.7) | copy-start | bytes 7077892
  673.5 4.8 copy-start.13
  673.5 11.9 %copy-start.6 = (f32[8,24,4,3,256]{4,1,2,3,0:T(8,128)S(1)}, f32[8,24,4,3,256]{4,1,2,3,0:T(8,128)}, u32[]{:S(2)}) copy-start(f32[8,24,4,3,256]{4,1,2,3,0:T(8,128)} %get-tuple-element.6) | copy-start | bytes 7077892
  692.7 6.0 copy-start.60
  692.7 6.0 copy-start.68
  692.7 11.6 %copy-start.15 = (bf16[8,2,24,4,3,256]{5,2,3,4,1,0:T(8,128)(2,1)S(1)}, bf16[8,2,24,4,3,256]{5,2,3,4,1,0:T(8,128)(2,1)}, u32[]{:S(2)}) copy-start(bf16[8,2,24,4,3,256]{5,2,3,4,1,0:T(8,128)(2,1)} %copy-done.14) | copy-start | bytes 7077892
  706.0 9.1 %copy-start.5 = (f32[8,24,4,3,256]{4,1,2,3,0:T(8,128)S(1)}, f32[8,24,4,3,256]{4,1,2,3,0:T(8,128)}, u32[]{:S(2)}) copy-start(f32[8,24,4,3,256]{4,1,2,3,0:T(8,128)} %get-tuple-element.15) | copy-start | bytes 7077892
  707.5 7.6 copy-start.4
  753.4 6.8 copy-start.30
  771.6 5.7 copy-start.47
  771.6 7.6 copy-start.61
  771.6 7.6 copy-start.62
  781.0 6.0 copy-start.75
  781.1 6.0 copy-start.76
  781.1 6.0 copy-start.73
  781.1 6.0 copy-start.74
  781.1 6.1 copy-start.79
  781.1 6.1 copy-start.80
  781.1 6.2 copy-start.77
  781.1 6.2 copy-start.78
  787.1 29.9 %collective-permute-start.3 = (f32[1,1,1,8,2,48]{5,3,4,2,1,0:T(8,128)S(1)}, f32[1,1,1,8,2,48]{5,3,4,2,1,0:T(8,128)S(1)}, u32[]{:S(2)}, u32[]{:S(2)}) collective-permute-start(f32[1,1,1,8,2,48]{5,3,4,2,1,0:T(8,128)S(1)} %pad_maximum_fusion.27), channel_id=1, source_target_pairs={{0,8},{8,16},{16,24},{24,32},{32,40},{40,48},{48,56},{56,64},{64,7... | collective-permute-start | bytes 9224 | tf_op jit(solution)/shard_map/ppermute | solution.py:22
  787.3 29.8 %collective-permute-start.5 = (f32[1,1,1,8,2,48]{5,3,4,2,1,0:T(8,128)S(1)}, f32[1,1,1,8,2,48]{5,3,4,2,1,0:T(8,128)S(1)}, u32[]{:S(2)}, u32[]{:S(2)}) collective-permute-start(f32[1,1,1,8,2,48]{5,3,4,2,1,0:T(8,128)S(1)} %pad_maximum_fusion.28), channel_id=1, source_target_pairs={{0,1},{1,2},{2,3},{3,4},{4,5},{5,6},{6,7},{7,0},{8,9},{9,10},{10,1... | collective-permute-start | bytes 9224 | tf_op jit(solution)/shard_map/ppermute | solution.py:22
  797.7 4.5 copy-start.87
  797.8 4.6 copy-start.69
  797.8 4.6 copy-start.70
  797.8 4.6 copy-start.85
  797.8 4.6 copy-start.86
  799.0 7.9 copy-start.31
  801.2 5.9 copy-start.32
  827.0 7.8 collective-permute-start.8
  831.2 5.3 collective-permute-start.6
  834.5 7.3 collective-permute-start.9
  834.7 7.2 collective-permute-start.7
  (57 other events, 137.4 us)
where the time goes:
time: 851 us; the launch traced here: 843 us
  local copies, waits for them, and re-layouts  562 us (66%)
  other arithmetic  165 us (19%)
  matrix products  87.2 us (10%)
  starting transfers between devices  21.2 us (2%)
    gather x9, local copies, waits for them, and re-layouts, regroup(): picked = jnp.take(flat, order, axis=-1)  263 us
    reshape x9, local copies, waits for them, and re-layouts, regroup(): picked = picked.reshape(leading + (-1, depth * 16))  86.3 us
    select_n x2, other arithmetic, regroup(): picked = jnp.take(flat, order, axis=-1)  63.9 us
    reshape x4, local copies, waits for them, and re-layouts, regroup(): flat = field.reshape(leading + (depth * plane_size,))  60.8 us
    dot_general x72, matrix products, times_vector(): jnp.einsum('...ij,...j->...i', matrix, column, precision=lax.Precision.HI...  60.6 us
    gather x2, local copies, waits for them, and re-layouts, per_device(): shifted = jnp.take(null_vectors, next_col, axis=-1)  29.3 us
    unnamed x197, local copies, waits for them, and re-layouts  28 us
    dot_general x18, matrix products, pair_product(): jnp.einsum('arvsck,aqwsck->arvqw', left_side, right_side, preferred_eleme...  26.6 us
  transfers between devices with their start and end apart: 10, of which 1 were waited for; matrix products, arithmetic and copies ran while one was open for 94% of the time, Pallas kernels for 0%

commit v1 on v0

v1 whole, which is shorter than its diff:
```python
import jax
import jax.numpy as jnp
from jax import lax
from jax.experimental import pallas as pl
from jax.experimental.pallas import tpu as pltpu
from jax.sharding import PartitionSpec as P

NV = 24
ROWS = 48
F32 = jnp.float32
BF16 = jnp.bfloat16


def lane_ids(rows):
    return lax.broadcasted_iota(jnp.int32, (rows, 128), 1)


def roll(value, shift):
    return pltpu.roll(value, shift % 128, 1)


def exchange(planes):
    rows = planes[0].shape[0]
    lanes = lane_ids(rows)
    for bit in range(3):
        step = 4 << bit
        chosen = (lanes & step) != 0
        out = [None] * 8
        for low in range(8):
            if low >> bit & 1:
                continue
            high = low | 1 << bit
            out[low] = jnp.where(chosen, roll(planes[high], step), planes[low])
            out[high] = jnp.where(chosen, planes[high], roll(planes[low], -step))
        planes = out
    return planes


def colour(link, vector):
    out = []
    for c in range(3):
        real = imag = None
        for d in range(3):
            lr, li = link[(c * 3 + d) * 2], link[(c * 3 + d) * 2 + 1]
            vr, vi = vector[d * 2], vector[d * 2 + 1]
            re, im = lr * vr - li * vi, lr * vi + li * vr
            real = re if real is None else real + re
            imag = im if imag is None else imag + im
        out.append((real, imag))
    return out


def nt(a, b):
    return lax.dot_general(a, b, (((1,), (1,)), ((), ())), preferred_element_type=F32)


def variants(plain):
    second = (lane_ids(plain.shape[0]) & 16) != 0
    swapped = jnp.where(second, roll(plain, 16), roll(plain, -16))
    return (
        plain,
        jnp.where(second, -plain, plain),
        swapped,
        jnp.where(second, swapped, -swapped),
    )


def inner_kernel(
    v_ref, u_ref, out_ref, lt_ref, lz_ref, ut_ref, uz_ref, vf, vm, uf, cm, flat
):
    flat[...] = jnp.zeros_like(flat)

    @pl.loop(0, 4)
    def _(mu):
        for c in range(3):
            for d in range(3):
                for ri in range(2):
                    row = ((c * 3 + d) * 2 + ri) * 16
                    flat[0, pl.ds(row, 16), :] = 0.5 * u_ref[ri, mu, c, d].astype(F32)

        lanes = lane_ids(24)
        drop = ((lanes & 12) == 12) & (mu == 1)
        for t in range(4):
            z_planes = [flat[0, pl.ds(t * 4 + z, 24, stride=16), :] for z in range(4)]
            for a, value in enumerate(exchange(z_planes + z_planes)):
                uf[a, mu, t] = jnp.where(drop, 0.0, value)

        @pl.when(mu == 1)
        def _():
            t_planes = [flat[0, pl.ds(t * 4 + 3, 24, stride=16), :] for t in range(4)]
            for a, value in enumerate(exchange(t_planes + t_planes)):
                uz_ref[a] = value

    for a in range(8):
        ut_ref[a] = uf[a, 0, 3]

    @pl.loop(0, 6)
    def _(step):
        chi, c = step // 3, step % 3
        for sb in range(2):
            for ri in range(2):
                block = v_ref[ri, :, 2 * chi + sb, c].astype(F32)
                flat[sb, pl.ds(ri * 384, 384), :] = block.reshape(384, 128)
        for t in range(4):
            planes = [
                flat[sb, pl.ds(t * 4 + z, ROWS, stride=16), :] for sb in range(2) for z in range(4)
            ]
            column = pl.multiple_of((t * 3 + c) * 128, 128)
            for a, value in enumerate(exchange(planes)):
                vf[a, chi, t, c] = value
                for kind, operand in enumerate(variants(value)):
                    vm[kind, a, chi, :, pl.ds(column, 128)] = operand.astype(BF16)
        planes = [
            flat[sb, pl.ds(t * 4 + 3, ROWS, stride=16), :] for sb in range(2) for t in range(4)
        ]
        column = pl.multiple_of(c * 128, 128)
        for a, value in enumerate(exchange(planes)):
            both = variants(value)
            lz_ref[0, a, chi, :, pl.ds(column, 128)] = both[0].astype(BF16)
            lz_ref[1, a, chi, :, pl.ds(column, 128)] = both[1].astype(BF16)

    for a in range(8):
        for chi in range(2):
            lt_ref[a, chi] = vm[0, a, chi, :, 9 * 128 :]

    cm[...] = jnp.zeros_like(cm)

    @pl.loop(0, 8)
    def _(a):
        ahead = (a + 1) % 8
        lanes = lane_ids(24)
        x_last = (lanes & 3) == 3
        y_last = lanes >= 96
        blocks = []
        for chi in range(2):
            for t in range(4):
                for mu in range(4):
                    if mu == 0 and t == 3:
                        continue
                    link = [uf[a, mu, t, pl.ds(k, 1), :] for k in range(18)]
                    vector = []
                    for d in range(3):
                        for ri in range(2):
                            rows = pl.ds(ri * 24, 24)
                            if mu == 0:
                                value = vf[a, chi, t + 1, d, rows, :]
                            else:
                                value = vf[a, chi, t, d, rows, :]
                            if mu == 1:
                                value = roll(value, -4)
                            elif mu == 2:
                                value = roll(value, -32)
                            elif mu == 3:
                                other = vf[ahead, chi, t, d, rows, :]
                                value = jnp.where(x_last, roll(other, 3), roll(value, -1))
                            vector.append(value)
                    for c, parts in enumerate(colour(link, vector)):
                        column = slice((t * 3 + c) * 128, (t * 3 + c + 1) * 128)
                        for ri in range(2):
                            if mu < 2:
                                row = ri * 64 + mu * 32
                                cm[0, row : row + 24, column] = parts[ri].astype(BF16)
                            else:
                                last = y_last if mu == 2 else x_last
                                full = parts[ri]
                                outer = jnp.where(last, -full, 0.0)
                                row = ri * 64
                                cm[mu - 1, row : row + 24, column] = full.astype(BF16)
                                cm[mu - 1, row + 32 : row + 56, column] = outer.astype(BF16)
            near, far = vm[0, a, chi], vm[0, a, 1 - chi]
            tz = nt(jnp.concatenate([near, far, vm[1, a, 1 - chi]], 0), cm[0])
            y = nt(jnp.concatenate([near, vm[3, a, 1 - chi]], 0), cm[1])
            x = nt(jnp.concatenate([near, vm[2, a, 1 - chi]], 0), cm[2])
            gram = nt(near, near)
            blocks.append((tz, y, x, gram))
        combine_inner(blocks, a, out_ref)


def complex_of(product, sign):
    return product[:24] + sign * roll(product[24:], 64)


def times_i(value, sign):
    return -sign * roll(value, 64)


def combine_inner(blocks, a, out_ref):
    sign = sides()
    second = (lane_ids(NV) & 32) != 0
    upper = {}
    for chi, (tz, y, x, gram) in enumerate(blocks):
        phase = 1.0 if chi == 0 else -1.0
        z_tz = complex_of(tz[:48], sign)
        z_y = complex_of(y[:48], sign)
        z_x = complex_of(x[:48], sign)
        cross_t = complex_of(tz[48:96], sign)
        cross_z = phase * times_i(complex_of(tz[96:144], sign), sign)
        cross_y = phase * complex_of(y[48:96], sign)
        cross_x = phase * times_i(complex_of(x[48:96], sign), sign)
        same = -(z_tz + z_y + z_x)
        cross = jnp.where(second, cross_z, cross_t) + cross_y + cross_x
        same = same + roll(same, -32)
        cross = cross + roll(cross, -32)
        gram = jnp.concatenate([gram, jnp.zeros((ROWS, 128 - ROWS), F32)], 1)
        gram_r = gram[:24] + roll(gram[24:], -24)
        gram_i = roll(gram[:24], -24) - gram[24:]
        y_same, y_cross = roll(z_y, -32), -roll(cross_y, -32)
        x_same, x_cross = roll(z_x, -32), -roll(cross_x, -32)
        upper[chi, chi] = (same, y_same, x_same, gram_r, gram_i)
        upper[1 - chi, chi] = (cross, y_cross, x_cross, None, None)

    def whole(item, ri):
        return placed([[upper[row, col][item] for col in range(2)] for row in range(2)], ri)

    first_rows = lax.broadcasted_iota(jnp.int32, (ROWS, 128), 0) < NV
    cols = lane_ids(ROWS)
    flip = jnp.where(first_rows == (cols < NV), 1.0, -1.0).astype(F32)
    zero = jnp.zeros((NV, 128), F32)
    for ri in range(2):
        out_ref[a, 1, ri] = whole(1, ri)
        out_ref[a, 2, ri] = whole(2, ri)
        inner = whole(0, ri)
        turned = jnp.concatenate([inner, jnp.zeros((80, 128), F32)], 0).T[:ROWS]
        turned = flip * turned if ri == 0 else -flip * turned
        gram = [[upper[0, 0][3 + ri], zero], [zero, upper[1, 1][3 + ri]]]
        out_ref[a, 0, ri] = placed(gram, 0) + inner + turned


def placed(parts, ri):
    lanes = lane_ids(NV)
    left, right = lanes < NV, (lanes >= NV) & (lanes < 2 * NV)
    rows = []
    for row in range(2):
        second = jnp.where(right, roll(parts[row][1], NV - 64 * ri), 0.0)
        rows.append(jnp.where(left, roll(parts[row][0], -64 * ri), second))
    return jnp.concatenate(rows, 0)


def sides():
    return jnp.where(lane_ids(NV) < 64, 1.0, -1.0).astype(F32)


def inner_call(vectors, links):
    shape = jax.ShapeDtypeStruct
    vmem = pl.BlockSpec(memory_space=pltpu.VMEM)
    return pl.pallas_call(
        inner_kernel,
        out_shape=(
            shape((8, 3, 2, ROWS, 128), F32),
            shape((8, 2, ROWS, 384), BF16),
            shape((2, 8, 2, ROWS, 384), BF16),
            shape((8, 24, 128), F32),
            shape((8, 24, 128), F32),
        ),
        in_specs=[vmem] * 2,
        out_specs=(vmem,) * 5,
        scratch_shapes=[
            pltpu.VMEM((8, 2, 4, 3, ROWS, 128), F32),
            pltpu.VMEM((4, 8, 2, ROWS, 1536), BF16),
            pltpu.VMEM((8, 4, 4, 24, 128), F32),
            pltpu.VMEM((3, 128, 1536), BF16),
            pltpu.VMEM((2, 768, 128), F32),
        ],
        compiler_params=pltpu.CompilerParams(vmem_limit_bytes=56 * 1024 * 1024),
        cost_estimate=pl.CostEstimate(
            flops=40_000_000_000, bytes_accessed=6_000_000, transcendentals=0
        ),
        name="inner",
    )(vectors, links)


def face_kernel(v_ref, t_ref, z_ref, flat):
    @pl.loop(0, 6)
    def _(step):
        chi, c = step // 3, step % 3
        for sb in range(2):
            for ri in range(2):
                block = v_ref[ri, :, 2 * chi + sb, c].astype(F32)
                flat[sb, pl.ds(ri * 384, 384), :] = block.reshape(384, 128)
        column = pl.multiple_of(c * 128, 128)
        for out, stride in ((t_ref, 1), (z_ref, 4)):
            planes = [
                flat[sb, pl.ds(q * stride, ROWS, stride=16), :] for sb in range(2) for q in range(4)
            ]
            for a, value in enumerate(exchange(planes)):
                out[a, chi, :, pl.ds(column, 128)] = value.astype(BF16)


def face_call(vectors):
    face = jax.ShapeDtypeStruct((8, 2, ROWS, 384), BF16)
    vmem = pl.BlockSpec(memory_space=pltpu.VMEM)
    return pl.pallas_call(
        face_kernel,
        out_shape=(face, face),
        in_specs=[vmem],
        out_specs=(vmem, vmem),
        scratch_shapes=[pltpu.VMEM((2, 768, 128), F32)],
        compiler_params=pltpu.CompilerParams(vmem_limit_bytes=24 * 1024 * 1024),
        name="faces",
    )(vectors)


def outer_kernel(ft_ref, fz_ref, lt_ref, lz_ref, ut_ref, uz_ref, out_ref, cm):
    cm[...] = jnp.zeros_like(cm)

    @pl.loop(0, 8)
    def _(a):
        sign = sides()
        parts = ([[None, None], [None, None]], [[None, None], [None, None]])
        for chi in range(2):
            phase = 1.0 if chi == 0 else -1.0
            for mu, (face, links) in enumerate(((ft_ref, ut_ref), (fz_ref, uz_ref))):
                link = [links[a, pl.ds(k, 1), :] for k in range(18)]
                vector = []
                for d in range(3):
                    value = face[a, chi, :, d * 128 : (d + 1) * 128].astype(F32)
                    vector += [value[:NV], value[NV:]]
                for c, both in enumerate(colour(link, vector)):
                    column = slice(c * 128, (c + 1) * 128)
                    cm[mu, 0:24, column] = both[0].astype(BF16)
                    cm[mu, 64:88, column] = both[1].astype(BF16)
                if mu == 0:
                    left = jnp.concatenate([lt_ref[a, chi], lt_ref[a, 1 - chi]], 0)
                else:
                    left = jnp.concatenate([lz_ref[0, a, chi], lz_ref[1, a, 1 - chi]], 0)
                product = nt(left, cm[mu])
                cross = complex_of(product[ROWS:], sign)
                if mu == 1:
                    cross = phase * times_i(cross, sign)
                parts[mu][chi][chi] = -complex_of(product[:ROWS], sign)
                parts[mu][1 - chi][chi] = cross
        for mu in range(2):
            for ri in range(2):
                out_ref[a, mu, ri] = placed(parts[mu], ri)


def outer_call(face_t, face_z, left_t, left_z, link_t, link_z):
    vmem = pl.BlockSpec(memory_space=pltpu.VMEM)
    return pl.pallas_call(
        outer_kernel,
        out_shape=jax.ShapeDtypeStruct((8, 2, 2, ROWS, 128), F32),
        in_specs=[vmem] * 6,
        out_specs=vmem,
        scratch_shapes=[pltpu.VMEM((2, 128, 384), BF16)],
        compiler_params=pltpu.CompilerParams(vmem_limit_bytes=24 * 1024 * 1024),
        name="outer",
    )(face_t, face_z, left_t, left_z, link_t, link_z)


def signs():
    rows = lax.broadcasted_iota(jnp.int32, (ROWS, 128), 0)
    return jnp.where(rows < NV, 1.0, -1.0).astype(F32), jnp.where(lane_ids(1) < NV, 1.0, -1.0).astype(F32)


def split(row):
    keep = lane_ids(1) < ROWS
    return jnp.where(keep, row, 0.0), jnp.where(keep, roll(row, -ROWS), 0.0)


def joined(real, imag):
    lanes = lane_ids(1)
    low, high = lanes < ROWS, (lanes >= ROWS) & (lanes < 2 * ROWS)
    return jnp.where(low, real, jnp.where(high, roll(imag, ROWS), 0.0))


def forward(block, row):
    pr, pi = split(row)
    br, bi = block
    return br * pr - bi * pi, br * pi + bi * pr


def column_of(row, eye):
    return jnp.sum(jnp.where(eye, row, 0.0), axis=1, keepdims=True)


def row_of(column, eye):
    return jnp.sum(jnp.where(eye, column, 0.0), axis=0, keepdims=True)


def backward(block, column_r, column_i, col_sign):
    br, bi = block
    real = jnp.sum(br * column_r + bi * column_i, axis=0, keepdims=True)
    imag = jnp.sum(br * column_i - bi * column_r, axis=0, keepdims=True)
    return joined(col_sign * real, col_sign * imag)


def eye_mask():
    rows = lax.broadcasted_iota(jnp.int32, (ROWS, 128), 0)
    return rows == lane_ids(ROWS)


def local_apply(inner, outer, vec, part_ref, bt_ref, bz_ref):
    eye = eye_mask()
    row_sign, col_sign = signs()
    part_ref[...] = jnp.zeros_like(part_ref)

    @pl.loop(0, 8)
    def _(a):
        own = vec[pl.ds(a, 1), :]
        ahead = (a + 1) % 8
        nxt = vec[pl.ds(ahead, 1), :]
        block = lambda ref, slot: (ref[a, slot, 0], ref[a, slot, 1])
        f0 = forward(block(inner, 0), own)
        f1 = forward(block(inner, 1), own)
        f2 = forward(block(inner, 2), nxt)
        real = jnp.sum(f0[0] + f1[0] + f2[0], axis=1, keepdims=True)
        imag = jnp.sum(f0[1] + f1[1] + f2[1], axis=1, keepdims=True)
        pr, pi = split(own)
        column_r = row_sign * column_of(pr, eye)
        column_i = row_sign * column_of(pi, eye)
        back_y = backward(block(inner, 1), column_r, column_i, col_sign)
        back_x = backward(block(inner, 2), column_r, column_i, col_sign)
        bt_ref[pl.ds(a, 1), :] = backward(block(outer, 0), column_r, column_i, col_sign)
        bz_ref[pl.ds(a, 1), :] = backward(block(outer, 1), column_r, column_i, col_sign)
        part_ref[pl.ds(a, 1), :] += joined(row_of(real, eye), row_of(imag, eye)) + back_y
        part_ref[pl.ds(ahead, 1), :] += back_x


def ahead_apply(outer, vt, vz, part_ref):
    eye = eye_mask()

    @pl.loop(0, 8)
    def _(a):
        ft = forward((outer[a, 0, 0], outer[a, 0, 1]), vt[pl.ds(a, 1), :])
        fz = forward((outer[a, 1, 0], outer[a, 1, 1]), vz[pl.ds(a, 1), :])
        real = jnp.sum(ft[0] + fz[0], axis=1, keepdims=True)
        imag = jnp.sum(ft[1] + fz[1], axis=1, keepdims=True)
        part_ref[pl.ds(a, 1), :] += joined(row_of(real, eye), row_of(imag, eye))


def first_kernel(inner, outer, vec, vt, vz, part_ref, bt_ref, bz_ref):
    local_apply(inner, outer, vec, part_ref, bt_ref, bz_ref)
    ahead_apply(outer, vt, vz, part_ref)


def second_kernel(inner, outer, part, rt, rz, vec_ref, part_ref, bt_ref, bz_ref):
    vec_ref[...] = part[...] + rt[...] + rz[...]
    local_apply(inner, outer, vec_ref, part_ref, bt_ref, bz_ref)


def last_kernel(outer, part, rt, rz, vt, vz, out_ref):
    out_ref[...] = part[...] + rt[...] + rz[...]
    ahead_apply(outer, vt, vz, out_ref)


def small_call(kernel, count, name, *args):
    vmem = pl.BlockSpec(memory_space=pltpu.VMEM)
    row = jax.ShapeDtypeStruct((8, 128), F32)
    return pl.pallas_call(
        kernel,
        out_shape=(row,) * count,
        in_specs=[vmem] * len(args),
        out_specs=(vmem,) * count,
        compiler_params=pltpu.CompilerParams(vmem_limit_bytes=24 * 1024 * 1024),
        name=name,
    )(*args)


def shifted(value, axis, steps):
    count = lax.axis_size(axis)
    return lax.ppermute(value, axis, [(k, (k + steps) % count) for k in range(count)])


def per_device(null_vectors, gauge_links, coarse_in):
    vectors = null_vectors.reshape(2, NV, 4, 3, 16, 128)
    links = gauge_links.reshape(2, 4, 3, 3, 16, 128)
    vec = jnp.pad(coarse_in.reshape(8, 2 * ROWS), ((0, 0), (0, 32)))
    face_t, face_z = face_call(vectors)
    face_z = shifted(face_z, "sa", -1)
    face_t = shifted(face_t, "ta", -1)
    vec_t, vec_z = shifted(vec, "ta", -1), shifted(vec, "sa", -1)
    inner, left_t, left_z, link_t, link_z = inner_call(vectors, links)
    outer = outer_call(face_t, face_z, left_t, left_z, link_t, link_z)
    part, bt, bz = small_call(first_kernel, 3, "first", inner, outer, vec, vec_t, vec_z)
    rt, rz = shifted(bt, "ta", 1), shifted(bz, "sa", 1)
    once, part, bt, bz = small_call(second_kernel, 4, "second", inner, outer, part, rt, rz)
    rt, rz = shifted(bt, "ta", 1), shifted(bz, "sa", 1)
    vec_t, vec_z = shifted(once, "ta", -1), shifted(once, "sa", -1)
    (twice,) = small_call(last_kernel, 1, "last", outer, part, rt, rz, vec_t, vec_z)
    blocks = jnp.concatenate([inner[:, :1], outer, inner[:, 1:]], 1)[..., :ROWS]
    return blocks.reshape(1, 1, 8, 5, 2 * ROWS * ROWS), twice[:, : 2 * ROWS].reshape(1, 1, 8, 2 * ROWS)


def solution(mesh):
    placed_sites = P(None, None, None, None, "ta", "sa", None)
    return jax.shard_map(
        per_device,
        mesh=mesh,
        in_specs=(placed_sites, placed_sites, P("ta", "sa", None, None)),
        out_specs=(P("ta", "sa", None, None, None), P("ta", "sa", None, None)),
        check_vma=False,
    )
```

time: 851 us -> 84.1 us (0.10)
  local copies, waits for them, and re-layouts: 562 us -> 12.1 us
  other arithmetic: 165 us -> 0.15 us
  matrix products: 87.2 us -> 0 us
  Pallas kernels: 0 us -> 45.9 us
    gather x11 -> x0, local copies, waits for them, and re-layouts: 293 us -> none  [the longest x9 263 us: regroup(): picked = jnp.take(flat, order, axis=-1)]
    reshape x15 -> x3, local copies, waits for them, and re-layouts: 149 us -> 5.54 us  [the longest x2 4.94 us: per_device(): blocks.reshape(1, 1, 8, 5, 2 * ROWS * ROWS)]
    dot_general x90 -> x0, matrix products: 87.2 us -> none  [the longest x72 60.6 us: times_vector(): jnp.einsum('...ij,...j->...i', matrix, column, precision=lax.Precision.HI...]
    select_n x4 -> x0, other arithmetic: 75.1 us -> none  [the longest x2 63.9 us: regroup(): picked = jnp.take(flat, order, axis=-1)]
    pallas_call x0 -> x6, Pallas kernels: none -> 45.9 us  [the longest x1 30.7 us: inner_call(): pl.pallas_call(inner_kernel, out_shape=(shape((8, 3, 2, ROWS, 128), F32),...]
    another operation x15 -> x0, local copies, waits for them, and re-layouts: 30.2 us -> none  [the longest x4 22.9 us: regroup(): flat = field.reshape(leading + (depth * plane_size,))]
    concatenate x24 -> x1, other arithmetic: 29.2 us -> 0.15 us  [per_device(): blocks = jnp.concatenate([inner[:, :1], outer, inner[:, 1:]], 1)[..., :ROWS]]
    slice x36 -> x2, local copies, waits for them, and re-layouts: 23.8 us -> 0.08 us  [per_device(): blocks = jnp.concatenate([inner[:, :1], outer, inner[:, 1:]], 1)[..., :ROWS]]
  transfers between devices with their start and end apart: 10 -> 10, of which waited for: 1 -> 2; matrix products, arithmetic and copies ran while one was open for 94% -> 6% of each run, Pallas kernels for 0% -> 46%
where the time goes in v1:
time: 84.1 us; the launch traced here: 83.8 us
  Pallas kernels  45.9 us (55%)
  starting transfers between devices  19.7 us (23%)
  local copies, waits for them, and re-layouts  12.1 us (14%)
  waiting for transfers between devices  5.1 us (6%)
    pallas_call x1, Pallas kernels, inner_call(): pl.pallas_call(inner_kernel, out_shape=(shape((8, 3, 2, ROWS, 128), F32),...  30.7 us
    ppermute x10, starting transfers between devices, shifted(): lax.ppermute(value, axis, [(k, (k + steps) % count) for k in range(count)])  19.7 us
    pallas_call x3, Pallas kernels, small_call(): pl.pallas_call(kernel, out_shape=(row,) * count, in_specs=[vmem] * len(ar...  7.7 us
    unnamed x12, local copies, waits for them, and re-layouts  5.78 us
    ppermute x10, waiting for transfers between devices, shifted(): lax.ppermute(value, axis, [(k, (k + steps) % count) for k in range(count)])  5.1 us
    pallas_call x1, Pallas kernels, outer_call(): pl.pallas_call(outer_kernel, out_shape=jax.ShapeDtypeStruct((8, 2, 2, ROW...  5.1 us
    reshape x2, local copies, waits for them, and re-layouts, per_device(): blocks.reshape(1, 1, 8, 5, 2 * ROWS * ROWS)  4.94 us
    pallas_call x1, Pallas kernels, face_call(): pl.pallas_call(face_kernel, out_shape=(face, face), in_specs=[vmem], out_...  2.41 us
  transfers between devices with their start and end apart: 10, of which 2 were waited for; matrix products, arithmetic and copies ran while one was open for 6% of the time, Pallas kernels for 46%

profile of v1, /device:TPU:0, one launch (start us, length us, event | category | flops | bytes accessed | tf_op | source)
XLA Modules:
  0.0 83.8 jit_solution(5874028224764117184)
XLA Ops:
  0.6 0.7 pad.4.vec
  1.3 3.3 %collective-permute-start.2 = (f32[8,128]{1,0:T(8,128)S(1)}, f32[8,128]{1,0:T(8,128)S(1)}, u32[]{:S(2)}, u32[]{:S(2)}) collective-permute-start(f32[8,128]{1,0:T(8,128)S(1)} %pad.4.vec), channel_id=1, source_target_pairs={{0,120},{8,0},{16,8},{24,16},{32,24},{40,32},{48,40},{56,48},{64,5... | collective-permute-start | bytes 12296 | tf_op jit(solution)/shard_map/ppermute | solution.py:461
  4.6 6.4 %collective-permute-start.3 = (f32[8,128]{1,0:T(8,128)S(1)}, f32[8,128]{1,0:T(8,128)S(1)}, u32[]{:S(2)}, u32[]{:S(2)}) collective-permute-start(f32[8,128]{1,0:T(8,128)S(1)} %pad.4.vec), channel_id=1, source_target_pairs={{0,7},{1,0},{2,1},{3,2},{4,3},{5,4},{6,5},{7,6},{8,15},{9,8},{10,9... | collective-permute-start | bytes 12296 | tf_op jit(solution)/shard_map/ppermute | solution.py:461
  11.0 0.0 copy-start.1
  11.0 1.7 %copy-done.1 = bf16[2,24,4,3,4,4,128]{6,5,4,3,2,1,0:T(4,128)(2,1)S(1)} copy-done((bf16[2,24,4,3,4,4,128]{6,5,4,3,2,1,0:T(4,128)(2,1)S(1)}, bf16[2,24,4,3,4,4,128]{6,5,4,3,2,1,0:T(4,128)(2,1)}, u32[]{:S(2)}) %copy-start.1) | copy-done | bytes 2359320
  12.7 2.4 %faces.1 = (bf16[8,2,48,384]{3,2,1,0:T(8,128)(2,1)S(1)}, bf16[8,2,48,384]{3,2,1,0:T(8,128)(2,1)S(1)}) custom-call(bf16[2,24,4,3,16,128]{5,4,3,2,1,0:T(8,128)(2,1)S(1)} %bitcast.8), custom_call_target="tpu_custom_call" | custom-call | tf_op jit(solution)/shard_map/faces/pallas_call | solution.py:292
  15.1 0.1 collective-permute-start
  15.2 1.6 %collective-permute-start.1 = (bf16[8,2,48,384]{3,2,1,0:T(8,128)(2,1)S(1)}, bf16[8,2,48,384]{3,2,1,0:T(8,128)(2,1)S(1)}, u32[]{:S(2)}, u32[]{:S(2)}) collective-permute-start(bf16[8,2,48,384]{3,2,1,0:T(8,128)(2,1)S(1)} %get-tuple-element.18), channel_id=1, source_target_pairs={{0,7},{1,0},{2,1},{3,2},{4,3},{5,4},{6,5},{7,6},{8,15},{9,8},{10,9... | collective-permute-start | bytes 1769480 | tf_op jit(solution)/shard_map/ppermute | solution.py:461
  16.8 30.7 %inner.1 = (f32[8,3,2,48,128]{4,3,2,1,0:T(8,128)}, bf16[8,2,48,384]{3,2,1,0:T(8,128)(2,1)}, bf16[2,8,2,48,384]{4,3,2,1,0:T(8,128)(2,1)}, f32[8,24,128]{2,1,0:T(8,128)}, f32[8,24,128]{2,1,0:T(8,128)}) custom-call(bf16[2,24,4,3,16,128]{5,4,3,2,1,0:T(8,128)(2,1)} %bitcast.7, bf16[2,4,3,3,16,128]{5,4,3,2,1,0:T(8,128)(2,1)} %bitcast.10), custom_call_target="tpu_custom_call" | custom-call | flops 40000000000 | bytes 6000000 | tf_op jit(solution)/shard_map/inner/pallas_call | solution.py:246
  47.5 0.0 collective-permute-done.ft_ref
  47.5 0.0 collective-permute-done.1.fz_ref
  47.5 0.0 copy-start.2
  47.5 1.3 %copy-done.2 = bf16[2,8,2,48,384]{4,3,2,1,0:T(8,128)(2,1)S(1)} copy-done((bf16[2,8,2,48,384]{4,3,2,1,0:T(8,128)(2,1)S(1)}, bf16[2,8,2,48,384]{4,3,2,1,0:T(8,128)(2,1)}, u32[]{:S(2)}) %copy-start.2) | copy-done | bytes 1179672
  48.8 0.0 copy-start.3
  48.8 1.1 %copy-done.3 = bf16[8,2,48,384]{3,2,1,0:T(8,128)(2,1)S(1)} copy-done((bf16[8,2,48,384]{3,2,1,0:T(8,128)(2,1)S(1)}, bf16[8,2,48,384]{3,2,1,0:T(8,128)(2,1)}, u32[]{:S(2)}) %copy-start.3) | copy-done | bytes 589848
  49.8 0.0 copy-start.4
  49.8 0.9 %copy-done.4 = f32[8,24,128]{2,1,0:T(8,128)S(1)} copy-done((f32[8,24,128]{2,1,0:T(8,128)S(1)}, f32[8,24,128]{2,1,0:T(8,128)}, u32[]{:S(2)}) %copy-start.4) | copy-done | bytes 98328
  50.7 0.0 copy-start.5
  50.7 0.9 %copy-done.5 = f32[8,24,128]{2,1,0:T(8,128)S(1)} copy-done((f32[8,24,128]{2,1,0:T(8,128)S(1)}, f32[8,24,128]{2,1,0:T(8,128)}, u32[]{:S(2)}) %copy-start.5) | copy-done | bytes 98328
  51.6 0.0 copy-start
  51.6 5.1 %outer.1 = f32[8,2,2,48,128]{4,3,2,1,0:T(8,128)S(1)} custom-call(bf16[8,2,48,384]{3,2,1,0:T(8,128)(2,1)S(1)} %collective-permute-done.ft_ref, bf16[8,2,48,384]{3,2,1,0:T(8,128)(2,1)S(1)} %collective-permute-done.1.fz_ref, bf16[8,2,48,384]{3,2,1,0:T(8,128)(2,1)S(1)} %copy-done.3, bf16[2,8,2,48,384]{4,3,2,1,0:T(8,128)(2,1)S(1)} %copy-done.2, ...), custom_call_target="tpu_custom_call" | custom-call | tf_op jit(solution)/shard_map/outer/pallas_call | solution.py:339
  56.7 0.0 collective-permute-done.2.vt
  56.7 0.0 collective-permute-done.3.vz
  56.8 0.0 copy-done
  56.8 3.8 %first.1 = (f32[8,128]{1,0:T(8,128)S(1)}, f32[8,128]{1,0:T(8,128)S(1)}, f32[8,128]{1,0:T(8,128)S(1)}) custom-call(f32[8,3,2,48,128]{4,3,2,1,0:T(8,128)S(1)} %copy-done, f32[8,2,2,48,128]{4,3,2,1,0:T(8,128)S(1)} %outer.1, f32[8,128]{1,0:T(8,128)S(1)} %pad.4.vec, f32[8,128]{1,0:T(8,128)S(1)} %collective-permute-done.2.vt, f32[8,128]{1,0:T(8,128)S(1)} %collective-permute-done.3.vz), custom_call_target="tpu_custom_call" | custom-call | tf_op jit(solution)/shard_map/first/pallas_call | solution.py:449
  60.6 0.0 collective-permute-start.4
  60.6 2.1 %collective-permute-start.5 = (f32[8,128]{1,0:T(8,128)S(1)}, f32[8,128]{1,0:T(8,128)S(1)}, u32[]{:S(2)}, u32[]{:S(2)}) collective-permute-start(f32[8,128]{1,0:T(8,128)S(1)} %get-tuple-element.25), channel_id=1, source_target_pairs={{0,1},{1,2},{2,3},{3,4},{4,5},{5,6},{6,7},{7,0},{8,9},{9,10},{10,1... | collective-permute-start | bytes 12296 | tf_op jit(solution)/shard_map/ppermute | solution.py:461
  62.8 0.1 slice.13
  62.9 2.9 %collective-permute-done.4.rt = f32[8,128]{1,0:T(8,128)S(1)} collective-permute-done((f32[8,128]{1,0:T(8,128)S(1)}, f32[8,128]{1,0:T(8,128)S(1)}, u32[]{:S(2)}, u32[]{:S(2)}) %collective-permute-start.4) | collective-permute-done | bytes 4128 | tf_op jit(solution)/shard_map/ppermute | solution.py:461
  65.8 2.2 %collective-permute-done.5.rz = f32[8,128]{1,0:T(8,128)S(1)} collective-permute-done((f32[8,128]{1,0:T(8,128)S(1)}, f32[8,128]{1,0:T(8,128)S(1)}, u32[]{:S(2)}, u32[]{:S(2)}) %collective-permute-start.5) | collective-permute-done | bytes 4128 | tf_op jit(solution)/shard_map/ppermute | solution.py:461
  67.9 2.0 %second.1 = (f32[8,128]{1,0:T(8,128)S(1)}, f32[8,128]{1,0:T(8,128)S(1)}, f32[8,128]{1,0:T(8,128)S(1)}, f32[8,128]{1,0:T(8,128)S(1)}) custom-call(f32[8,3,2,48,128]{4,3,2,1,0:T(8,128)S(1)} %copy-done, f32[8,2,2,48,128]{4,3,2,1,0:T(8,128)S(1)} %outer.1, f32[8,128]{1,0:T(8,128)S(1)} %get-tuple-element.23.part, f32[8,128]{1,0:T(8,128)S(1)} %collective-permute-done.4.rt, ...), custom_call_target="tpu_custom_call" | custom-call | tf_op jit(solution)/shard_map/second/pallas_call | solution.py:449
  69.9 2.7 %collective-permute-start.8 = (f32[8,128]{1,0:T(8,128)S(1)}, f32[8,128]{1,0:T(8,128)S(1)}, u32[]{:S(2)}, u32[]{:S(2)}) collective-permute-start(f32[8,128]{1,0:T(8,128)S(1)} %get-tuple-element.29), channel_id=1, source_target_pairs={{0,120},{8,0},{16,8},{24,16},{32,24},{40,32},{48,40},{56,48},{64,5... | collective-permute-start | bytes 12296 | tf_op jit(solution)/shard_map/ppermute | solution.py:461
  72.6 0.6 collective-permute-start.9
  73.2 0.0 collective-permute-start.6
  73.2 2.9 %collective-permute-start.7 = (f32[8,128]{1,0:T(8,128)S(1)}, f32[8,128]{1,0:T(8,128)S(1)}, u32[]{:S(2)}, u32[]{:S(2)}) collective-permute-start(f32[8,128]{1,0:T(8,128)S(1)} %get-tuple-element.28), channel_id=1, source_target_pairs={{0,1},{1,2},{2,3},{3,4},{4,5},{5,6},{6,7},{7,0},{8,9},{9,10},{10,1... | collective-permute-start | bytes 12296 | tf_op jit(solution)/shard_map/ppermute | solution.py:461
  76.1 0.2 pad_maximum_fusion
  76.3 2.4 %reshape.24 = f32[1,1,8,5,4608]{4,3,2,1,0:T(8,128)} reshape(f32[8,5,2,48,48]{4,3,2,1,0:T(8,128)S(1)} %pad_maximum_fusion) | data formatting | bytes 1474560 | tf_op jit(solution)/shard_map/reshape | solution.py:481
  78.7 2.6 %copy.7 = f32[1,1,8,5,4608]{4,2,3,1,0:T(8,128)} copy(f32[1,1,8,5,4608]{4,3,2,1,0:T(8,128)} %reshape.24) | data formatting | bytes 1474560 | tf_op jit(solution)/shard_map/reshape | solution.py:481
  81.2 0.0 collective-permute-done.6.rt
  81.2 0.0 collective-permute-done.7.rz
  81.2 0.0 collective-permute-done.8.vt
  81.2 0.0 collective-permute-done.9.vz
  81.3 1.9 %last.1 = f32[8,128]{1,0:T(8,128)S(1)} custom-call(f32[8,2,2,48,128]{4,3,2,1,0:T(8,128)S(1)} %outer.1, f32[8,128]{1,0:T(8,128)S(1)} %get-tuple-element.26.part, f32[8,128]{1,0:T(8,128)S(1)} %collective-permute-done.6.rt, f32[8,128]{1,0:T(8,128)S(1)} %collective-permute-done.7.rz, f32[8,128]{1,0:T(8,128)S(1)} %collective-permute-done.8.vt, ...), custom_call_target="tpu_custom_call" | custom-call | tf_op jit(solution)/shard_map/last/pallas_call | solution.py:449
  83.1 0.6 slice_bitcast_fusion
  (1 shorter events, 0.0 us)
Async XLA Ops:
  1.3 55.4 %collective-permute-start.2 = (f32[8,128]{1,0:T(8,128)S(1)}, f32[8,128]{1,0:T(8,128)S(1)}, u32[]{:S(2)}, u32[]{:S(2)}) collective-permute-start(f32[8,128]{1,0:T(8,128)S(1)} %pad.4.vec), channel_id=1, source_target_pairs={{0,120},{8,0},{16,8},{24,16},{32,24},{40,32},{48,40},{56,48},{64,5... | collective-permute-start | bytes 12296 | tf_op jit(solution)/shard_map/ppermute | solution.py:461
  4.6 52.1 %collective-permute-start.3 = (f32[8,128]{1,0:T(8,128)S(1)}, f32[8,128]{1,0:T(8,128)S(1)}, u32[]{:S(2)}, u32[]{:S(2)}) collective-permute-start(f32[8,128]{1,0:T(8,128)S(1)} %pad.4.vec), channel_id=1, source_target_pairs={{0,7},{1,0},{2,1},{3,2},{4,3},{5,4},{6,5},{7,6},{8,15},{9,8},{10,9... | collective-permute-start | bytes 12296 | tf_op jit(solution)/shard_map/ppermute | solution.py:461
  11.0 1.7 %copy-start.1 = (bf16[2,24,4,3,4,4,128]{6,5,4,3,2,1,0:T(4,128)(2,1)S(1)}, bf16[2,24,4,3,4,4,128]{6,5,4,3,2,1,0:T(4,128)(2,1)}, u32[]{:S(2)}) copy-start(bf16[2,24,4,3,4,4,128]{6,5,4,3,2,1,0:T(4,128)(2,1)} %param.3) | copy-start | bytes 7077892
  15.1 32.4 %collective-permute-start = (bf16[8,2,48,384]{3,2,1,0:T(8,128)(2,1)S(1)}, bf16[8,2,48,384]{3,2,1,0:T(8,128)(2,1)S(1)}, u32[]{:S(2)}, u32[]{:S(2)}) collective-permute-start(bf16[8,2,48,384]{3,2,1,0:T(8,128)(2,1)S(1)} %get-tuple-element.17), channel_id=1, source_target_pairs={{0,120},{8,0},{16,8},{24,16},{32,24},{40,32},{48,40},{56,48},{64,5... | collective-permute-start | bytes 1769480 | tf_op jit(solution)/shard_map/ppermute | solution.py:461
  15.2 32.3 %collective-permute-start.1 = (bf16[8,2,48,384]{3,2,1,0:T(8,128)(2,1)S(1)}, bf16[8,2,48,384]{3,2,1,0:T(8,128)(2,1)S(1)}, u32[]{:S(2)}, u32[]{:S(2)}) collective-permute-start(bf16[8,2,48,384]{3,2,1,0:T(8,128)(2,1)S(1)} %get-tuple-element.18), channel_id=1, source_target_pairs={{0,7},{1,0},{2,1},{3,2},{4,3},{5,4},{6,5},{7,6},{8,15},{9,8},{10,9... | collective-permute-start | bytes 1769480 | tf_op jit(solution)/shard_map/ppermute | solution.py:461
  47.5 1.3 %copy-start.2 = (bf16[2,8,2,48,384]{4,3,2,1,0:T(8,128)(2,1)S(1)}, bf16[2,8,2,48,384]{4,3,2,1,0:T(8,128)(2,1)}, u32[]{:S(2)}) copy-start(bf16[2,8,2,48,384]{4,3,2,1,0:T(8,128)(2,1)} %get-tuple-element.20.lz_ref) | copy-start | bytes 3538948
  48.8 1.1 %copy-start.3 = (bf16[8,2,48,384]{3,2,1,0:T(8,128)(2,1)S(1)}, bf16[8,2,48,384]{3,2,1,0:T(8,128)(2,1)}, u32[]{:S(2)}) copy-start(bf16[8,2,48,384]{3,2,1,0:T(8,128)(2,1)} %get-tuple-element.19.lt_ref) | copy-start | bytes 1769476
  49.8 0.9 %copy-start.4 = (f32[8,24,128]{2,1,0:T(8,128)S(1)}, f32[8,24,128]{2,1,0:T(8,128)}, u32[]{:S(2)}) copy-start(f32[8,24,128]{2,1,0:T(8,128)} %get-tuple-element.21.ut_ref) | copy-start | bytes 294916
  50.7 0.9 %copy-start.5 = (f32[8,24,128]{2,1,0:T(8,128)S(1)}, f32[8,24,128]{2,1,0:T(8,128)}, u32[]{:S(2)}) copy-start(f32[8,24,128]{2,1,0:T(8,128)} %get-tuple-element.22.uz_ref) | copy-start | bytes 294916
  51.6 5.1 %copy-start = (f32[8,3,2,48,128]{4,3,2,1,0:T(8,128)S(1)}, f32[8,3,2,48,128]{4,3,2,1,0:T(8,128)}, u32[]{:S(2)}) copy-start(f32[8,3,2,48,128]{4,3,2,1,0:T(8,128)} %get-tuple-element.16.inner) | copy-start | bytes 3538948
  60.6 5.2 %collective-permute-start.4 = (f32[8,128]{1,0:T(8,128)S(1)}, f32[8,128]{1,0:T(8,128)S(1)}, u32[]{:S(2)}, u32[]{:S(2)}) collective-permute-start(f32[8,128]{1,0:T(8,128)S(1)} %get-tuple-element.24), channel_id=1, source_target_pairs={{0,8},{8,16},{16,24},{24,32},{32,40},{40,48},{48,56},{56,64},{64,7... | collective-permute-start | bytes 12296 | tf_op jit(solution)/shard_map/ppermute | solution.py:461
  60.6 7.3 %collective-permute-start.5 = (f32[8,128]{1,0:T(8,128)S(1)}, f32[8,128]{1,0:T(8,128)S(1)}, u32[]{:S(2)}, u32[]{:S(2)}) collective-permute-start(f32[8,128]{1,0:T(8,128)S(1)} %get-tuple-element.25), channel_id=1, source_target_pairs={{0,1},{1,2},{2,3},{3,4},{4,5},{5,6},{6,7},{7,0},{8,9},{9,10},{10,1... | collective-permute-start | bytes 12296 | tf_op jit(solution)/shard_map/ppermute | solution.py:461
  69.9 11.3 %collective-permute-start.8 = (f32[8,128]{1,0:T(8,128)S(1)}, f32[8,128]{1,0:T(8,128)S(1)}, u32[]{:S(2)}, u32[]{:S(2)}) collective-permute-start(f32[8,128]{1,0:T(8,128)S(1)} %get-tuple-element.29), channel_id=1, source_target_pairs={{0,120},{8,0},{16,8},{24,16},{32,24},{40,32},{48,40},{56,48},{64,5... | collective-permute-start | bytes 12296 | tf_op jit(solution)/shard_map/ppermute | solution.py:461
  72.6 8.6 %collective-permute-start.9 = (f32[8,128]{1,0:T(8,128)S(1)}, f32[8,128]{1,0:T(8,128)S(1)}, u32[]{:S(2)}, u32[]{:S(2)}) collective-permute-start(f32[8,128]{1,0:T(8,128)S(1)} %get-tuple-element.29), channel_id=1, source_target_pairs={{0,7},{1,0},{2,1},{3,2},{4,3},{5,4},{6,5},{7,6},{8,15},{9,8},{10,9... | collective-permute-start | bytes 12296 | tf_op jit(solution)/shard_map/ppermute | solution.py:461
  73.2 8.0 %collective-permute-start.6 = (f32[8,128]{1,0:T(8,128)S(1)}, f32[8,128]{1,0:T(8,128)S(1)}, u32[]{:S(2)}, u32[]{:S(2)}) collective-permute-start(f32[8,128]{1,0:T(8,128)S(1)} %get-tuple-element.27), channel_id=1, source_target_pairs={{0,8},{8,16},{16,24},{24,32},{32,40},{40,48},{48,56},{56,64},{64,7... | collective-permute-start | bytes 12296 | tf_op jit(solution)/shard_map/ppermute | solution.py:461
  73.2 8.0 %collective-permute-start.7 = (f32[8,128]{1,0:T(8,128)S(1)}, f32[8,128]{1,0:T(8,128)S(1)}, u32[]{:S(2)}, u32[]{:S(2)}) collective-permute-start(f32[8,128]{1,0:T(8,128)S(1)} %get-tuple-element.28), channel_id=1, source_target_pairs={{0,1},{1,2},{2,3},{3,4},{4,5},{5,6},{6,7},{7,0},{8,9},{9,10},{10,1... | collective-permute-start | bytes 12296 | tf_op jit(solution)/shard_map/ppermute | solution.py:461

commit v2 on v1

--- a/solution.py
+++ b/solution.py
@@ -19,21 +19,20 @@
     return pltpu.roll(value, shift % 128, 1)
 
 
-def exchange(planes):
-    rows = planes[0].shape[0]
-    lanes = lane_ids(rows)
+def exchange_bit(low, high, bit):
+    step = 4 << bit
+    chosen = (lane_ids(low.shape[0]) & step) != 0
+    return jnp.where(chosen, roll(high, step), low), jnp.where(chosen, high, roll(low, -step))
+
+
+def exchange(sets):
     for bit in range(3):
-        step = 4 << bit
-        chosen = (lanes & step) != 0
-        out = [None] * 8
-        for low in range(8):
-            if low >> bit & 1:
-                continue
-            high = low | 1 << bit
-            out[low] = jnp.where(chosen, roll(planes[high], step), planes[low])
-            out[high] = jnp.where(chosen, planes[high], roll(planes[low], -step))
-        planes = out
-    return planes
+        for planes in sets:
+            for low in range(8):
+                if not low >> bit & 1:
+                    high = low | 1 << bit
+                    planes[low], planes[high] = exchange_bit(planes[low], planes[high], bit)
+    return sets
 
 
 def colour(link, vector):
@@ -54,19 +53,8 @@
     return lax.dot_general(a, b, (((1,), (1,)), ((), ())), preferred_element_type=F32)
 
 
-def variants(plain):
-    second = (lane_ids(plain.shape[0]) & 16) != 0
-    swapped = jnp.where(second, roll(plain, 16), roll(plain, -16))
-    return (
-        plain,
-        jnp.where(second, -plain, plain),
-        swapped,
-        jnp.where(second, swapped, -swapped),
-    )
-
-
 def inner_kernel(
-    v_ref, u_ref, out_ref, lt_ref, lz_ref, ut_ref, uz_ref, vf, vm, uf, cm, flat
+    v_ref, u_ref, out_ref, lt_ref, lz_ref, ut_ref, uz_ref, vm, uf, cm, flat, kept
 ):
     flat[...] = jnp.zeros_like(flat)
 
@@ -78,18 +66,20 @@
                     row = ((c * 3 + d) * 2 + ri) * 16
                     flat[0, pl.ds(row, 16), :] = 0.5 * u_ref[ri, mu, c, d].astype(F32)
 
-        lanes = lane_ids(24)
-        drop = ((lanes & 12) == 12) & (mu == 1)
-        for t in range(4):
-            z_planes = [flat[0, pl.ds(t * 4 + z, 24, stride=16), :] for z in range(4)]
-            for a, value in enumerate(exchange(z_planes + z_planes)):
-                uf[a, mu, t] = jnp.where(drop, 0.0, value)
-
-        @pl.when(mu == 1)
-        def _():
-            t_planes = [flat[0, pl.ds(t * 4 + 3, 24, stride=16), :] for t in range(4)]
-            for a, value in enumerate(exchange(t_planes + t_planes)):
-                uz_ref[a] = value
+        drop = ((lane_ids(24) & 12) == 12) & (mu == 1)
+
+        def load(t, plane):
+            first = plane % 4 * 4 + 3 if t == 4 else t * 4 + plane % 4
+            return flat[0, pl.ds(first, 24, stride=16), :]
+
+        for group in ((0, 1), (2, 3), (4,)):
+            done = exchange([[load(t, plane) for plane in range(8)] for t in group])
+            for t, values in zip(group, done):
+                for a, value in enumerate(values):
+                    uf[a, mu, t] = value if t == 4 else jnp.where(drop, 0.0, value)
+
+    for a in range(8):
+        uz_ref[a] = uf[a, 1, 4]
 
     for a in range(8):
         ut_ref[a] = uf[a, 0, 3]
@@ -101,23 +91,34 @@
             for ri in range(2):
                 block = v_ref[ri, :, 2 * chi + sb, c].astype(F32)
                 flat[sb, pl.ds(ri * 384, 384), :] = block.reshape(384, 128)
-        for t in range(4):
-            planes = [
-                flat[sb, pl.ds(t * 4 + z, ROWS, stride=16), :] for sb in range(2) for z in range(4)
-            ]
-            column = pl.multiple_of((t * 3 + c) * 128, 128)
-            for a, value in enumerate(exchange(planes)):
-                vf[a, chi, t, c] = value
-                for kind, operand in enumerate(variants(value)):
-                    vm[kind, a, chi, :, pl.ds(column, 128)] = operand.astype(BF16)
-        planes = [
-            flat[sb, pl.ds(t * 4 + 3, ROWS, stride=16), :] for sb in range(2) for t in range(4)
-        ]
-        column = pl.multiple_of(c * 128, 128)
-        for a, value in enumerate(exchange(planes)):
-            both = variants(value)
-            lz_ref[0, a, chi, :, pl.ds(column, 128)] = both[0].astype(BF16)
-            lz_ref[1, a, chi, :, pl.ds(column, 128)] = both[1].astype(BF16)
+
+        def load(t, plane):
+            sb, q = plane // 4, plane % 4
+            first = q * 4 + 3 if t == 4 else t * 4 + q
+            return flat[sb, pl.ds(first, ROWS, stride=16), :].astype(BF16)
+
+        second = (lane_ids(ROWS) & 16) != 0
+        for group in ((0, 1), (2, 3), (4,)):
+            done = exchange([[load(t, plane) for plane in range(8)] for t in group])
+            turned = [[jnp.where(second, -value, value) for value in values] for values in done]
+            if group != (4,):
+                swapped = [
+                    [jnp.where(second, roll(value, 16), roll(value, -16)) for value in values]
+                    for values in done
+                ]
+            for k, t in enumerate(group):
+                for a in range(8):
+                    if t == 4:
+                        column = pl.multiple_of(c * 128, 128)
+                        lz_ref[0, a, chi, :, pl.ds(column, 128)] = done[k][a]
+                        lz_ref[1, a, chi, :, pl.ds(column, 128)] = turned[k][a]
+                        continue
+                    column = pl.multiple_of((t * 3 + c) * 128, 128)
+                    vm[0, a, chi, :, pl.ds(column, 128)] = done[k][a]
+                    vm[1, a, chi, :, pl.ds(column, 128)] = turned[k][a]
+                    value = swapped[k][a]
+                    vm[2, a, chi, :, pl.ds(column, 128)] = value
+                    vm[3, a, chi, :, pl.ds(column, 128)] = jnp.where(second, value, -value)
 
     for a in range(8):
         for chi in range(2):
@@ -125,55 +126,71 @@
 
     cm[...] = jnp.zeros_like(cm)
 
-    @pl.loop(0, 8)
+    def fill(a, chi):
+        ahead = lax.rem(a + 1, 8)
+        x_last = (lane_ids(NV) & 3) == 3
+        x_last_pair = (lane_ids(ROWS) & 3) == 3
+        y_last = lane_ids(NV) >= 96
+        for t in range(4):
+            for mu in range(4):
+                if mu == 0 and t == 3:
+                    continue
+                link = [uf[a, mu, t, pl.ds(k, 1), :] for k in range(18)]
+                vector = []
+                for d in range(3):
+                    first = (((t + 1) if mu == 0 else t) * 3 + d) * 128
+                    value = vm[0, a, chi, :, first : first + 128]
+                    if mu == 1:
+                        value = roll(value, -4)
+                    elif mu == 2:
+                        value = roll(value, -32)
+                    elif mu == 3:
+                        other = vm[0, ahead, chi, :, first : first + 128]
+                        value = jnp.where(x_last_pair, roll(other, 3), roll(value, -1))
+                    value = value.astype(F32)
+                    vector += [value[:NV], value[NV:]]
+                for c, parts in enumerate(colour(link, vector)):
+                    column = slice((t * 3 + c) * 128, (t * 3 + c + 1) * 128)
+                    for ri in range(2):
+                        if mu < 2:
+                            row = ri * 64 + mu * 32
+                            cm[chi, 0, row : row + 24, column] = parts[ri].astype(BF16)
+                        else:
+                            last = y_last if mu == 2 else x_last
+                            outer = jnp.where(last, -parts[ri], 0.0)
+                            row = ri * 64
+                            cm[chi, mu - 1, row : row + 24, column] = parts[ri].astype(BF16)
+                            cm[chi, mu - 1, row + 32 : row + 56, column] = outer.astype(BF16)
+
+    def multiply(a, chi):
+        near, far = vm[0, a, chi], vm[0, a, 1 - chi]
+        return (
+            nt(jnp.concatenate([near, far, vm[1, a, 1 - chi]], 0), cm[chi, 0]),
+            nt(jnp.concatenate([near, vm[3, a, 1 - chi]], 0), cm[chi, 1]),
+            nt(jnp.concatenate([near, vm[2, a, 1 - chi]], 0), cm[chi, 2]),
+            nt(near, near),
+        )
+
+    def keep(blocks):
+        for value, (start, rows) in zip(blocks, ((0, 144), (144, 96), (240, 96), (336, 48))):
+            kept[start : start + rows, : value.shape[1]] = value
+
+    def finish(a):
+        first = (kept[0:144, :], kept[144:240, :], kept[240:336, :], kept[336:384, :ROWS])
+        combine_inner([first, multiply(a, 1)], a, out_ref)
+
+    fill(0, 0)
+    keep(multiply(0, 0))
+    fill(0, 1)
+
+    @pl.loop(1, 8)
     def _(a):
-        ahead = (a + 1) % 8
-        lanes = lane_ids(24)
-        x_last = (lanes & 3) == 3
-        y_last = lanes >= 96
-        blocks = []
-        for chi in range(2):
-            for t in range(4):
-                for mu in range(4):
-                    if mu == 0 and t == 3:
-                        continue
-                    link = [uf[a, mu, t, pl.ds(k, 1), :] for k in range(18)]
-                    vector = []
-                    for d in range(3):
-                        for ri in range(2):
-                            rows = pl.ds(ri * 24, 24)
-                            if mu == 0:
-                                value = vf[a, chi, t + 1, d, rows, :]
-                            else:
-                                value = vf[a, chi, t, d, rows, :]
-                            if mu == 1:
-                                value = roll(value, -4)
-                            elif mu == 2:
-                                value = roll(value, -32)
-                            elif mu == 3:
-                                other = vf[ahead, chi, t, d, rows, :]
-                                value = jnp.where(x_last, roll(other, 3), roll(value, -1))
-                            vector.append(value)
-                    for c, parts in enumerate(colour(link, vector)):
-                        column = slice((t * 3 + c) * 128, (t * 3 + c + 1) * 128)
-                        for ri in range(2):
-                            if mu < 2:
-                                row = ri * 64 + mu * 32
-                                cm[0, row : row + 24, column] = parts[ri].astype(BF16)
-                            else:
-                                last = y_last if mu == 2 else x_last
-                                full = parts[ri]
-                                outer = jnp.where(last, -full, 0.0)
-                                row = ri * 64
-                                cm[mu - 1, row : row + 24, column] = full.astype(BF16)
-                                cm[mu - 1, row + 32 : row + 56, column] = outer.astype(BF16)
-            near, far = vm[0, a, chi], vm[0, a, 1 - chi]
-            tz = nt(jnp.concatenate([near, far, vm[1, a, 1 - chi]], 0), cm[0])
-            y = nt(jnp.concatenate([near, vm[3, a, 1 - chi]], 0), cm[1])
-            x = nt(jnp.concatenate([near, vm[2, a, 1 - chi]], 0), cm[2])
-            gram = nt(near, near)
-            blocks.append((tz, y, x, gram))
-        combine_inner(blocks, a, out_ref)
+        finish(a - 1)
+        fill(a, 0)
+        keep(multiply(a, 0))
+        fill(a, 1)
+
+    finish(7)
 
 
 def complex_of(product, sign):
@@ -255,13 +272,13 @@
         in_specs=[vmem] * 2,
         out_specs=(vmem,) * 5,
         scratch_shapes=[
-            pltpu.VMEM((8, 2, 4, 3, ROWS, 128), F32),
             pltpu.VMEM((4, 8, 2, ROWS, 1536), BF16),
-            pltpu.VMEM((8, 4, 4, 24, 128), F32),
-            pltpu.VMEM((3, 128, 1536), BF16),
+            pltpu.VMEM((8, 4, 5, 24, 128), F32),
+            pltpu.VMEM((2, 3, 128, 1536), BF16),
             pltpu.VMEM((2, 768, 128), F32),
+            pltpu.VMEM((384, 128), F32),
         ],
-        compiler_params=pltpu.CompilerParams(vmem_limit_bytes=56 * 1024 * 1024),
+        compiler_params=pltpu.CompilerParams(vmem_limit_bytes=24 * 1024 * 1024),
         cost_estimate=pl.CostEstimate(
             flops=40_000_000_000, bytes_accessed=6_000_000, transcendentals=0
         ),
@@ -278,12 +295,14 @@
                 block = v_ref[ri, :, 2 * chi + sb, c].astype(F32)
                 flat[sb, pl.ds(ri * 384, 384), :] = block.reshape(384, 128)
         column = pl.multiple_of(c * 128, 128)
-        for out, stride in ((t_ref, 1), (z_ref, 4)):
-            planes = [
-                flat[sb, pl.ds(q * stride, ROWS, stride=16), :] for sb in range(2) for q in range(4)
-            ]
-            for a, value in enumerate(exchange(planes)):
-                out[a, chi, :, pl.ds(column, 128)] = value.astype(BF16)
+
+        def load(k, plane):
+            return flat[plane // 4, pl.ds(plane % 4 * (1, 4)[k], ROWS, stride=16), :].astype(BF16)
+
+        done = exchange([[load(k, plane) for plane in range(8)] for k in range(2)])
+        for out, values in zip((t_ref, z_ref), done):
+            for a, value in enumerate(values):
+                out[a, chi, :, pl.ds(column, 128)] = value
 
 
 def face_call(vectors):
@@ -295,7 +314,7 @@
         in_specs=[vmem],
         out_specs=(vmem, vmem),
         scratch_shapes=[pltpu.VMEM((2, 768, 128), F32)],
-        compiler_params=pltpu.CompilerParams(vmem_limit_bytes=24 * 1024 * 1024),
+        compiler_params=pltpu.CompilerParams(vmem_limit_bytes=12 * 1024 * 1024),
         name="faces",
     )(vectors)
 
@@ -342,7 +361,7 @@
         in_specs=[vmem] * 6,
         out_specs=vmem,
         scratch_shapes=[pltpu.VMEM((2, 128, 384), BF16)],
-        compiler_params=pltpu.CompilerParams(vmem_limit_bytes=24 * 1024 * 1024),
+        compiler_params=pltpu.CompilerParams(vmem_limit_bytes=12 * 1024 * 1024),
         name="outer",
     )(face_t, face_z, left_t, left_z, link_t, link_z)
 
@@ -451,7 +470,7 @@
         out_shape=(row,) * count,
         in_specs=[vmem] * len(args),
         out_specs=(vmem,) * count,
-        compiler_params=pltpu.CompilerParams(vmem_limit_bytes=24 * 1024 * 1024),
+        compiler_params=pltpu.CompilerParams(vmem_limit_bytes=12 * 1024 * 1024),
         name=name,
     )(*args)
 

time: 84.1 us -> 72.3 us (0.86)
  Pallas kernels: 45.9 us -> 37.4 us
  local copies, waits for them, and re-layouts: 12.1 us -> 8.92 us
    pallas_call x1, Pallas kernels: 30.7 us -> 22.3 us  [inner_call(): pl.pallas_call(inner_kernel, out_shape=(shape((8, 3, 2, ROWS, 128), F32),...]
    unnamed x12 -> x6, local copies, waits for them, and re-layouts: 5.78 us -> 2.63 us
  transfers between devices with their start and end apart: 10 -> 10, of which waited for: 2 -> 2; matrix products, arithmetic and copies ran while one was open for 6% -> 7% of each run, Pallas kernels for 46% -> 41%
where the time goes in v2:
time: 72.3 us; the launch traced here: 72.1 us
  Pallas kernels  37.4 us (52%)
  starting transfers between devices  19.7 us (27%)
  local copies, waits for them, and re-layouts  8.92 us (12%)
  waiting for transfers between devices  5.09 us (7%)
  between operations  0.73 us (1%)
    pallas_call x1, Pallas kernels, inner_call(): pl.pallas_call(inner_kernel, out_shape=(shape((8, 3, 2, ROWS, 128), F32),...  22.3 us
    ppermute x10, starting transfers between devices, shifted(): lax.ppermute(value, axis, [(k, (k + steps) % count) for k in range(count)])  19.7 us
    pallas_call x3, Pallas kernels, small_call(): pl.pallas_call(kernel, out_shape=(row,) * count, in_specs=[vmem] * len(ar...  7.7 us
    pallas_call x1, Pallas kernels, outer_call(): pl.pallas_call(outer_kernel, out_shape=jax.ShapeDtypeStruct((8, 2, 2, ROW...  5.1 us
    ppermute x10, waiting for transfers between devices, shifted(): lax.ppermute(value, axis, [(k, (k + steps) % count) for k in range(count)])  5.09 us
    reshape x2, local copies, waits for them, and re-layouts, per_device(): blocks.reshape(1, 1, 8, 5, 2 * ROWS * ROWS)  4.92 us
    unnamed x6, local copies, waits for them, and re-layouts  2.63 us
    pallas_call x1, Pallas kernels, face_call(): pl.pallas_call(face_kernel, out_shape=(face, face), in_specs=[vmem], out_...  2.3 us
  transfers between devices with their start and end apart: 10, of which 2 were waited for; matrix products, arithmetic and copies ran while one was open for 7% of the time, Pallas kernels for 41%

profile of v2, /device:TPU:0, one launch (start us, length us, event | category | flops | bytes accessed | tf_op | source)
XLA Modules:
  0.0 72.1 jit_solution(13888969846822696863)
XLA Ops:
  0.6 0.7 pad.4.vec
  1.3 3.3 %collective-permute-start.2 = (f32[8,128]{1,0:T(8,128)S(1)}, f32[8,128]{1,0:T(8,128)S(1)}, u32[]{:S(2)}, u32[]{:S(2)}) collective-permute-start(f32[8,128]{1,0:T(8,128)S(1)} %pad.4.vec), channel_id=1, source_target_pairs={{0,120},{8,0},{16,8},{24,16},{32,24},{40,32},{48,40},{56,48},{64,5... | collective-permute-start | bytes 12296 | tf_op jit(solution)/shard_map/ppermute | solution.py:480
  4.6 6.4 %collective-permute-start.3 = (f32[8,128]{1,0:T(8,128)S(1)}, f32[8,128]{1,0:T(8,128)S(1)}, u32[]{:S(2)}, u32[]{:S(2)}) collective-permute-start(f32[8,128]{1,0:T(8,128)S(1)} %pad.4.vec), channel_id=1, source_target_pairs={{0,7},{1,0},{2,1},{3,2},{4,3},{5,4},{6,5},{7,6},{8,15},{9,8},{10,9... | collective-permute-start | bytes 12296 | tf_op jit(solution)/shard_map/ppermute | solution.py:480
  11.0 0.0 copy-start
  11.0 1.7 %copy-done = bf16[2,24,4,3,4,4,128]{6,5,4,3,2,1,0:T(4,128)(2,1)S(1)} copy-done((bf16[2,24,4,3,4,4,128]{6,5,4,3,2,1,0:T(4,128)(2,1)S(1)}, bf16[2,24,4,3,4,4,128]{6,5,4,3,2,1,0:T(4,128)(2,1)}, u32[]{:S(2)}) %copy-start) | copy-done | bytes 2359320
  12.7 0.0 copy-start.1
  12.7 2.3 %faces.1 = (bf16[8,2,48,384]{3,2,1,0:T(8,128)(2,1)S(1)}, bf16[8,2,48,384]{3,2,1,0:T(8,128)(2,1)S(1)}) custom-call(bf16[2,24,4,3,16,128]{5,4,3,2,1,0:T(8,128)(2,1)S(1)} %bitcast.7), custom_call_target="tpu_custom_call" | custom-call | tf_op jit(solution)/shard_map/faces/pallas_call | solution.py:311
  15.0 0.1 collective-permute-start
  15.0 1.6 %collective-permute-start.1 = (bf16[8,2,48,384]{3,2,1,0:T(8,128)(2,1)S(1)}, bf16[8,2,48,384]{3,2,1,0:T(8,128)(2,1)S(1)}, u32[]{:S(2)}, u32[]{:S(2)}) collective-permute-start(bf16[8,2,48,384]{3,2,1,0:T(8,128)(2,1)S(1)} %get-tuple-element.18), channel_id=1, source_target_pairs={{0,7},{1,0},{2,1},{3,2},{4,3},{5,4},{6,5},{7,6},{8,15},{9,8},{10,9... | collective-permute-start | bytes 1769480 | tf_op jit(solution)/shard_map/ppermute | solution.py:480
  16.7 0.0 copy-done.1
  16.7 0.0 copy-start.2
  16.7 1.0 %copy-done.2 = bf16[2,4,3,3,4,4,128]{6,5,4,3,2,1,0:T(4,128)(2,1)S(1)} copy-done((bf16[2,4,3,3,4,4,128]{6,5,4,3,2,1,0:T(4,128)(2,1)S(1)}, bf16[2,4,3,3,4,4,128]{6,5,4,3,2,1,0:T(4,128)(2,1)}, u32[]{:S(2)}) %copy-start.2) | copy-done | bytes 294936
  17.6 22.3 %inner.1 = (f32[8,3,2,48,128]{4,3,2,1,0:T(8,128)S(1)}, bf16[8,2,48,384]{3,2,1,0:T(8,128)(2,1)S(1)}, bf16[2,8,2,48,384]{4,3,2,1,0:T(8,128)(2,1)S(1)}, f32[8,24,128]{2,1,0:T(8,128)S(1)}, f32[8,24,128]{2,1,0:T(8,128)S(1)}) custom-call(bf16[2,24,4,3,16,128]{5,4,3,2,1,0:T(8,128)(2,1)S(1)} %bitcast.8, bf16[2,4,3,3,16,128]{5,4,3,2,1,0:T(8,128)(2,1)S(1)} %bitcast.9), custom_call_target="tpu_custom_call" | custom-call | flops 40000000000 | bytes 6000000 | tf_op jit(solution)/shard_map/inner/pallas_call | solution.py:263
  40.0 0.0 collective-permute-done.ft_ref
  40.0 0.0 collective-permute-done.1.fz_ref
  40.0 5.1 %outer.1 = f32[8,2,2,48,128]{4,3,2,1,0:T(8,128)S(1)} custom-call(bf16[8,2,48,384]{3,2,1,0:T(8,128)(2,1)S(1)} %collective-permute-done.ft_ref, bf16[8,2,48,384]{3,2,1,0:T(8,128)(2,1)S(1)} %collective-permute-done.1.fz_ref, bf16[8,2,48,384]{3,2,1,0:T(8,128)(2,1)S(1)} %get-tuple-element.19.lt_ref, bf16[2,8,2,48,384]{4,3,2,1,0:T(8,128)(2,1)S(1)} %get-tuple-element.20.lz_ref, ...), custom_call_target="tpu_custom_call" | custom-call | tf_op jit(solution)/shard_map/outer/pallas_call | solution.py:358
  45.1 0.0 collective-permute-done.2.vt
  45.1 0.0 collective-permute-done.3.vz
  45.1 3.8 %first.1 = (f32[8,128]{1,0:T(8,128)S(1)}, f32[8,128]{1,0:T(8,128)S(1)}, f32[8,128]{1,0:T(8,128)S(1)}) custom-call(f32[8,3,2,48,128]{4,3,2,1,0:T(8,128)S(1)} %get-tuple-element.16.inner, f32[8,2,2,48,128]{4,3,2,1,0:T(8,128)S(1)} %outer.1, f32[8,128]{1,0:T(8,128)S(1)} %pad.4.vec, f32[8,128]{1,0:T(8,128)S(1)} %collective-permute-done.2.vt, ...), custom_call_target="tpu_custom_call" | custom-call | tf_op jit(solution)/shard_map/first/pallas_call | solution.py:468
  48.9 0.0 collective-permute-start.4
  49.0 2.1 %collective-permute-start.5 = (f32[8,128]{1,0:T(8,128)S(1)}, f32[8,128]{1,0:T(8,128)S(1)}, u32[]{:S(2)}, u32[]{:S(2)}) collective-permute-start(f32[8,128]{1,0:T(8,128)S(1)} %get-tuple-element.25), channel_id=1, source_target_pairs={{0,1},{1,2},{2,3},{3,4},{4,5},{5,6},{6,7},{7,0},{8,9},{9,10},{10,1... | collective-permute-start | bytes 12296 | tf_op jit(solution)/shard_map/ppermute | solution.py:480
  51.1 0.1 slice.13
  51.2 2.9 %collective-permute-done.4.rt = f32[8,128]{1,0:T(8,128)S(1)} collective-permute-done((f32[8,128]{1,0:T(8,128)S(1)}, f32[8,128]{1,0:T(8,128)S(1)}, u32[]{:S(2)}, u32[]{:S(2)}) %collective-permute-start.4) | collective-permute-done | bytes 4128 | tf_op jit(solution)/shard_map/ppermute | solution.py:480
  54.1 2.2 %collective-permute-done.5.rz = f32[8,128]{1,0:T(8,128)S(1)} collective-permute-done((f32[8,128]{1,0:T(8,128)S(1)}, f32[8,128]{1,0:T(8,128)S(1)}, u32[]{:S(2)}, u32[]{:S(2)}) %collective-permute-start.5) | collective-permute-done | bytes 4128 | tf_op jit(solution)/shard_map/ppermute | solution.py:480
  56.3 2.0 %second.1 = (f32[8,128]{1,0:T(8,128)S(1)}, f32[8,128]{1,0:T(8,128)S(1)}, f32[8,128]{1,0:T(8,128)S(1)}, f32[8,128]{1,0:T(8,128)S(1)}) custom-call(f32[8,3,2,48,128]{4,3,2,1,0:T(8,128)S(1)} %get-tuple-element.16.inner, f32[8,2,2,48,128]{4,3,2,1,0:T(8,128)S(1)} %outer.1, f32[8,128]{1,0:T(8,128)S(1)} %get-tuple-element.23.part, ...), custom_call_target="tpu_custom_call" | custom-call | tf_op jit(solution)/shard_map/second/pallas_call | solution.py:468
  58.2 2.7 %collective-permute-start.8 = (f32[8,128]{1,0:T(8,128)S(1)}, f32[8,128]{1,0:T(8,128)S(1)}, u32[]{:S(2)}, u32[]{:S(2)}) collective-permute-start(f32[8,128]{1,0:T(8,128)S(1)} %get-tuple-element.29), channel_id=1, source_target_pairs={{0,120},{8,0},{16,8},{24,16},{32,24},{40,32},{48,40},{56,48},{64,5... | collective-permute-start | bytes 12296 | tf_op jit(solution)/shard_map/ppermute | solution.py:480
  60.9 0.6 collective-permute-start.9
  61.6 0.0 collective-permute-start.6
  61.6 2.9 %collective-permute-start.7 = (f32[8,128]{1,0:T(8,128)S(1)}, f32[8,128]{1,0:T(8,128)S(1)}, u32[]{:S(2)}, u32[]{:S(2)}) collective-permute-start(f32[8,128]{1,0:T(8,128)S(1)} %get-tuple-element.28), channel_id=1, source_target_pairs={{0,1},{1,2},{2,3},{3,4},{4,5},{5,6},{6,7},{7,0},{8,9},{9,10},{10,1... | collective-permute-start | bytes 12296 | tf_op jit(solution)/shard_map/ppermute | solution.py:480
  64.5 0.2 pad_maximum_fusion
  64.6 2.4 %reshape.24 = f32[1,1,8,5,4608]{4,3,2,1,0:T(8,128)} reshape(f32[8,5,2,48,48]{4,3,2,1,0:T(8,128)S(1)} %pad_maximum_fusion) | data formatting | bytes 1474560 | tf_op jit(solution)/shard_map/reshape | solution.py:500
  67.0 2.6 %copy.7 = f32[1,1,8,5,4608]{4,2,3,1,0:T(8,128)} copy(f32[1,1,8,5,4608]{4,3,2,1,0:T(8,128)} %reshape.24) | data formatting | bytes 1474560 | tf_op jit(solution)/shard_map/reshape | solution.py:500
  69.6 0.0 collective-permute-done.6.rt
  69.6 0.0 collective-permute-done.7.rz
  69.6 0.0 collective-permute-done.8.vt
  69.6 0.0 collective-permute-done.9.vz
  69.6 1.9 %last.1 = f32[8,128]{1,0:T(8,128)S(1)} custom-call(f32[8,2,2,48,128]{4,3,2,1,0:T(8,128)S(1)} %outer.1, f32[8,128]{1,0:T(8,128)S(1)} %get-tuple-element.26.part, f32[8,128]{1,0:T(8,128)S(1)} %collective-permute-done.6.rt, f32[8,128]{1,0:T(8,128)S(1)} %collective-permute-done.7.rz, f32[8,128]{1,0:T(8,128)S(1)} %collective-permute-done.8.vt, ...), custom_call_target="tpu_custom_call" | custom-call | tf_op jit(solution)/shard_map/last/pallas_call | solution.py:468
  71.5 0.6 slice_bitcast_fusion
  (1 shorter events, 0.0 us)
Async XLA Ops:
  1.3 43.8 %collective-permute-start.2 = (f32[8,128]{1,0:T(8,128)S(1)}, f32[8,128]{1,0:T(8,128)S(1)}, u32[]{:S(2)}, u32[]{:S(2)}) collective-permute-start(f32[8,128]{1,0:T(8,128)S(1)} %pad.4.vec), channel_id=1, source_target_pairs={{0,120},{8,0},{16,8},{24,16},{32,24},{40,32},{48,40},{56,48},{64,5... | collective-permute-start | bytes 12296 | tf_op jit(solution)/shard_map/ppermute | solution.py:480
  4.6 40.5 %collective-permute-start.3 = (f32[8,128]{1,0:T(8,128)S(1)}, f32[8,128]{1,0:T(8,128)S(1)}, u32[]{:S(2)}, u32[]{:S(2)}) collective-permute-start(f32[8,128]{1,0:T(8,128)S(1)} %pad.4.vec), channel_id=1, source_target_pairs={{0,7},{1,0},{2,1},{3,2},{4,3},{5,4},{6,5},{7,6},{8,15},{9,8},{10,9... | collective-permute-start | bytes 12296 | tf_op jit(solution)/shard_map/ppermute | solution.py:480
  11.0 1.7 %copy-start = (bf16[2,24,4,3,4,4,128]{6,5,4,3,2,1,0:T(4,128)(2,1)S(1)}, bf16[2,24,4,3,4,4,128]{6,5,4,3,2,1,0:T(4,128)(2,1)}, u32[]{:S(2)}) copy-start(bf16[2,24,4,3,4,4,128]{6,5,4,3,2,1,0:T(4,128)(2,1)} %param.3) | copy-start | bytes 7077892
  12.7 4.0 %copy-start.1 = (bf16[2,24,4,3,4,4,128]{6,5,4,3,2,1,0:T(4,128)(2,1)S(1)}, bf16[2,24,4,3,4,4,128]{6,5,4,3,2,1,0:T(4,128)(2,1)}, u32[]{:S(2)}) copy-start(bf16[2,24,4,3,4,4,128]{6,5,4,3,2,1,0:T(4,128)(2,1)} %param.3) | copy-start | bytes 7077892
  15.0 25.0 %collective-permute-start = (bf16[8,2,48,384]{3,2,1,0:T(8,128)(2,1)S(1)}, bf16[8,2,48,384]{3,2,1,0:T(8,128)(2,1)S(1)}, u32[]{:S(2)}, u32[]{:S(2)}) collective-permute-start(bf16[8,2,48,384]{3,2,1,0:T(8,128)(2,1)S(1)} %get-tuple-element.17), channel_id=1, source_target_pairs={{0,120},{8,0},{16,8},{24,16},{32,24},{40,32},{48,40},{56,48},{64,5... | collective-permute-start | bytes 1769480 | tf_op jit(solution)/shard_map/ppermute | solution.py:480
  15.0 24.9 %collective-permute-start.1 = (bf16[8,2,48,384]{3,2,1,0:T(8,128)(2,1)S(1)}, bf16[8,2,48,384]{3,2,1,0:T(8,128)(2,1)S(1)}, u32[]{:S(2)}, u32[]{:S(2)}) collective-permute-start(bf16[8,2,48,384]{3,2,1,0:T(8,128)(2,1)S(1)} %get-tuple-element.18), channel_id=1, source_target_pairs={{0,7},{1,0},{2,1},{3,2},{4,3},{5,4},{6,5},{7,6},{8,15},{9,8},{10,9... | collective-permute-start | bytes 1769480 | tf_op jit(solution)/shard_map/ppermute | solution.py:480
  16.7 1.0 %copy-start.2 = (bf16[2,4,3,3,4,4,128]{6,5,4,3,2,1,0:T(4,128)(2,1)S(1)}, bf16[2,4,3,3,4,4,128]{6,5,4,3,2,1,0:T(4,128)(2,1)}, u32[]{:S(2)}) copy-start(bf16[2,4,3,3,4,4,128]{6,5,4,3,2,1,0:T(4,128)(2,1)} %param.4) | copy-start | bytes 884740
  48.9 5.2 %collective-permute-start.4 = (f32[8,128]{1,0:T(8,128)S(1)}, f32[8,128]{1,0:T(8,128)S(1)}, u32[]{:S(2)}, u32[]{:S(2)}) collective-permute-start(f32[8,128]{1,0:T(8,128)S(1)} %get-tuple-element.24), channel_id=1, source_target_pairs={{0,8},{8,16},{16,24},{24,32},{32,40},{40,48},{48,56},{56,64},{64,7... | collective-permute-start | bytes 12296 | tf_op jit(solution)/shard_map/ppermute | solution.py:480
  49.0 7.3 %collective-permute-start.5 = (f32[8,128]{1,0:T(8,128)S(1)}, f32[8,128]{1,0:T(8,128)S(1)}, u32[]{:S(2)}, u32[]{:S(2)}) collective-permute-start(f32[8,128]{1,0:T(8,128)S(1)} %get-tuple-element.25), channel_id=1, source_target_pairs={{0,1},{1,2},{2,3},{3,4},{4,5},{5,6},{6,7},{7,0},{8,9},{9,10},{10,1... | collective-permute-start | bytes 12296 | tf_op jit(solution)/shard_map/ppermute | solution.py:480
  58.2 11.3 %collective-permute-start.8 = (f32[8,128]{1,0:T(8,128)S(1)}, f32[8,128]{1,0:T(8,128)S(1)}, u32[]{:S(2)}, u32[]{:S(2)}) collective-permute-start(f32[8,128]{1,0:T(8,128)S(1)} %get-tuple-element.29), channel_id=1, source_target_pairs={{0,120},{8,0},{16,8},{24,16},{32,24},{40,32},{48,40},{56,48},{64,5... | collective-permute-start | bytes 12296 | tf_op jit(solution)/shard_map/ppermute | solution.py:480
  60.9 8.7 %collective-permute-start.9 = (f32[8,128]{1,0:T(8,128)S(1)}, f32[8,128]{1,0:T(8,128)S(1)}, u32[]{:S(2)}, u32[]{:S(2)}) collective-permute-start(f32[8,128]{1,0:T(8,128)S(1)} %get-tuple-element.29), channel_id=1, source_target_pairs={{0,7},{1,0},{2,1},{3,2},{4,3},{5,4},{6,5},{7,6},{8,15},{9,8},{10,9... | collective-permute-start | bytes 12296 | tf_op jit(solution)/shard_map/ppermute | solution.py:480
  61.6 8.0 %collective-permute-start.6 = (f32[8,128]{1,0:T(8,128)S(1)}, f32[8,128]{1,0:T(8,128)S(1)}, u32[]{:S(2)}, u32[]{:S(2)}) collective-permute-start(f32[8,128]{1,0:T(8,128)S(1)} %get-tuple-element.27), channel_id=1, source_target_pairs={{0,8},{8,16},{16,24},{24,32},{32,40},{40,48},{48,56},{56,64},{64,7... | collective-permute-start | bytes 12296 | tf_op jit(solution)/shard_map/ppermute | solution.py:480
  61.6 8.0 %collective-permute-start.7 = (f32[8,128]{1,0:T(8,128)S(1)}, f32[8,128]{1,0:T(8,128)S(1)}, u32[]{:S(2)}, u32[]{:S(2)}) collective-permute-start(f32[8,128]{1,0:T(8,128)S(1)} %get-tuple-element.28), channel_id=1, source_target_pairs={{0,1},{1,2},{2,3},{3,4},{4,5},{5,6},{6,7},{7,0},{8,9},{9,10},{10,1... | collective-permute-start | bytes 12296 | tf_op jit(solution)/shard_map/ppermute | solution.py:480

commit v3 on v2

--- a/solution.py
+++ b/solution.py
@@ -319,15 +319,12 @@
     )(vectors)
 
 
-def outer_kernel(ft_ref, fz_ref, lt_ref, lz_ref, ut_ref, uz_ref, out_ref, cm):
+def outer_kernel(ft_ref, fz_ref, lt_ref, lz_ref, ut_ref, uz_ref, vec_ref, out_ref, bt_ref, bz_ref, cm):
     cm[...] = jnp.zeros_like(cm)
 
     @pl.loop(0, 8)
     def _(a):
-        sign = sides()
-        parts = ([[None, None], [None, None]], [[None, None], [None, None]])
         for chi in range(2):
-            phase = 1.0 if chi == 0 else -1.0
             for mu, (face, links) in enumerate(((ft_ref, ut_ref), (fz_ref, uz_ref))):
                 link = [links[a, pl.ds(k, 1), :] for k in range(18)]
                 vector = []
@@ -336,34 +333,49 @@
                     vector += [value[:NV], value[NV:]]
                 for c, both in enumerate(colour(link, vector)):
                     column = slice(c * 128, (c + 1) * 128)
-                    cm[mu, 0:24, column] = both[0].astype(BF16)
-                    cm[mu, 64:88, column] = both[1].astype(BF16)
+                    cm[a, chi, mu, 0:24, column] = both[0].astype(BF16)
+                    cm[a, chi, mu, 64:88, column] = both[1].astype(BF16)
+
+    sign = sides()
+    eye = eye_mask()
+    row_sign, col_sign = signs()
+    for a in range(8):
+        parts = ([[None, None], [None, None]], [[None, None], [None, None]])
+        for chi in range(2):
+            phase = 1.0 if chi == 0 else -1.0
+            for mu in range(2):
                 if mu == 0:
                     left = jnp.concatenate([lt_ref[a, chi], lt_ref[a, 1 - chi]], 0)
                 else:
                     left = jnp.concatenate([lz_ref[0, a, chi], lz_ref[1, a, 1 - chi]], 0)
-                product = nt(left, cm[mu])
+                product = nt(left, cm[a, chi, mu])
                 cross = complex_of(product[ROWS:], sign)
                 if mu == 1:
                     cross = phase * times_i(cross, sign)
                 parts[mu][chi][chi] = -complex_of(product[:ROWS], sign)
                 parts[mu][1 - chi][chi] = cross
-        for mu in range(2):
-            for ri in range(2):
-                out_ref[a, mu, ri] = placed(parts[mu], ri)
-
-
-def outer_call(face_t, face_z, left_t, left_z, link_t, link_z):
+        pr, pi = split(vec_ref[pl.ds(a, 1), :])
+        column_r = row_sign * column_of(pr, eye)
+        column_i = row_sign * column_of(pi, eye)
+        for mu, back in enumerate((bt_ref, bz_ref)):
+            block = placed(parts[mu], 0), placed(parts[mu], 1)
+            out_ref[a, mu, 0] = block[0]
+            out_ref[a, mu, 1] = block[1]
+            back[pl.ds(a, 1), :] = backward(block, column_r, column_i, col_sign)
+
+
+def outer_call(face_t, face_z, left_t, left_z, link_t, link_z, vec):
     vmem = pl.BlockSpec(memory_space=pltpu.VMEM)
+    row = jax.ShapeDtypeStruct((8, 128), F32)
     return pl.pallas_call(
         outer_kernel,
-        out_shape=jax.ShapeDtypeStruct((8, 2, 2, ROWS, 128), F32),
-        in_specs=[vmem] * 6,
-        out_specs=vmem,
-        scratch_shapes=[pltpu.VMEM((2, 128, 384), BF16)],
+        out_shape=(jax.ShapeDtypeStruct((8, 2, 2, ROWS, 128), F32), row, row),
+        in_specs=[vmem] * 7,
+        out_specs=(vmem,) * 3,
+        scratch_shapes=[pltpu.VMEM((8, 2, 2, 128, 384), BF16)],
         compiler_params=pltpu.CompilerParams(vmem_limit_bytes=12 * 1024 * 1024),
         name="outer",
-    )(face_t, face_z, left_t, left_z, link_t, link_z)
+    )(face_t, face_z, left_t, left_z, link_t, link_z, vec)
 
 
 def signs():
@@ -408,38 +420,29 @@
     return rows == lane_ids(ROWS)
 
 
-def local_apply(inner, outer, vec, part_ref, bt_ref, bz_ref):
+def local_apply(inner, vec, part_ref):
     eye = eye_mask()
     row_sign, col_sign = signs()
-    part_ref[...] = jnp.zeros_like(part_ref)
-
-    @pl.loop(0, 8)
-    def _(a):
-        own = vec[pl.ds(a, 1), :]
-        ahead = (a + 1) % 8
-        nxt = vec[pl.ds(ahead, 1), :]
-        block = lambda ref, slot: (ref[a, slot, 0], ref[a, slot, 1])
-        f0 = forward(block(inner, 0), own)
-        f1 = forward(block(inner, 1), own)
-        f2 = forward(block(inner, 2), nxt)
+    own, kept = [], []
+    for a in range(8):
+        here, ahead = vec[pl.ds(a, 1), :], vec[pl.ds((a + 1) % 8, 1), :]
+        diag, y, x = ((inner[a, k, 0], inner[a, k, 1]) for k in range(3))
+        f0, f1, f2 = forward(diag, here), forward(y, here), forward(x, ahead)
         real = jnp.sum(f0[0] + f1[0] + f2[0], axis=1, keepdims=True)
         imag = jnp.sum(f0[1] + f1[1] + f2[1], axis=1, keepdims=True)
-        pr, pi = split(own)
+        pr, pi = split(here)
         column_r = row_sign * column_of(pr, eye)
         column_i = row_sign * column_of(pi, eye)
-        back_y = backward(block(inner, 1), column_r, column_i, col_sign)
-        back_x = backward(block(inner, 2), column_r, column_i, col_sign)
-        bt_ref[pl.ds(a, 1), :] = backward(block(outer, 0), column_r, column_i, col_sign)
-        bz_ref[pl.ds(a, 1), :] = backward(block(outer, 1), column_r, column_i, col_sign)
-        part_ref[pl.ds(a, 1), :] += joined(row_of(real, eye), row_of(imag, eye)) + back_y
-        part_ref[pl.ds(ahead, 1), :] += back_x
+        back_y = backward(y, column_r, column_i, col_sign)
+        own.append(joined(row_of(real, eye), row_of(imag, eye)) + back_y)
+        kept.append(backward(x, column_r, column_i, col_sign))
+    for a in range(8):
+        part_ref[pl.ds(a, 1), :] = own[a] + kept[(a + 7) % 8]
 
 
 def ahead_apply(outer, vt, vz, part_ref):
     eye = eye_mask()
-
-    @pl.loop(0, 8)
-    def _(a):
+    for a in range(8):
         ft = forward((outer[a, 0, 0], outer[a, 0, 1]), vt[pl.ds(a, 1), :])
         fz = forward((outer[a, 1, 0], outer[a, 1, 1]), vz[pl.ds(a, 1), :])
         real = jnp.sum(ft[0] + fz[0], axis=1, keepdims=True)
@@ -447,19 +450,57 @@
         part_ref[pl.ds(a, 1), :] += joined(row_of(real, eye), row_of(imag, eye))
 
 
-def first_kernel(inner, outer, vec, vt, vz, part_ref, bt_ref, bz_ref):
-    local_apply(inner, outer, vec, part_ref, bt_ref, bz_ref)
+def first_kernel(inner, outer, vec, vt, vz, part_ref):
+    local_apply(inner, vec, part_ref)
     ahead_apply(outer, vt, vz, part_ref)
 
 
-def second_kernel(inner, outer, part, rt, rz, vec_ref, part_ref, bt_ref, bz_ref):
+def back_kernel(outer, part, rt, rz, vec_ref, bt_ref, bz_ref):
     vec_ref[...] = part[...] + rt[...] + rz[...]
-    local_apply(inner, outer, vec_ref, part_ref, bt_ref, bz_ref)
+    eye = eye_mask()
+    row_sign, col_sign = signs()
+    for a in range(8):
+        pr, pi = split(vec_ref[pl.ds(a, 1), :])
+        column_r = row_sign * column_of(pr, eye)
+        column_i = row_sign * column_of(pi, eye)
+        for mu, back in enumerate((bt_ref, bz_ref)):
+            block = outer[a, mu, 0], outer[a, mu, 1]
+            back[pl.ds(a, 1), :] = backward(block, column_r, column_i, col_sign)
 
 
 def last_kernel(outer, part, rt, rz, vt, vz, out_ref):
     out_ref[...] = part[...] + rt[...] + rz[...]
     ahead_apply(outer, vt, vz, out_ref)
+
+
+def blocks_kernel(inner, outer, out_ref):
+    sources = ((inner, 0), (outer, 0), (outer, 1), (inner, 1), (inner, 2))
+    for slot, (ref, k) in enumerate(sources):
+        for ri in range(2):
+            for group in range(ROWS // 8):
+                pieces = []
+                for row in range(group * 8, group * 8 + 8):
+                    pieces.append(jnp.concatenate([ref[a, k, ri, row : row + 1, :] for a in range(8)], 0))
+                wide = lane_rows(pieces)
+                first = ri * ROWS * ROWS + group * 8 * ROWS
+                out_ref[slot, :, first : first + 8 * ROWS] = wide
+
+
+def lane_rows(pieces):
+    tiles = []
+    for tile in range(3):
+        total = None
+        for k, piece in enumerate(pieces):
+            shift = k * ROWS - tile * 128
+            if -ROWS < shift < 128:
+                moved = piece if shift == 0 else roll(piece, shift)
+                if shift < 0:
+                    moved = jnp.where(lane_ids(8) < ROWS + shift, moved, 0.0)
+                elif shift + ROWS > 128:
+                    moved = jnp.where(lane_ids(8) >= shift, moved, 0.0)
+                total = moved if total is None else total + moved
+        tiles.append(total)
+    return jnp.concatenate(tiles, 1)
 
 
 def small_call(kernel, count, name, *args):
@@ -475,6 +516,19 @@
     )(*args)
 
 
+def blocks_call(inner, outer):
+    vmem = pl.BlockSpec(memory_space=pltpu.VMEM)
+    return pl.pallas_call(
+        blocks_kernel,
+        out_shape=jax.ShapeDtypeStruct((5, 8, 2 * ROWS * ROWS), F32),
+        in_specs=[vmem] * 2,
+        out_specs=vmem,
+        compiler_params=pltpu.CompilerParams(vmem_limit_bytes=12 * 1024 * 1024),
+        cost_estimate=pl.CostEstimate(flops=0, bytes_accessed=6_000_000, transcendentals=0),
+        name="blocks",
+    )(inner, outer)
+
+
 def shifted(value, axis, steps):
     count = lax.axis_size(axis)
     return lax.ppermute(value, axis, [(k, (k + steps) % count) for k in range(count)])
@@ -489,14 +543,16 @@
     face_t = shifted(face_t, "ta", -1)
     vec_t, vec_z = shifted(vec, "ta", -1), shifted(vec, "sa", -1)
     inner, left_t, left_z, link_t, link_z = inner_call(vectors, links)
-    outer = outer_call(face_t, face_z, left_t, left_z, link_t, link_z)
-    part, bt, bz = small_call(first_kernel, 3, "first", inner, outer, vec, vec_t, vec_z)
-    rt, rz = shifted(bt, "ta", 1), shifted(bz, "sa", 1)
-    once, part, bt, bz = small_call(second_kernel, 4, "second", inner, outer, part, rt, rz)
-    rt, rz = shifted(bt, "ta", 1), shifted(bz, "sa", 1)
-    vec_t, vec_z = shifted(once, "ta", -1), shifted(once, "sa", -1)
+    outer, bt, bz = outer_call(face_t, face_z, left_t, left_z, link_t, link_z, vec)
+    rz, rt = shifted(bz, "sa", 1), shifted(bt, "ta", 1)
+    (part,) = small_call(first_kernel, 1, "first", inner, outer, vec, vec_t, vec_z)
+    once, bt, bz = small_call(back_kernel, 3, "back", outer, part, rt, rz)
+    vec_z, vec_t = shifted(once, "sa", -1), shifted(once, "ta", -1)
+    rz, rt = shifted(bz, "sa", 1), shifted(bt, "ta", 1)
+    (part,) = small_call(local_apply, 1, "local", inner, once)
+    blocks = blocks_call(inner, outer)
     (twice,) = small_call(last_kernel, 1, "last", outer, part, rt, rz, vec_t, vec_z)
-    blocks = jnp.concatenate([inner[:, :1], outer, inner[:, 1:]], 1)[..., :ROWS]
+    blocks = jnp.swapaxes(blocks, 0, 1)
     return blocks.reshape(1, 1, 8, 5, 2 * ROWS * ROWS), twice[:, : 2 * ROWS].reshape(1, 1, 8, 2 * ROWS)
 
 

time: 72.3 us -> 65.1 us (0.900)
  local copies, waits for them, and re-layouts: 8.92 us -> 3.92 us
  starting transfers between devices: 19.7 us -> 23.4 us
  Pallas kernels: 37.4 us -> 33.7 us
  waiting for transfers between devices: 5.09 us -> 3.19 us
    reshape x2 -> x0, local copies, waits for them, and re-layouts: 4.92 us -> none  [per_device(): blocks.reshape(1, 1, 8, 5, 2 * ROWS * ROWS)]
    pallas_call x3 -> x4, Pallas kernels: 7.7 us -> 3.93 us  [small_call(): pl.pallas_call(kernel, out_shape=(row,) * count, in_specs=[vmem] * len(ar...]
    ppermute x10, starting transfers between devices: 19.7 us -> 23.4 us  [shifted(): lax.ppermute(value, axis, [(k, (k + steps) % count) for k in range(count)])]
    ppermute x10, waiting for transfers between devices: 5.09 us -> 3.19 us  [shifted(): lax.ppermute(value, axis, [(k, (k + steps) % count) for k in range(count)])]
    pallas_call x1 -> x2, Pallas kernels: 5.1 us -> 5.18 us  [the longest x1 3.23 us: outer_call(): pl.pallas_call(outer_kernel, out_shape=(jax.ShapeDtypeStruct((8, 2, 2, RO...]
  transfers between devices with their start and end apart: 10 -> 10, of which waited for: 2 -> 2; matrix products, arithmetic and copies ran while one was open for 7% -> 0% of each run, Pallas kernels for 41% -> 50%
where the time goes in v3:
time: 65.1 us; the launch traced here: 64.9 us
  Pallas kernels  33.7 us (52%)
  starting transfers between devices  23.4 us (36%)
  local copies, waits for them, and re-layouts  3.92 us (6%)
  waiting for transfers between devices  3.19 us (5%)
  between operations  0.74 us (1%)
    ppermute x10, starting transfers between devices, shifted(): lax.ppermute(value, axis, [(k, (k + steps) % count) for k in range(count)])  23.4 us
    pallas_call x1, Pallas kernels, inner_call(): pl.pallas_call(inner_kernel, out_shape=(shape((8, 3, 2, ROWS, 128), F32),...  22.3 us
    pallas_call x4, Pallas kernels, small_call(): pl.pallas_call(kernel, out_shape=(row,) * count, in_specs=[vmem] * len(ar...  3.93 us
    pallas_call x1, Pallas kernels, outer_call(): pl.pallas_call(outer_kernel, out_shape=(jax.ShapeDtypeStruct((8, 2, 2, RO...  3.23 us
    ppermute x10, waiting for transfers between devices, shifted(): lax.ppermute(value, axis, [(k, (k + steps) % count) for k in range(count)])  3.19 us
    unnamed x6, local copies, waits for them, and re-layouts  2.63 us
    pallas_call x1, Pallas kernels, face_call(): pl.pallas_call(face_kernel, out_shape=(face, face), in_specs=[vmem], out_...  2.3 us
    pallas_call x1, Pallas kernels, blocks_call(): pl.pallas_call(blocks_kernel, out_shape=jax.ShapeDtypeStruct((5, 8, 2 * R...  1.95 us
  transfers between devices with their start and end apart: 10, of which 2 were waited for; matrix products, arithmetic and copies ran while one was open for 0% of the time, Pallas kernels for 50%

profile of v3, /device:TPU:0, one launch (start us, length us, event | category | flops | bytes accessed | tf_op | source)
XLA Modules:
  0.0 64.9 jit_solution(39654871724031333)
XLA Ops:
  0.6 0.7 %pad.4.vec_ref.vec = f32[8,128]{1,0:T(8,128)S(1)} pad(f32[8,96]{1,0:T(8,128)} %bitcast.12, f32[]{:T(128)} %constant.2.clone.1), padding=0_0x0_32 | pad | bytes 7172 | tf_op jit(solution)/shard_map/jit(_pad)/pad | solution.py:540
  1.3 3.3 %collective-permute-start.2 = (f32[8,128]{1,0:T(8,128)S(1)}, f32[8,128]{1,0:T(8,128)S(1)}, u32[]{:S(2)}, u32[]{:S(2)}) collective-permute-start(f32[8,128]{1,0:T(8,128)S(1)} %pad.4.vec_ref.vec), channel_id=1, source_target_pairs={{0,120},{8,0},{16,8},{24,16},{32,24},{40,32},{48,40},{56,48},{64,5... | collective-permute-start | bytes 12296 | tf_op jit(solution)/shard_map/ppermute | solution.py:534
  4.6 6.4 %collective-permute-start.3 = (f32[8,128]{1,0:T(8,128)S(1)}, f32[8,128]{1,0:T(8,128)S(1)}, u32[]{:S(2)}, u32[]{:S(2)}) collective-permute-start(f32[8,128]{1,0:T(8,128)S(1)} %pad.4.vec_ref.vec), channel_id=1, source_target_pairs={{0,7},{1,0},{2,1},{3,2},{4,3},{5,4},{6,5},{7,6},{8,15},{9,8},{10,9... | collective-permute-start | bytes 12296 | tf_op jit(solution)/shard_map/ppermute | solution.py:534
  11.0 0.0 copy-start
  11.0 1.7 %copy-done = bf16[2,24,4,3,4,4,128]{6,5,4,3,2,1,0:T(4,128)(2,1)S(1)} copy-done((bf16[2,24,4,3,4,4,128]{6,5,4,3,2,1,0:T(4,128)(2,1)S(1)}, bf16[2,24,4,3,4,4,128]{6,5,4,3,2,1,0:T(4,128)(2,1)}, u32[]{:S(2)}) %copy-start) | copy-done | bytes 2359320
  12.7 0.0 copy-start.1
  12.7 2.3 %faces.1 = (bf16[8,2,48,384]{3,2,1,0:T(8,128)(2,1)S(1)}, bf16[8,2,48,384]{3,2,1,0:T(8,128)(2,1)S(1)}) custom-call(bf16[2,24,4,3,16,128]{5,4,3,2,1,0:T(8,128)(2,1)S(1)} %bitcast.8), custom_call_target="tpu_custom_call" | custom-call | tf_op jit(solution)/shard_map/faces/pallas_call | solution.py:311
  15.0 0.1 collective-permute-start
  15.0 1.6 %collective-permute-start.1 = (bf16[8,2,48,384]{3,2,1,0:T(8,128)(2,1)S(1)}, bf16[8,2,48,384]{3,2,1,0:T(8,128)(2,1)S(1)}, u32[]{:S(2)}, u32[]{:S(2)}) collective-permute-start(bf16[8,2,48,384]{3,2,1,0:T(8,128)(2,1)S(1)} %get-tuple-element.17), channel_id=1, source_target_pairs={{0,7},{1,0},{2,1},{3,2},{4,3},{5,4},{6,5},{7,6},{8,15},{9,8},{10,9... | collective-permute-start | bytes 1769480 | tf_op jit(solution)/shard_map/ppermute | solution.py:534
  16.7 0.0 copy-done.1
  16.7 0.0 copy-start.2
  16.7 1.0 %copy-done.2 = bf16[2,4,3,3,4,4,128]{6,5,4,3,2,1,0:T(4,128)(2,1)S(1)} copy-done((bf16[2,4,3,3,4,4,128]{6,5,4,3,2,1,0:T(4,128)(2,1)S(1)}, bf16[2,4,3,3,4,4,128]{6,5,4,3,2,1,0:T(4,128)(2,1)}, u32[]{:S(2)}) %copy-start.2) | copy-done | bytes 294936
  17.6 22.3 %inner.1 = (f32[8,3,2,48,128]{4,3,2,1,0:T(8,128)S(1)}, bf16[8,2,48,384]{3,2,1,0:T(8,128)(2,1)S(1)}, bf16[2,8,2,48,384]{4,3,2,1,0:T(8,128)(2,1)S(1)}, f32[8,24,128]{2,1,0:T(8,128)S(1)}, f32[8,24,128]{2,1,0:T(8,128)S(1)}) custom-call(bf16[2,24,4,3,16,128]{5,4,3,2,1,0:T(8,128)(2,1)S(1)} %bitcast.9, bf16[2,4,3,3,16,128]{5,4,3,2,1,0:T(8,128)(2,1)S(1)} %bitcast.10), custom_call_target="tpu_custom_call" | custom-call | flops 40000000000 | bytes 6000000 | tf_op jit(solution)/shard_map/inner/pallas_call | solution.py:263
  39.9 0.0 collective-permute-done.ft_ref
  39.9 0.0 collective-permute-done.1.fz_ref
  39.9 3.2 %outer.1 = (f32[8,2,2,48,128]{4,3,2,1,0:T(8,128)S(1)}, f32[8,128]{1,0:T(8,128)S(1)}, f32[8,128]{1,0:T(8,128)S(1)}) custom-call(bf16[8,2,48,384]{3,2,1,0:T(8,128)(2,1)S(1)} %collective-permute-done.ft_ref, bf16[8,2,48,384]{3,2,1,0:T(8,128)(2,1)S(1)} %collective-permute-done.1.fz_ref, bf16[8,2,48,384]{3,2,1,0:T(8,128)(2,1)S(1)} %get-tuple-element.18.lt_ref, ...), custom_call_target="tpu_custom_call" | custom-call | tf_op jit(solution)/shard_map/outer/pallas_call | solution.py:370
  43.2 0.0 collective-permute-start.4
  43.2 2.1 %collective-permute-start.5 = (f32[8,128]{1,0:T(8,128)S(1)}, f32[8,128]{1,0:T(8,128)S(1)}, u32[]{:S(2)}, u32[]{:S(2)}) collective-permute-start(f32[8,128]{1,0:T(8,128)S(1)} %get-tuple-element.24), channel_id=1, source_target_pairs={{0,1},{1,2},{2,3},{3,4},{4,5},{5,6},{6,7},{7,0},{8,9},{9,10},{10,1... | collective-permute-start | bytes 12296 | tf_op jit(solution)/shard_map/ppermute | solution.py:534
  45.3 0.0 collective-permute-done.2.vt
  45.3 0.0 collective-permute-done.3.vz
  45.3 2.0 %first.1.part = f32[8,128]{1,0:T(8,128)S(1)} custom-call(f32[8,3,2,48,128]{4,3,2,1,0:T(8,128)S(1)} %get-tuple-element.15.inner, f32[8,2,2,48,128]{4,3,2,1,0:T(8,128)S(1)} %get-tuple-element.22.outer, f32[8,128]{1,0:T(8,128)S(1)} %pad.4.vec_ref.vec, f32[8,128]{1,0:T(8,128)S(1)} %collective-permute-done.2.vt, f32[8,128]{1,0:T(8,128)S(1)} %collective-permute-done.3.vz), custom_call_target="tpu_custom_call" | custom-call | tf_op jit(solution)/shard_map/first/pallas_call | solution.py:509
  47.3 1.0 %collective-permute-done.4.rt = f32[8,128]{1,0:T(8,128)S(1)} collective-permute-done((f32[8,128]{1,0:T(8,128)S(1)}, f32[8,128]{1,0:T(8,128)S(1)}, u32[]{:S(2)}, u32[]{:S(2)}) %collective-permute-start.4) | collective-permute-done | bytes 4128 | tf_op jit(solution)/shard_map/ppermute | solution.py:534
  48.3 2.2 %collective-permute-done.5.rz = f32[8,128]{1,0:T(8,128)S(1)} collective-permute-done((f32[8,128]{1,0:T(8,128)S(1)}, f32[8,128]{1,0:T(8,128)S(1)}, u32[]{:S(2)}, u32[]{:S(2)}) %collective-permute-start.5) | collective-permute-done | bytes 4128 | tf_op jit(solution)/shard_map/ppermute | solution.py:534
  50.5 0.6 back.1
  51.1 0.1 collective-permute-start.6
  51.1 0.1 collective-permute-start.7
  51.2 3.8 %collective-permute-start.8 = (f32[8,128]{1,0:T(8,128)S(1)}, f32[8,128]{1,0:T(8,128)S(1)}, u32[]{:S(2)}, u32[]{:S(2)}) collective-permute-start(f32[8,128]{1,0:T(8,128)S(1)} %get-tuple-element.25.vec), channel_id=1, source_target_pairs={{0,120},{8,0},{16,8},{24,16},{32,24},{40,32},{48,40},{56,48},{64,5... | collective-permute-start | bytes 12296 | tf_op jit(solution)/shard_map/ppermute | solution.py:534
  55.0 6.0 %collective-permute-start.9 = (f32[8,128]{1,0:T(8,128)S(1)}, f32[8,128]{1,0:T(8,128)S(1)}, u32[]{:S(2)}, u32[]{:S(2)}) collective-permute-start(f32[8,128]{1,0:T(8,128)S(1)} %get-tuple-element.25.vec), channel_id=1, source_target_pairs={{0,7},{1,0},{2,1},{3,2},{4,3},{5,4},{6,5},{7,6},{8,15},{9,8},{10,9... | collective-permute-start | bytes 12296 | tf_op jit(solution)/shard_map/ppermute | solution.py:534
  60.9 1.9 %blocks.1 = f32[5,8,4608]{2,1,0:T(8,128)} custom-call(f32[8,3,2,48,128]{4,3,2,1,0:T(8,128)S(1)} %get-tuple-element.15.inner, f32[8,2,2,48,128]{4,3,2,1,0:T(8,128)S(1)} %get-tuple-element.22.outer), custom_call_target="tpu_custom_call" | custom-call | bytes 6000000 | tf_op jit(solution)/shard_map/blocks/pallas_call | solution.py:521
  62.9 0.9 %local.1.part = f32[8,128]{1,0:T(8,128)S(1)} custom-call(f32[8,3,2,48,128]{4,3,2,1,0:T(8,128)S(1)} %get-tuple-element.15.inner, f32[8,128]{1,0:T(8,128)S(1)} %get-tuple-element.25.vec), custom_call_target="tpu_custom_call" | custom-call | tf_op jit(solution)/shard_map/local/pallas_call | solution.py:509
  63.8 0.0 collective-permute-done.6.rt
  63.8 0.0 collective-permute-done.7.rz
  63.8 0.0 collective-permute-done.8.vt
  63.8 0.0 collective-permute-done.9.vz
  63.8 0.5 last.1
  64.3 0.6 slice_bitcast_fusion
Async XLA Ops:
  1.3 44.0 %collective-permute-start.2 = (f32[8,128]{1,0:T(8,128)S(1)}, f32[8,128]{1,0:T(8,128)S(1)}, u32[]{:S(2)}, u32[]{:S(2)}) collective-permute-start(f32[8,128]{1,0:T(8,128)S(1)} %pad.4.vec_ref.vec), channel_id=1, source_target_pairs={{0,120},{8,0},{16,8},{24,16},{32,24},{40,32},{48,40},{56,48},{64,5... | collective-permute-start | bytes 12296 | tf_op jit(solution)/shard_map/ppermute | solution.py:534
  4.6 40.7 %collective-permute-start.3 = (f32[8,128]{1,0:T(8,128)S(1)}, f32[8,128]{1,0:T(8,128)S(1)}, u32[]{:S(2)}, u32[]{:S(2)}) collective-permute-start(f32[8,128]{1,0:T(8,128)S(1)} %pad.4.vec_ref.vec), channel_id=1, source_target_pairs={{0,7},{1,0},{2,1},{3,2},{4,3},{5,4},{6,5},{7,6},{8,15},{9,8},{10,9... | collective-permute-start | bytes 12296 | tf_op jit(solution)/shard_map/ppermute | solution.py:534
  11.0 1.7 %copy-start = (bf16[2,24,4,3,4,4,128]{6,5,4,3,2,1,0:T(4,128)(2,1)S(1)}, bf16[2,24,4,3,4,4,128]{6,5,4,3,2,1,0:T(4,128)(2,1)}, u32[]{:S(2)}) copy-start(bf16[2,24,4,3,4,4,128]{6,5,4,3,2,1,0:T(4,128)(2,1)} %param.3) | copy-start | bytes 7077892
  12.7 4.0 %copy-start.1 = (bf16[2,24,4,3,4,4,128]{6,5,4,3,2,1,0:T(4,128)(2,1)S(1)}, bf16[2,24,4,3,4,4,128]{6,5,4,3,2,1,0:T(4,128)(2,1)}, u32[]{:S(2)}) copy-start(bf16[2,24,4,3,4,4,128]{6,5,4,3,2,1,0:T(4,128)(2,1)} %param.3) | copy-start | bytes 7077892
  15.0 25.0 %collective-permute-start = (bf16[8,2,48,384]{3,2,1,0:T(8,128)(2,1)S(1)}, bf16[8,2,48,384]{3,2,1,0:T(8,128)(2,1)S(1)}, u32[]{:S(2)}, u32[]{:S(2)}) collective-permute-start(bf16[8,2,48,384]{3,2,1,0:T(8,128)(2,1)S(1)} %get-tuple-element.16), channel_id=1, source_target_pairs={{0,120},{8,0},{16,8},{24,16},{32,24},{40,32},{48,40},{56,48},{64,5... | collective-permute-start | bytes 1769480 | tf_op jit(solution)/shard_map/ppermute | solution.py:534
  15.0 24.9 %collective-permute-start.1 = (bf16[8,2,48,384]{3,2,1,0:T(8,128)(2,1)S(1)}, bf16[8,2,48,384]{3,2,1,0:T(8,128)(2,1)S(1)}, u32[]{:S(2)}, u32[]{:S(2)}) collective-permute-start(bf16[8,2,48,384]{3,2,1,0:T(8,128)(2,1)S(1)} %get-tuple-element.17), channel_id=1, source_target_pairs={{0,7},{1,0},{2,1},{3,2},{4,3},{5,4},{6,5},{7,6},{8,15},{9,8},{10,9... | collective-permute-start | bytes 1769480 | tf_op jit(solution)/shard_map/ppermute | solution.py:534
  16.7 1.0 %copy-start.2 = (bf16[2,4,3,3,4,4,128]{6,5,4,3,2,1,0:T(4,128)(2,1)S(1)}, bf16[2,4,3,3,4,4,128]{6,5,4,3,2,1,0:T(4,128)(2,1)}, u32[]{:S(2)}) copy-start(bf16[2,4,3,3,4,4,128]{6,5,4,3,2,1,0:T(4,128)(2,1)} %param.4) | copy-start | bytes 884740
  43.2 5.2 %collective-permute-start.4 = (f32[8,128]{1,0:T(8,128)S(1)}, f32[8,128]{1,0:T(8,128)S(1)}, u32[]{:S(2)}, u32[]{:S(2)}) collective-permute-start(f32[8,128]{1,0:T(8,128)S(1)} %get-tuple-element.23), channel_id=1, source_target_pairs={{0,8},{8,16},{16,24},{24,32},{32,40},{40,48},{48,56},{56,64},{64,7... | collective-permute-start | bytes 12296 | tf_op jit(solution)/shard_map/ppermute | solution.py:534
  43.2 7.3 %collective-permute-start.5 = (f32[8,128]{1,0:T(8,128)S(1)}, f32[8,128]{1,0:T(8,128)S(1)}, u32[]{:S(2)}, u32[]{:S(2)}) collective-permute-start(f32[8,128]{1,0:T(8,128)S(1)} %get-tuple-element.24), channel_id=1, source_target_pairs={{0,1},{1,2},{2,3},{3,4},{4,5},{5,6},{6,7},{7,0},{8,9},{9,10},{10,1... | collective-permute-start | bytes 12296 | tf_op jit(solution)/shard_map/ppermute | solution.py:534
  51.1 12.7 %collective-permute-start.6 = (f32[8,128]{1,0:T(8,128)S(1)}, f32[8,128]{1,0:T(8,128)S(1)}, u32[]{:S(2)}, u32[]{:S(2)}) collective-permute-start(f32[8,128]{1,0:T(8,128)S(1)} %get-tuple-element.26), channel_id=1, source_target_pairs={{0,8},{8,16},{16,24},{24,32},{32,40},{40,48},{48,56},{56,64},{64,7... | collective-permute-start | bytes 12296 | tf_op jit(solution)/shard_map/ppermute | solution.py:534
  51.1 12.7 %collective-permute-start.7 = (f32[8,128]{1,0:T(8,128)S(1)}, f32[8,128]{1,0:T(8,128)S(1)}, u32[]{:S(2)}, u32[]{:S(2)}) collective-permute-start(f32[8,128]{1,0:T(8,128)S(1)} %get-tuple-element.27), channel_id=1, source_target_pairs={{0,1},{1,2},{2,3},{3,4},{4,5},{5,6},{6,7},{7,0},{8,9},{9,10},{10,1... | collective-permute-start | bytes 12296 | tf_op jit(solution)/shard_map/ppermute | solution.py:534
  51.2 12.6 %collective-permute-start.8 = (f32[8,128]{1,0:T(8,128)S(1)}, f32[8,128]{1,0:T(8,128)S(1)}, u32[]{:S(2)}, u32[]{:S(2)}) collective-permute-start(f32[8,128]{1,0:T(8,128)S(1)} %get-tuple-element.25.vec), channel_id=1, source_target_pairs={{0,120},{8,0},{16,8},{24,16},{32,24},{40,32},{48,40},{56,48},{64,5... | collective-permute-start | bytes 12296 | tf_op jit(solution)/shard_map/ppermute | solution.py:534
  55.0 8.8 %collective-permute-start.9 = (f32[8,128]{1,0:T(8,128)S(1)}, f32[8,128]{1,0:T(8,128)S(1)}, u32[]{:S(2)}, u32[]{:S(2)}) collective-permute-start(f32[8,128]{1,0:T(8,128)S(1)} %get-tuple-element.25.vec), channel_id=1, source_target_pairs={{0,7},{1,0},{2,1},{3,2},{4,3},{5,4},{6,5},{7,6},{8,15},{9,8},{10,9... | collective-permute-start | bytes 12296 | tf_op jit(solution)/shard_map/ppermute | solution.py:534

commit v4 on v3

--- a/solution.py
+++ b/solution.py
@@ -54,35 +54,10 @@
 
 
 def inner_kernel(
-    v_ref, u_ref, out_ref, lt_ref, lz_ref, ut_ref, uz_ref, vm, uf, cm, flat, kept
+    v_ref, u_hbm, out_ref, lt_ref, lz_ref, ut_ref, uz_ref, vm, uf, cm, flat, kept, u_ref, sem
 ):
-    flat[...] = jnp.zeros_like(flat)
-
-    @pl.loop(0, 4)
-    def _(mu):
-        for c in range(3):
-            for d in range(3):
-                for ri in range(2):
-                    row = ((c * 3 + d) * 2 + ri) * 16
-                    flat[0, pl.ds(row, 16), :] = 0.5 * u_ref[ri, mu, c, d].astype(F32)
-
-        drop = ((lane_ids(24) & 12) == 12) & (mu == 1)
-
-        def load(t, plane):
-            first = plane % 4 * 4 + 3 if t == 4 else t * 4 + plane % 4
-            return flat[0, pl.ds(first, 24, stride=16), :]
-
-        for group in ((0, 1), (2, 3), (4,)):
-            done = exchange([[load(t, plane) for plane in range(8)] for t in group])
-            for t, values in zip(group, done):
-                for a, value in enumerate(values):
-                    uf[a, mu, t] = value if t == 4 else jnp.where(drop, 0.0, value)
-
-    for a in range(8):
-        uz_ref[a] = uf[a, 1, 4]
-
-    for a in range(8):
-        ut_ref[a] = uf[a, 0, 3]
+    fetch = pltpu.make_async_copy(u_hbm, u_ref, sem)
+    fetch.start()
 
     @pl.loop(0, 6)
     def _(step):
@@ -123,6 +98,36 @@
     for a in range(8):
         for chi in range(2):
             lt_ref[a, chi] = vm[0, a, chi, :, 9 * 128 :]
+
+    fetch.wait()
+
+    flat[...] = jnp.zeros_like(flat)
+
+    @pl.loop(0, 4)
+    def _(mu):
+        for c in range(3):
+            for d in range(3):
+                for ri in range(2):
+                    row = ((c * 3 + d) * 2 + ri) * 16
+                    flat[0, pl.ds(row, 16), :] = 0.5 * u_ref[ri, mu, c, d].astype(F32)
+
+        drop = ((lane_ids(24) & 12) == 12) & (mu == 1)
+
+        def load(t, plane):
+            first = plane % 4 * 4 + 3 if t == 4 else t * 4 + plane % 4
+            return flat[0, pl.ds(first, 24, stride=16), :]
+
+        for group in ((0, 1), (2, 3), (4,)):
+            done = exchange([[load(t, plane) for plane in range(8)] for t in group])
+            for t, values in zip(group, done):
+                for a, value in enumerate(values):
+                    uf[a, mu, t] = value if t == 4 else jnp.where(drop, 0.0, value)
+
+    for a in range(8):
+        uz_ref[a] = uf[a, 1, 4]
+
+    for a in range(8):
+        ut_ref[a] = uf[a, 0, 3]
 
     cm[...] = jnp.zeros_like(cm)
 
@@ -269,7 +274,7 @@
             shape((8, 24, 128), F32),
             shape((8, 24, 128), F32),
         ),
-        in_specs=[vmem] * 2,
+        in_specs=[vmem, pl.BlockSpec(memory_space=pltpu.HBM)],
         out_specs=(vmem,) * 5,
         scratch_shapes=[
             pltpu.VMEM((4, 8, 2, ROWS, 1536), BF16),
@@ -277,19 +282,31 @@
             pltpu.VMEM((2, 3, 128, 1536), BF16),
             pltpu.VMEM((2, 768, 128), F32),
             pltpu.VMEM((384, 128), F32),
+            pltpu.VMEM((2, 4, 3, 3, 16, 128), BF16),
+            pltpu.SemaphoreType.DMA,
         ],
         compiler_params=pltpu.CompilerParams(vmem_limit_bytes=24 * 1024 * 1024),
         cost_estimate=pl.CostEstimate(
             flops=40_000_000_000, bytes_accessed=6_000_000, transcendentals=0
         ),
         name="inner",
-    )(vectors, links)
-
-
-def face_kernel(v_ref, t_ref, z_ref, flat):
+    )(vectors, pltpu.with_memory_space_constraint(links, pltpu.HBM))
+
+
+def face_kernel(v_hbm, phi_hbm, t_ref, z_ref, vec_ref, flat, v_ref, phi_ref, sem):
+    def fetch(chi, c, k):
+        part = (slice(None), slice(None), pl.ds(2 * chi, 2), c)
+        return pltpu.make_async_copy(v_hbm.at[part], v_ref.at[part], sem.at[k])
+
+    for k in range(6):
+        fetch(k // 3, k % 3, k).start()
+    small = pltpu.make_async_copy(phi_hbm, phi_ref, sem.at[6])
+    small.start()
+
     @pl.loop(0, 6)
     def _(step):
         chi, c = step // 3, step % 3
+        fetch(chi, c, step).wait()
         for sb in range(2):
             for ri in range(2):
                 block = v_ref[ri, :, 2 * chi + sb, c].astype(F32)
@@ -302,21 +319,43 @@
         done = exchange([[load(k, plane) for plane in range(8)] for k in range(2)])
         for out, values in zip((t_ref, z_ref), done):
             for a, value in enumerate(values):
-                out[a, chi, :, pl.ds(column, 128)] = value
-
-
-def face_call(vectors):
-    face = jax.ShapeDtypeStruct((8, 2, ROWS, 384), BF16)
+                out[a * 2 + chi, :, pl.ds(column, 128)] = value
+
+    small.wait()
+    vec = jnp.concatenate([phi_ref[...], jnp.zeros((8, 32), F32)], 1)
+    vec_ref[...] = vec
+    pieces = []
+    for _ in range(3):
+        piece = vec.astype(BF16)
+        vec = vec - piece.astype(F32)
+        pieces += [piece, jnp.zeros((8, 128), BF16)]
+    rider = jnp.concatenate([p.astype(F32) for p in pieces], 0).astype(BF16)
+    for ref in (t_ref, z_ref):
+        ref[16, :, 0:128] = rider
+        ref[16, :, 128:384] = jnp.zeros((ROWS, 256), BF16)
+
+
+def ridden(face):
+    return sum(face[16, 16 * k : 16 * k + 16, 0:128].astype(F32)[:8] for k in range(3))
+
+
+def face_call(vectors, phi):
+    face = jax.ShapeDtypeStruct((17, ROWS, 384), BF16)
     vmem = pl.BlockSpec(memory_space=pltpu.VMEM)
     return pl.pallas_call(
         face_kernel,
-        out_shape=(face, face),
-        in_specs=[vmem],
-        out_specs=(vmem, vmem),
-        scratch_shapes=[pltpu.VMEM((2, 768, 128), F32)],
+        out_shape=(face, face, jax.ShapeDtypeStruct((8, 128), F32)),
+        in_specs=[pl.BlockSpec(memory_space=pltpu.HBM)] * 2,
+        out_specs=(vmem,) * 3,
+        scratch_shapes=[
+            pltpu.VMEM((2, 768, 128), F32),
+            pltpu.VMEM((2, NV, 4, 3, 16, 128), BF16),
+            pltpu.VMEM((8, 2 * ROWS), F32),
+            pltpu.SemaphoreType.DMA((7,)),
+        ],
         compiler_params=pltpu.CompilerParams(vmem_limit_bytes=12 * 1024 * 1024),
         name="faces",
-    )(vectors)
+    )(*(pltpu.with_memory_space_constraint(x, pltpu.HBM) for x in (vectors, phi)))
 
 
 def outer_kernel(ft_ref, fz_ref, lt_ref, lz_ref, ut_ref, uz_ref, vec_ref, out_ref, bt_ref, bz_ref, cm):
@@ -329,7 +368,7 @@
                 link = [links[a, pl.ds(k, 1), :] for k in range(18)]
                 vector = []
                 for d in range(3):
-                    value = face[a, chi, :, d * 128 : (d + 1) * 128].astype(F32)
+                    value = face[a * 2 + chi, :, d * 128 : (d + 1) * 128].astype(F32)
                     vector += [value[:NV], value[NV:]]
                 for c, both in enumerate(colour(link, vector)):
                     column = slice(c * 128, (c + 1) * 128)
@@ -440,19 +479,21 @@
         part_ref[pl.ds(a, 1), :] = own[a] + kept[(a + 7) % 8]
 
 
-def ahead_apply(outer, vt, vz, part_ref):
+def ahead_apply(outer, vt, vz):
     eye = eye_mask()
-    for a in range(8):
-        ft = forward((outer[a, 0, 0], outer[a, 0, 1]), vt[pl.ds(a, 1), :])
-        fz = forward((outer[a, 1, 0], outer[a, 1, 1]), vz[pl.ds(a, 1), :])
+    rows = []
+    for a in range(8):
+        ft = forward((outer[a, 0, 0], outer[a, 0, 1]), vt[a : a + 1])
+        fz = forward((outer[a, 1, 0], outer[a, 1, 1]), vz[a : a + 1])
         real = jnp.sum(ft[0] + fz[0], axis=1, keepdims=True)
         imag = jnp.sum(ft[1] + fz[1], axis=1, keepdims=True)
-        part_ref[pl.ds(a, 1), :] += joined(row_of(real, eye), row_of(imag, eye))
-
-
-def first_kernel(inner, outer, vec, vt, vz, part_ref):
+        rows.append(joined(row_of(real, eye), row_of(imag, eye)))
+    return jnp.concatenate(rows, 0)
+
+
+def first_kernel(inner, outer, vec, ft, fz, part_ref):
     local_apply(inner, vec, part_ref)
-    ahead_apply(outer, vt, vz, part_ref)
+    part_ref[...] += ahead_apply(outer, ridden(ft), ridden(fz))
 
 
 def back_kernel(outer, part, rt, rz, vec_ref, bt_ref, bz_ref):
@@ -469,8 +510,8 @@
 
 
 def last_kernel(outer, part, rt, rz, vt, vz, out_ref):
-    out_ref[...] = part[...] + rt[...] + rz[...]
-    ahead_apply(outer, vt, vz, out_ref)
+    total = part[...] + rt[...] + rz[...] + ahead_apply(outer, vt[...], vz[...])
+    out_ref[...] = total[:, : 2 * ROWS]
 
 
 def blocks_kernel(inner, outer, out_ref):
@@ -503,9 +544,9 @@
     return jnp.concatenate(tiles, 1)
 
 
-def small_call(kernel, count, name, *args):
+def small_call(kernel, count, name, *args, width=128):
     vmem = pl.BlockSpec(memory_space=pltpu.VMEM)
-    row = jax.ShapeDtypeStruct((8, 128), F32)
+    row = jax.ShapeDtypeStruct((8, width), F32)
     return pl.pallas_call(
         kernel,
         out_shape=(row,) * count,
@@ -537,23 +578,20 @@
 def per_device(null_vectors, gauge_links, coarse_in):
     vectors = null_vectors.reshape(2, NV, 4, 3, 16, 128)
     links = gauge_links.reshape(2, 4, 3, 3, 16, 128)
-    vec = jnp.pad(coarse_in.reshape(8, 2 * ROWS), ((0, 0), (0, 32)))
-    face_t, face_z = face_call(vectors)
-    face_z = shifted(face_z, "sa", -1)
-    face_t = shifted(face_t, "ta", -1)
-    vec_t, vec_z = shifted(vec, "ta", -1), shifted(vec, "sa", -1)
+    face_t, face_z, vec = face_call(vectors, coarse_in.reshape(8, 2 * ROWS))
+    face_t, face_z = shifted(face_t, "ta", -1), shifted(face_z, "sa", -1)
     inner, left_t, left_z, link_t, link_z = inner_call(vectors, links)
     outer, bt, bz = outer_call(face_t, face_z, left_t, left_z, link_t, link_z, vec)
-    rz, rt = shifted(bz, "sa", 1), shifted(bt, "ta", 1)
-    (part,) = small_call(first_kernel, 1, "first", inner, outer, vec, vec_t, vec_z)
+    rt, rz = shifted(bt, "ta", 1), shifted(bz, "sa", 1)
+    (part,) = small_call(first_kernel, 1, "first", inner, outer, vec, face_t, face_z)
     once, bt, bz = small_call(back_kernel, 3, "back", outer, part, rt, rz)
-    vec_z, vec_t = shifted(once, "sa", -1), shifted(once, "ta", -1)
-    rz, rt = shifted(bz, "sa", 1), shifted(bt, "ta", 1)
+    vec_t, rt = shifted(once, "ta", -1), shifted(bt, "ta", 1)
+    vec_z, rz = shifted(once, "sa", -1), shifted(bz, "sa", 1)
     (part,) = small_call(local_apply, 1, "local", inner, once)
     blocks = blocks_call(inner, outer)
-    (twice,) = small_call(last_kernel, 1, "last", outer, part, rt, rz, vec_t, vec_z)
+    (twice,) = small_call(last_kernel, 1, "last", outer, part, rt, rz, vec_t, vec_z, width=2 * ROWS)
     blocks = jnp.swapaxes(blocks, 0, 1)
-    return blocks.reshape(1, 1, 8, 5, 2 * ROWS * ROWS), twice[:, : 2 * ROWS].reshape(1, 1, 8, 2 * ROWS)
+    return blocks.reshape(1, 1, 8, 5, 2 * ROWS * ROWS), twice.reshape(1, 1, 8, 2 * ROWS)
 
 
 def solution(mesh):

time: 65.1 us -> 60.4 us (0.928)
  starting transfers between devices: 23.4 us -> 18.8 us
  local copies, waits for them, and re-layouts: 3.92 us -> 0.01 us
  waiting for transfers between devices: 3.19 us -> 5.25 us
  Pallas kernels: 33.7 us -> 35.5 us
    ppermute x10 -> x8, starting transfers between devices: 23.4 us -> 18.8 us  [shifted(): lax.ppermute(value, axis, [(k, (k + steps) % count) for k in range(count)])]
    unnamed x6 -> x2, local copies, waits for them, and re-layouts: 2.63 us -> 0.01 us
    ppermute x10 -> x8, waiting for transfers between devices: 3.19 us -> 5.25 us  [shifted(): lax.ppermute(value, axis, [(k, (k + steps) % count) for k in range(count)])]
    pallas_call x1, Pallas kernels: 2.3 us -> 3.54 us  [face_call(): pl.pallas_call(face_kernel, out_shape=(face, face, jax.ShapeDtypeStruct((...]
    pad x1 -> x0, local copies, waits for them, and re-layouts: 0.69 us -> none  [per_device(): vec = jnp.pad(coarse_in.reshape(8, 2 * ROWS), ((0, 0), (0, 32)))]
  transfers between devices with their start and end apart: 10 -> 8, of which waited for: 2 -> 2; matrix products, arithmetic and copies ran while one was open for 0% -> 0% of each run, Pallas kernels for 50% -> 45%
where the time goes in v4:
time: 60.4 us; the launch traced here: 60.3 us
  Pallas kernels  35.5 us (59%)
  starting transfers between devices  18.8 us (31%)
  waiting for transfers between devices  5.25 us (9%)
  between operations  0.75 us (1%)
    pallas_call x1, Pallas kernels, inner_call(): pl.pallas_call(inner_kernel, out_shape=(shape((8, 3, 2, ROWS, 128), F32),...  22.3 us
    ppermute x8, starting transfers between devices, shifted(): lax.ppermute(value, axis, [(k, (k + steps) % count) for k in range(count)])  18.8 us
    ppermute x8, waiting for transfers between devices, shifted(): lax.ppermute(value, axis, [(k, (k + steps) % count) for k in range(count)])  5.25 us
    pallas_call x4, Pallas kernels, small_call(): pl.pallas_call(kernel, out_shape=(row,) * count, in_specs=[vmem] * len(ar...  4.51 us
    pallas_call x1, Pallas kernels, face_call(): pl.pallas_call(face_kernel, out_shape=(face, face, jax.ShapeDtypeStruct((...  3.54 us
    pallas_call x1, Pallas kernels, outer_call(): pl.pallas_call(outer_kernel, out_shape=(jax.ShapeDtypeStruct((8, 2, 2, RO...  3.23 us
    pallas_call x1, Pallas kernels, blocks_call(): pl.pallas_call(blocks_kernel, out_shape=jax.ShapeDtypeStruct((5, 8, 2 * R...  1.95 us
  transfers between devices with their start and end apart: 8, of which 2 were waited for; matrix products, arithmetic and copies ran while one was open for 0% of the time, Pallas kernels for 45%

profile of v4, /device:TPU:0, one launch (start us, length us, event | category | flops | bytes accessed | tf_op | source)
XLA Modules:
  0.0 60.3 jit_solution(866719804479935478)
XLA Ops:
  0.6 0.0 copy-start
  0.6 3.5 %faces.1 = (bf16[17,48,384]{2,1,0:T(8,128)(2,1)S(1)}, bf16[17,48,384]{2,1,0:T(8,128)(2,1)S(1)}, f32[8,128]{1,0:T(8,128)S(1)}) custom-call(bf16[2,24,4,3,16,128]{5,4,3,2,1,0:T(8,128)(2,1)} %bitcast.7, f32[8,96]{1,0:T(8,128)} %bitcast.10), custom_call_target="tpu_custom_call" | custom-call | tf_op jit(solution)/shard_map/faces/pallas_call | solution.py:345
  4.2 3.4 %collective-permute-start = (bf16[17,48,384]{2,1,0:T(8,128)(2,1)S(1)}, bf16[17,48,384]{2,1,0:T(8,128)(2,1)S(1)}, u32[]{:S(2)}, u32[]{:S(2)}) collective-permute-start(bf16[17,48,384]{2,1,0:T(8,128)(2,1)S(1)} %get-tuple-element.17), channel_id=1, source_target_pairs={{0,120},{8,0},{16,8},{24,16},{32,24},{40,32},{48,40},{56,48},{64,5... | collective-permute-start | bytes 1880072 | tf_op jit(solution)/shard_map/ppermute | solution.py:575
  7.5 6.4 %collective-permute-start.1 = (bf16[17,48,384]{2,1,0:T(8,128)(2,1)S(1)}, bf16[17,48,384]{2,1,0:T(8,128)(2,1)S(1)}, u32[]{:S(2)}, u32[]{:S(2)}) collective-permute-start(bf16[17,48,384]{2,1,0:T(8,128)(2,1)S(1)} %get-tuple-element.18), channel_id=1, source_target_pairs={{0,7},{1,0},{2,1},{3,2},{4,3},{5,4},{6,5},{7,6},{8,15},{9,8},{10,9... | collective-permute-start | bytes 1880072 | tf_op jit(solution)/shard_map/ppermute | solution.py:575
  13.9 0.0 copy-done
  13.9 22.3 %inner.1 = (f32[8,3,2,48,128]{4,3,2,1,0:T(8,128)S(1)}, bf16[8,2,48,384]{3,2,1,0:T(8,128)(2,1)S(1)}, bf16[2,8,2,48,384]{4,3,2,1,0:T(8,128)(2,1)S(1)}, f32[8,24,128]{2,1,0:T(8,128)S(1)}, f32[8,24,128]{2,1,0:T(8,128)S(1)}) custom-call(bf16[2,24,4,3,16,128]{5,4,3,2,1,0:T(8,128)(2,1)S(1)} %bitcast.8, bf16[2,4,3,3,16,128]{5,4,3,2,1,0:T(8,128)(2,1)} %bitcast.12), custom_call_target="tpu_custom_call" | custom-call | flops 40000000000 | bytes 6000000 | tf_op jit(solution)/shard_map/inner/pallas_call | solution.py:268
  36.2 0.0 collective-permute-done.ft_ref.ft
  36.2 0.0 collective-permute-done.1.fz_ref.fz
  36.2 3.2 %outer.1 = (f32[8,2,2,48,128]{4,3,2,1,0:T(8,128)S(1)}, f32[8,128]{1,0:T(8,128)S(1)}, f32[8,128]{1,0:T(8,128)S(1)}) custom-call(bf16[17,48,384]{2,1,0:T(8,128)(2,1)S(1)} %collective-permute-done.ft_ref.ft, bf16[17,48,384]{2,1,0:T(8,128)(2,1)S(1)} %collective-permute-done.1.fz_ref.fz, bf16[8,2,48,384]{3,2,1,0:T(8,128)(2,1)S(1)} %get-tuple-element.19.lt_ref, ...), custom_call_target="tpu_custom_call" | custom-call | tf_op jit(solution)/shard_map/outer/pallas_call | solution.py:409
  39.5 0.0 collective-permute-start.2
  39.5 0.1 collective-permute-start.3
  39.6 2.0 %first.1.part = f32[8,128]{1,0:T(8,128)S(1)} custom-call(f32[8,3,2,48,128]{4,3,2,1,0:T(8,128)S(1)} %get-tuple-element.16.inner, f32[8,2,2,48,128]{4,3,2,1,0:T(8,128)S(1)} %get-tuple-element.24.outer, f32[8,128]{1,0:T(8,128)S(1)} %get-tuple-element.23.vec_ref.vec, bf16[17,48,384]{2,1,0:T(8,128)(2,1)S(1)} %collective-permute-done.ft_ref.ft, ...), custom_call_target="tpu_custom_call" | custom-call | tf_op jit(solution)/shard_map/first/pallas_call | solution.py:550
  41.6 3.1 %collective-permute-done.2.rt = f32[8,128]{1,0:T(8,128)S(1)} collective-permute-done((f32[8,128]{1,0:T(8,128)S(1)}, f32[8,128]{1,0:T(8,128)S(1)}, u32[]{:S(2)}, u32[]{:S(2)}) %collective-permute-start.2) | collective-permute-done | bytes 4128 | tf_op jit(solution)/shard_map/ppermute | solution.py:575
  44.6 2.2 %collective-permute-done.3.rz = f32[8,128]{1,0:T(8,128)S(1)} collective-permute-done((f32[8,128]{1,0:T(8,128)S(1)}, f32[8,128]{1,0:T(8,128)S(1)}, u32[]{:S(2)}, u32[]{:S(2)}) %collective-permute-start.3) | collective-permute-done | bytes 4128 | tf_op jit(solution)/shard_map/ppermute | solution.py:575
  46.8 0.6 back.1
  47.4 0.1 collective-permute-start.4
  47.4 0.1 collective-permute-start.5
  47.5 5.6 %collective-permute-start.7 = (f32[8,128]{1,0:T(8,128)S(1)}, f32[8,128]{1,0:T(8,128)S(1)}, u32[]{:S(2)}, u32[]{:S(2)}) collective-permute-start(f32[8,128]{1,0:T(8,128)S(1)} %get-tuple-element.27.vec), channel_id=1, source_target_pairs={{0,7},{1,0},{2,1},{3,2},{4,3},{5,4},{6,5},{7,6},{8,15},{9,8},{10,9... | collective-permute-start | bytes 12296 | tf_op jit(solution)/shard_map/ppermute | solution.py:575
  53.1 3.2 %collective-permute-start.6 = (f32[8,128]{1,0:T(8,128)S(1)}, f32[8,128]{1,0:T(8,128)S(1)}, u32[]{:S(2)}, u32[]{:S(2)}) collective-permute-start(f32[8,128]{1,0:T(8,128)S(1)} %get-tuple-element.27.vec), channel_id=1, source_target_pairs={{0,120},{8,0},{16,8},{24,16},{32,24},{40,32},{48,40},{56,48},{64,5... | collective-permute-start | bytes 12296 | tf_op jit(solution)/shard_map/ppermute | solution.py:575
  56.4 1.9 %blocks.1 = f32[5,8,4608]{2,1,0:T(8,128)} custom-call(f32[8,3,2,48,128]{4,3,2,1,0:T(8,128)S(1)} %get-tuple-element.16.inner, f32[8,2,2,48,128]{4,3,2,1,0:T(8,128)S(1)} %get-tuple-element.24.outer), custom_call_target="tpu_custom_call" | custom-call | bytes 6000000 | tf_op jit(solution)/shard_map/blocks/pallas_call | solution.py:562
  58.3 0.9 %local.1.part = f32[8,128]{1,0:T(8,128)S(1)} custom-call(f32[8,3,2,48,128]{4,3,2,1,0:T(8,128)S(1)} %get-tuple-element.16.inner, f32[8,128]{1,0:T(8,128)S(1)} %get-tuple-element.27.vec), custom_call_target="tpu_custom_call" | custom-call | tf_op jit(solution)/shard_map/local/pallas_call | solution.py:550
  59.2 0.0 collective-permute-done.4.rt
  59.2 0.0 collective-permute-done.5.rz
  59.2 0.0 collective-permute-done.7.vz
  59.2 0.0 collective-permute-done.6.vt
  59.2 1.1 %last.1 = f32[8,96]{1,0:T(8,128)} custom-call(f32[8,2,2,48,128]{4,3,2,1,0:T(8,128)S(1)} %get-tuple-element.24.outer, f32[8,128]{1,0:T(8,128)S(1)} %local.1.part, f32[8,128]{1,0:T(8,128)S(1)} %collective-permute-done.4.rt, f32[8,128]{1,0:T(8,128)S(1)} %collective-permute-done.5.rz, f32[8,128]{1,0:T(8,128)S(1)} %collective-permute-done.6.vt, ...), custom_call_target="tpu_custom_call" | custom-call | tf_op jit(solution)/shard_map/last/pallas_call | solution.py:550
Async XLA Ops:
  0.6 13.3 %copy-start = (bf16[2,24,4,3,4,4,128]{6,5,4,3,2,1,0:T(4,128)(2,1)S(1)}, bf16[2,24,4,3,4,4,128]{6,5,4,3,2,1,0:T(4,128)(2,1)}, u32[]{:S(2)}) copy-start(bf16[2,24,4,3,4,4,128]{6,5,4,3,2,1,0:T(4,128)(2,1)} %param.3) | copy-start | bytes 7077892
  4.2 32.0 %collective-permute-start = (bf16[17,48,384]{2,1,0:T(8,128)(2,1)S(1)}, bf16[17,48,384]{2,1,0:T(8,128)(2,1)S(1)}, u32[]{:S(2)}, u32[]{:S(2)}) collective-permute-start(bf16[17,48,384]{2,1,0:T(8,128)(2,1)S(1)} %get-tuple-element.17), channel_id=1, source_target_pairs={{0,120},{8,0},{16,8},{24,16},{32,24},{40,32},{48,40},{56,48},{64,5... | collective-permute-start | bytes 1880072 | tf_op jit(solution)/shard_map/ppermute | solution.py:575
  7.5 28.7 %collective-permute-start.1 = (bf16[17,48,384]{2,1,0:T(8,128)(2,1)S(1)}, bf16[17,48,384]{2,1,0:T(8,128)(2,1)S(1)}, u32[]{:S(2)}, u32[]{:S(2)}) collective-permute-start(bf16[17,48,384]{2,1,0:T(8,128)(2,1)S(1)} %get-tuple-element.18), channel_id=1, source_target_pairs={{0,7},{1,0},{2,1},{3,2},{4,3},{5,4},{6,5},{7,6},{8,15},{9,8},{10,9... | collective-permute-start | bytes 1880072 | tf_op jit(solution)/shard_map/ppermute | solution.py:575
  39.5 5.2 %collective-permute-start.2 = (f32[8,128]{1,0:T(8,128)S(1)}, f32[8,128]{1,0:T(8,128)S(1)}, u32[]{:S(2)}, u32[]{:S(2)}) collective-permute-start(f32[8,128]{1,0:T(8,128)S(1)} %get-tuple-element.25), channel_id=1, source_target_pairs={{0,8},{8,16},{16,24},{24,32},{32,40},{40,48},{48,56},{56,64},{64,7... | collective-permute-start | bytes 12296 | tf_op jit(solution)/shard_map/ppermute | solution.py:575
  39.5 7.3 %collective-permute-start.3 = (f32[8,128]{1,0:T(8,128)S(1)}, f32[8,128]{1,0:T(8,128)S(1)}, u32[]{:S(2)}, u32[]{:S(2)}) collective-permute-start(f32[8,128]{1,0:T(8,128)S(1)} %get-tuple-element.26), channel_id=1, source_target_pairs={{0,1},{1,2},{2,3},{3,4},{4,5},{5,6},{6,7},{7,0},{8,9},{9,10},{10,1... | collective-permute-start | bytes 12296 | tf_op jit(solution)/shard_map/ppermute | solution.py:575
  47.4 11.8 %collective-permute-start.4 = (f32[8,128]{1,0:T(8,128)S(1)}, f32[8,128]{1,0:T(8,128)S(1)}, u32[]{:S(2)}, u32[]{:S(2)}) collective-permute-start(f32[8,128]{1,0:T(8,128)S(1)} %get-tuple-element.28), channel_id=1, source_target_pairs={{0,8},{8,16},{16,24},{24,32},{32,40},{40,48},{48,56},{56,64},{64,7... | collective-permute-start | bytes 12296 | tf_op jit(solution)/shard_map/ppermute | solution.py:575
  47.4 11.8 %collective-permute-start.5 = (f32[8,128]{1,0:T(8,128)S(1)}, f32[8,128]{1,0:T(8,128)S(1)}, u32[]{:S(2)}, u32[]{:S(2)}) collective-permute-start(f32[8,128]{1,0:T(8,128)S(1)} %get-tuple-element.29), channel_id=1, source_target_pairs={{0,1},{1,2},{2,3},{3,4},{4,5},{5,6},{6,7},{7,0},{8,9},{9,10},{10,1... | collective-permute-start | bytes 12296 | tf_op jit(solution)/shard_map/ppermute | solution.py:575
  47.5 11.7 %collective-permute-start.7 = (f32[8,128]{1,0:T(8,128)S(1)}, f32[8,128]{1,0:T(8,128)S(1)}, u32[]{:S(2)}, u32[]{:S(2)}) collective-permute-start(f32[8,128]{1,0:T(8,128)S(1)} %get-tuple-element.27.vec), channel_id=1, source_target_pairs={{0,7},{1,0},{2,1},{3,2},{4,3},{5,4},{6,5},{7,6},{8,15},{9,8},{10,9... | collective-permute-start | bytes 12296 | tf_op jit(solution)/shard_map/ppermute | solution.py:575
  53.1 6.1 %collective-permute-start.6 = (f32[8,128]{1,0:T(8,128)S(1)}, f32[8,128]{1,0:T(8,128)S(1)}, u32[]{:S(2)}, u32[]{:S(2)}) collective-permute-start(f32[8,128]{1,0:T(8,128)S(1)} %get-tuple-element.27.vec), channel_id=1, source_target_pairs={{0,120},{8,0},{16,8},{24,16},{32,24},{40,32},{48,40},{56,48},{64,5... | collective-permute-start | bytes 12296 | tf_op jit(solution)/shard_map/ppermute | solution.py:575

commit v5 on v4

--- a/solution.py
+++ b/solution.py
@@ -1,3 +1,5 @@
+import functools
+
 import jax
 import jax.numpy as jnp
 from jax import lax
@@ -16,7 +18,7 @@
 
 
 def roll(value, shift):
-    return pltpu.roll(value, shift % 128, 1)
+    return pltpu.roll(value, shift % 128, 1) if shift % 128 else value
 
 
 def exchange_bit(low, high, bit):
@@ -129,43 +131,43 @@
     for a in range(8):
         ut_ref[a] = uf[a, 0, 3]
 
-    cm[...] = jnp.zeros_like(cm)
-
     def fill(a, chi):
         ahead = lax.rem(a + 1, 8)
         x_last = (lane_ids(NV) & 3) == 3
         x_last_pair = (lane_ids(ROWS) & 3) == 3
         y_last = lane_ids(NV) >= 96
+
+        def hop(t, mu):
+            link = [uf[a, mu, t, pl.ds(k, 1), :] for k in range(18)]
+            vector = []
+            for d in range(3):
+                first = (((t + 1) if mu == 0 else t) * 3 + d) * 128
+                value = vm[0, a, chi, :, first : first + 128]
+                if mu == 1:
+                    value = roll(value, -4)
+                elif mu == 2:
+                    value = roll(value, -32)
+                elif mu == 3:
+                    other = vm[0, ahead, chi, :, first : first + 128]
+                    value = jnp.where(x_last_pair, roll(other, 3), roll(value, -1))
+                value = value.astype(F32)
+                vector += [value[:NV], value[NV:]]
+            return colour(link, vector)
+
+        nothing = [(jnp.zeros((NV, 128), F32),) * 2] * 3
         for t in range(4):
-            for mu in range(4):
-                if mu == 0 and t == 3:
-                    continue
-                link = [uf[a, mu, t, pl.ds(k, 1), :] for k in range(18)]
-                vector = []
-                for d in range(3):
-                    first = (((t + 1) if mu == 0 else t) * 3 + d) * 128
-                    value = vm[0, a, chi, :, first : first + 128]
-                    if mu == 1:
-                        value = roll(value, -4)
-                    elif mu == 2:
-                        value = roll(value, -32)
-                    elif mu == 3:
-                        other = vm[0, ahead, chi, :, first : first + 128]
-                        value = jnp.where(x_last_pair, roll(other, 3), roll(value, -1))
-                    value = value.astype(F32)
-                    vector += [value[:NV], value[NV:]]
-                for c, parts in enumerate(colour(link, vector)):
+            for slot in range(3):
+                if slot == 0:
+                    one, two = hop(t, 0) if t < 3 else nothing, hop(t, 1)
+                else:
+                    last = y_last if slot == 1 else x_last
+                    one = hop(t, slot + 1)
+                    two = [[jnp.where(last, -part, 0.0) for part in pair] for pair in one]
+                for c in range(3):
                     column = slice((t * 3 + c) * 128, (t * 3 + c + 1) * 128)
                     for ri in range(2):
-                        if mu < 2:
-                            row = ri * 64 + mu * 32
-                            cm[chi, 0, row : row + 24, column] = parts[ri].astype(BF16)
-                        else:
-                            last = y_last if mu == 2 else x_last
-                            outer = jnp.where(last, -parts[ri], 0.0)
-                            row = ri * 64
-                            cm[chi, mu - 1, row : row + 24, column] = parts[ri].astype(BF16)
-                            cm[chi, mu - 1, row + 32 : row + 56, column] = outer.astype(BF16)
+                        both = jnp.concatenate([one[c][ri], two[c][ri]], 0).astype(BF16)
+                        cm[chi, slot, ri * ROWS : ri * ROWS + ROWS, column] = both
 
     def multiply(a, chi):
         near, far = vm[0, a, chi], vm[0, a, 1 - chi]
@@ -181,7 +183,7 @@
             kept[start : start + rows, : value.shape[1]] = value
 
     def finish(a):
-        first = (kept[0:144, :], kept[144:240, :], kept[240:336, :], kept[336:384, :ROWS])
+        first = (kept[0:144, :96], kept[144:240, :96], kept[240:336, :96], kept[336:384, :ROWS])
         combine_inner([first, multiply(a, 1)], a, out_ref)
 
     fill(0, 0)
@@ -198,68 +200,71 @@
     finish(7)
 
 
-def complex_of(product, sign):
-    return product[:24] + sign * roll(product[24:], 64)
-
-
-def times_i(value, sign):
-    return -sign * roll(value, 64)
+def widened(value):
+    return jnp.concatenate([value, jnp.zeros((value.shape[0], 128 - value.shape[1]), F32)], 1)
+
+
+def other_side(value, half):
+    return jnp.where(lane_ids(value.shape[0]) < half, roll(value, -half), roll(value, half))
+
+
+def sides(half):
+    return jnp.where(lane_ids(NV) < half, 1.0, -1.0).astype(F32)
+
+
+def complex_of(product, half):
+    return product[:NV] + sides(half) * other_side(product[NV:], half)
+
+
+def times_i(value, half):
+    return -sides(half) * other_side(value, half)
 
 
 def combine_inner(blocks, a, out_ref):
-    sign = sides()
-    second = (lane_ids(NV) & 32) != 0
-    upper = {}
-    for chi, (tz, y, x, gram) in enumerate(blocks):
+    lanes = lane_ids(NV)
+    second = ((lanes >= 24) & (lanes < 48)) | (lanes >= 72)
+    upper, grams = {}, [[None, None], [None, None]]
+    zero = jnp.zeros((NV, 128), F32)
+    for chi, products in enumerate(blocks):
+        tz, y, x, gram = (widened(value) for value in products)
         phase = 1.0 if chi == 0 else -1.0
-        z_tz = complex_of(tz[:48], sign)
-        z_y = complex_of(y[:48], sign)
-        z_x = complex_of(x[:48], sign)
-        cross_t = complex_of(tz[48:96], sign)
-        cross_z = phase * times_i(complex_of(tz[96:144], sign), sign)
-        cross_y = phase * complex_of(y[48:96], sign)
-        cross_x = phase * times_i(complex_of(x[48:96], sign), sign)
+        z_tz, z_y, z_x = (complex_of(value[:ROWS], 48) for value in (tz, y, x))
+        cross_t = complex_of(tz[48:96], 48)
+        cross_z = phase * times_i(complex_of(tz[96:144], 48), 48)
+        cross_y = phase * complex_of(y[48:96], 48)
+        cross_x = phase * times_i(complex_of(x[48:96], 48), 48)
         same = -(z_tz + z_y + z_x)
         cross = jnp.where(second, cross_z, cross_t) + cross_y + cross_x
-        same = same + roll(same, -32)
-        cross = cross + roll(cross, -32)
-        gram = jnp.concatenate([gram, jnp.zeros((ROWS, 128 - ROWS), F32)], 1)
-        gram_r = gram[:24] + roll(gram[24:], -24)
-        gram_i = roll(gram[:24], -24) - gram[24:]
-        y_same, y_cross = roll(z_y, -32), -roll(cross_y, -32)
-        x_same, x_cross = roll(z_x, -32), -roll(cross_x, -32)
-        upper[chi, chi] = (same, y_same, x_same, gram_r, gram_i)
-        upper[1 - chi, chi] = (cross, y_cross, x_cross, None, None)
+        same = same + roll(same, -NV)
+        cross = cross + roll(cross, -NV)
+        upper[chi, chi] = same, roll(z_y, -NV), roll(z_x, -NV)
+        upper[1 - chi, chi] = cross, -roll(cross_y, -NV), -roll(cross_x, -NV)
+        grams[chi][chi] = complex_of(gram, NV)
+        grams[chi][1 - chi] = zero
 
     def whole(item, ri):
-        return placed([[upper[row, col][item] for col in range(2)] for row in range(2)], ri)
+        return placed([[upper[row, col][item] for col in range(2)] for row in range(2)], 48 * ri)
 
     first_rows = lax.broadcasted_iota(jnp.int32, (ROWS, 128), 0) < NV
     cols = lane_ids(ROWS)
     flip = jnp.where(first_rows == (cols < NV), 1.0, -1.0).astype(F32)
-    zero = jnp.zeros((NV, 128), F32)
     for ri in range(2):
         out_ref[a, 1, ri] = whole(1, ri)
         out_ref[a, 2, ri] = whole(2, ri)
         inner = whole(0, ri)
         turned = jnp.concatenate([inner, jnp.zeros((80, 128), F32)], 0).T[:ROWS]
         turned = flip * turned if ri == 0 else -flip * turned
-        gram = [[upper[0, 0][3 + ri], zero], [zero, upper[1, 1][3 + ri]]]
-        out_ref[a, 0, ri] = placed(gram, 0) + inner + turned
-
-
-def placed(parts, ri):
+        out_ref[a, 0, ri] = placed(grams, NV * ri) + inner + turned
+
+
+def placed(parts, start):
     lanes = lane_ids(NV)
     left, right = lanes < NV, (lanes >= NV) & (lanes < 2 * NV)
     rows = []
     for row in range(2):
-        second = jnp.where(right, roll(parts[row][1], NV - 64 * ri), 0.0)
-        rows.append(jnp.where(left, roll(parts[row][0], -64 * ri), second))
+        second = jnp.where(right, roll(parts[row][1], NV - start), 0.0)
+        rows.append(jnp.where(left, roll(parts[row][0], -start), second))
     return jnp.concatenate(rows, 0)
-
-
-def sides():
-    return jnp.where(lane_ids(NV) < 64, 1.0, -1.0).astype(F32)
 
 
 def inner_call(vectors, links):
@@ -279,7 +284,7 @@
         scratch_shapes=[
             pltpu.VMEM((4, 8, 2, ROWS, 1536), BF16),
             pltpu.VMEM((8, 4, 5, 24, 128), F32),
-            pltpu.VMEM((2, 3, 128, 1536), BF16),
+            pltpu.VMEM((2, 3, 96, 1536), BF16),
             pltpu.VMEM((2, 768, 128), F32),
             pltpu.VMEM((384, 128), F32),
             pltpu.VMEM((2, 4, 3, 3, 16, 128), BF16),
@@ -319,7 +324,8 @@
         done = exchange([[load(k, plane) for plane in range(8)] for k in range(2)])
         for out, values in zip((t_ref, z_ref), done):
             for a, value in enumerate(values):
-                out[a * 2 + chi, :, pl.ds(column, 128)] = value
+                rows = pl.ds(pl.multiple_of((a * 2 + chi) * ROWS, ROWS), ROWS)
+                out[rows, pl.ds(column, 128)] = value
 
     small.wait()
     vec = jnp.concatenate([phi_ref[...], jnp.zeros((8, 32), F32)], 1)
@@ -328,19 +334,19 @@
     for _ in range(3):
         piece = vec.astype(BF16)
         vec = vec - piece.astype(F32)
-        pieces += [piece, jnp.zeros((8, 128), BF16)]
-    rider = jnp.concatenate([p.astype(F32) for p in pieces], 0).astype(BF16)
+        pieces.append(piece.astype(F32))
+    rider = jnp.concatenate(pieces, 1)
+    rider = jnp.concatenate([rider, jnp.zeros((8, 384), F32)], 0).astype(BF16)
     for ref in (t_ref, z_ref):
-        ref[16, :, 0:128] = rider
-        ref[16, :, 128:384] = jnp.zeros((ROWS, 256), BF16)
+        ref[768:784, :] = rider
 
 
 def ridden(face):
-    return sum(face[16, 16 * k : 16 * k + 16, 0:128].astype(F32)[:8] for k in range(3))
+    return sum(face[768:784, 128 * k : 128 * k + 128].astype(F32)[:8] for k in range(3))
 
 
 def face_call(vectors, phi):
-    face = jax.ShapeDtypeStruct((17, ROWS, 384), BF16)
+    face = jax.ShapeDtypeStruct((784, 384), BF16)
     vmem = pl.BlockSpec(memory_space=pltpu.VMEM)
     return pl.pallas_call(
         face_kernel,
@@ -358,63 +364,57 @@
     )(*(pltpu.with_memory_space_constraint(x, pltpu.HBM) for x in (vectors, phi)))
 
 
-def outer_kernel(ft_ref, fz_ref, lt_ref, lz_ref, ut_ref, uz_ref, vec_ref, out_ref, bt_ref, bz_ref, cm):
-    cm[...] = jnp.zeros_like(cm)
+def outer_kernel(mu, face, *refs):
+    lefts, (links, vec_ref, out_ref, back_ref, cm) = refs[:-5], refs[-5:]
 
     @pl.loop(0, 8)
     def _(a):
         for chi in range(2):
-            for mu, (face, links) in enumerate(((ft_ref, ut_ref), (fz_ref, uz_ref))):
-                link = [links[a, pl.ds(k, 1), :] for k in range(18)]
-                vector = []
-                for d in range(3):
-                    value = face[a * 2 + chi, :, d * 128 : (d + 1) * 128].astype(F32)
-                    vector += [value[:NV], value[NV:]]
-                for c, both in enumerate(colour(link, vector)):
-                    column = slice(c * 128, (c + 1) * 128)
-                    cm[a, chi, mu, 0:24, column] = both[0].astype(BF16)
-                    cm[a, chi, mu, 64:88, column] = both[1].astype(BF16)
-
-    sign = sides()
+            link = [links[a, pl.ds(k, 1), :] for k in range(18)]
+            vector = []
+            rows = pl.ds(pl.multiple_of((a * 2 + chi) * ROWS, ROWS), ROWS)
+            for d in range(3):
+                value = face[rows, d * 128 : (d + 1) * 128].astype(F32)
+                vector += [value[:NV], value[NV:]]
+            for c, both in enumerate(colour(link, vector)):
+                cm[a, chi, :, c * 128 : (c + 1) * 128] = jnp.concatenate(both, 0).astype(BF16)
+
     eye = eye_mask()
     row_sign, col_sign = signs()
     for a in range(8):
-        parts = ([[None, None], [None, None]], [[None, None], [None, None]])
+        parts = [[None, None], [None, None]]
         for chi in range(2):
-            phase = 1.0 if chi == 0 else -1.0
-            for mu in range(2):
-                if mu == 0:
-                    left = jnp.concatenate([lt_ref[a, chi], lt_ref[a, 1 - chi]], 0)
-                else:
-                    left = jnp.concatenate([lz_ref[0, a, chi], lz_ref[1, a, 1 - chi]], 0)
-                product = nt(left, cm[a, chi, mu])
-                cross = complex_of(product[ROWS:], sign)
-                if mu == 1:
-                    cross = phase * times_i(cross, sign)
-                parts[mu][chi][chi] = -complex_of(product[:ROWS], sign)
-                parts[mu][1 - chi][chi] = cross
+            if mu == 0:
+                near, far = lefts[0][a, chi], lefts[0][a, 1 - chi]
+            else:
+                near, far = lefts[0][0, a, chi], lefts[0][1, a, 1 - chi]
+            product = widened(nt(jnp.concatenate([near, far], 0), cm[a, chi]))
+            cross = complex_of(product[ROWS:], NV)
+            if mu == 1:
+                cross = (1.0 if chi == 0 else -1.0) * times_i(cross, NV)
+            parts[chi][chi] = -complex_of(product[:ROWS], NV)
+            parts[1 - chi][chi] = cross
         pr, pi = split(vec_ref[pl.ds(a, 1), :])
         column_r = row_sign * column_of(pr, eye)
         column_i = row_sign * column_of(pi, eye)
-        for mu, back in enumerate((bt_ref, bz_ref)):
-            block = placed(parts[mu], 0), placed(parts[mu], 1)
-            out_ref[a, mu, 0] = block[0]
-            out_ref[a, mu, 1] = block[1]
-            back[pl.ds(a, 1), :] = backward(block, column_r, column_i, col_sign)
-
-
-def outer_call(face_t, face_z, left_t, left_z, link_t, link_z, vec):
+        block = placed(parts, 0), placed(parts, NV)
+        out_ref[a, 0] = block[0]
+        out_ref[a, 1] = block[1]
+        back_ref[pl.ds(a, 1), :] = backward(block, column_r, column_i, col_sign)
+
+
+def outer_call(mu, name, *args):
     vmem = pl.BlockSpec(memory_space=pltpu.VMEM)
-    row = jax.ShapeDtypeStruct((8, 128), F32)
+    shape = jax.ShapeDtypeStruct
     return pl.pallas_call(
-        outer_kernel,
-        out_shape=(jax.ShapeDtypeStruct((8, 2, 2, ROWS, 128), F32), row, row),
-        in_specs=[vmem] * 7,
-        out_specs=(vmem,) * 3,
-        scratch_shapes=[pltpu.VMEM((8, 2, 2, 128, 384), BF16)],
+        functools.partial(outer_kernel, mu),
+        out_shape=(shape((8, 2, ROWS, 128), F32), shape((8, 128), F32)),
+        in_specs=[vmem] * len(args),
+        out_specs=(vmem,) * 2,
+        scratch_shapes=[pltpu.VMEM((8, 2, ROWS, 384), BF16)],
         compiler_params=pltpu.CompilerParams(vmem_limit_bytes=12 * 1024 * 1024),
-        name="outer",
-    )(face_t, face_z, left_t, left_z, link_t, link_z, vec)
+        name=name,
+    )(*args)
 
 
 def signs():
@@ -479,24 +479,24 @@
         part_ref[pl.ds(a, 1), :] = own[a] + kept[(a + 7) % 8]
 
 
-def ahead_apply(outer, vt, vz):
+def ahead_apply(outer_t, outer_z, vt, vz):
     eye = eye_mask()
     rows = []
     for a in range(8):
-        ft = forward((outer[a, 0, 0], outer[a, 0, 1]), vt[a : a + 1])
-        fz = forward((outer[a, 1, 0], outer[a, 1, 1]), vz[a : a + 1])
+        ft = forward((outer_t[a, 0], outer_t[a, 1]), vt[a : a + 1])
+        fz = forward((outer_z[a, 0], outer_z[a, 1]), vz[a : a + 1])
         real = jnp.sum(ft[0] + fz[0], axis=1, keepdims=True)
         imag = jnp.sum(ft[1] + fz[1], axis=1, keepdims=True)
         rows.append(joined(row_of(real, eye), row_of(imag, eye)))
     return jnp.concatenate(rows, 0)
 
 
-def first_kernel(inner, outer, vec, ft, fz, part_ref):
+def first_kernel(inner, outer_t, outer_z, vec, ft, fz, part_ref):
     local_apply(inner, vec, part_ref)
-    part_ref[...] += ahead_apply(outer, ridden(ft), ridden(fz))
-
-
-def back_kernel(outer, part, rt, rz, vec_ref, bt_ref, bz_ref):
+    part_ref[...] += ahead_apply(outer_t, outer_z, ridden(ft), ridden(fz))
+
+
+def back_kernel(outer_t, outer_z, part, rt, rz, vec_ref, bt_ref, bz_ref):
     vec_ref[...] = part[...] + rt[...] + rz[...]
     eye = eye_mask()
     row_sign, col_sign = signs()
@@ -504,24 +504,24 @@
         pr, pi = split(vec_ref[pl.ds(a, 1), :])
         column_r = row_sign * column_of(pr, eye)
         column_i = row_sign * column_of(pi, eye)
-        for mu, back in enumerate((bt_ref, bz_ref)):
-            block = outer[a, mu, 0], outer[a, mu, 1]
+        for outer, back in ((outer_t, bt_ref), (outer_z, bz_ref)):
+            block = outer[a, 0], outer[a, 1]
             back[pl.ds(a, 1), :] = backward(block, column_r, column_i, col_sign)
 
 
-def last_kernel(outer, part, rt, rz, vt, vz, out_ref):
-    total = part[...] + rt[...] + rz[...] + ahead_apply(outer, vt[...], vz[...])
+def last_kernel(outer_t, outer_z, part, rt, rz, vt, vz, out_ref):
+    total = part[...] + rt[...] + rz[...] + ahead_apply(outer_t, outer_z, vt[...], vz[...])
     out_ref[...] = total[:, : 2 * ROWS]
 
 
-def blocks_kernel(inner, outer, out_ref):
-    sources = ((inner, 0), (outer, 0), (outer, 1), (inner, 1), (inner, 2))
-    for slot, (ref, k) in enumerate(sources):
+def blocks_kernel(inner, outer_t, outer_z, out_ref):
+    sources = (inner.at[:, 0], outer_t, outer_z, inner.at[:, 1], inner.at[:, 2])
+    for slot, ref in enumerate(sources):
         for ri in range(2):
             for group in range(ROWS // 8):
                 pieces = []
                 for row in range(group * 8, group * 8 + 8):
-                    pieces.append(jnp.concatenate([ref[a, k, ri, row : row + 1, :] for a in range(8)], 0))
+                    pieces.append(jnp.concatenate([ref[a, ri, row : row + 1, :] for a in range(8)], 0))
                 wide = lane_rows(pieces)
                 first = ri * ROWS * ROWS + group * 8 * ROWS
                 out_ref[slot, :, first : first + 8 * ROWS] = wide
@@ -557,17 +557,17 @@
     )(*args)
 
 
-def blocks_call(inner, outer):
+def blocks_call(inner, outer_t, outer_z):
     vmem = pl.BlockSpec(memory_space=pltpu.VMEM)
     return pl.pallas_call(
         blocks_kernel,
         out_shape=jax.ShapeDtypeStruct((5, 8, 2 * ROWS * ROWS), F32),
-        in_specs=[vmem] * 2,
+        in_specs=[vmem] * 3,
         out_specs=vmem,
         compiler_params=pltpu.CompilerParams(vmem_limit_bytes=12 * 1024 * 1024),
         cost_estimate=pl.CostEstimate(flops=0, bytes_accessed=6_000_000, transcendentals=0),
         name="blocks",
-    )(inner, outer)
+    )(inner, outer_t, outer_z)
 
 
 def shifted(value, axis, steps):
@@ -581,15 +581,16 @@
     face_t, face_z, vec = face_call(vectors, coarse_in.reshape(8, 2 * ROWS))
     face_t, face_z = shifted(face_t, "ta", -1), shifted(face_z, "sa", -1)
     inner, left_t, left_z, link_t, link_z = inner_call(vectors, links)
-    outer, bt, bz = outer_call(face_t, face_z, left_t, left_z, link_t, link_z, vec)
+    outer_t, bt = outer_call(0, "outer_t", face_t, left_t, link_t, vec)
+    outer_z, bz = outer_call(1, "outer_z", face_z, left_z, link_z, vec)
     rt, rz = shifted(bt, "ta", 1), shifted(bz, "sa", 1)
-    (part,) = small_call(first_kernel, 1, "first", inner, outer, vec, face_t, face_z)
-    once, bt, bz = small_call(back_kernel, 3, "back", outer, part, rt, rz)
+    (part,) = small_call(first_kernel, 1, "first", inner, outer_t, outer_z, vec, face_t, face_z)
+    once, bt, bz = small_call(back_kernel, 3, "back", outer_t, outer_z, part, rt, rz)
     vec_t, rt = shifted(once, "ta", -1), shifted(bt, "ta", 1)
     vec_z, rz = shifted(once, "sa", -1), shifted(bz, "sa", 1)
     (part,) = small_call(local_apply, 1, "local", inner, once)
-    blocks = blocks_call(inner, outer)
-    (twice,) = small_call(last_kernel, 1, "last", outer, part, rt, rz, vec_t, vec_z, width=2 * ROWS)
+    blocks = blocks_call(inner, outer_t, outer_z)
+    (twice,) = small_call(last_kernel, 1, "last", outer_t, outer_z, part, rt, rz, vec_t, vec_z, width=2 * ROWS)
     blocks = jnp.swapaxes(blocks, 0, 1)
     return blocks.reshape(1, 1, 8, 5, 2 * ROWS * ROWS), twice.reshape(1, 1, 8, 2 * ROWS)
 

time: 60.4 us -> 60 us (level)
    pallas_call x1, Pallas kernels: 22.3 us -> 21.5 us  [inner_call(): pl.pallas_call(inner_kernel, out_shape=(shape((8, 3, 2, ROWS, 128), F32),...]
    pallas_call x1 -> x2, Pallas kernels: 3.23 us -> 3.56 us  [outer_call(): pl.pallas_call(functools.partial(outer_kernel, mu), out_shape=(shape((8,...]
  transfers between devices with their start and end apart: 8 -> 8, of which waited for: 2 -> 2; matrix products, arithmetic and copies ran while one was open for 0% -> 0% of each run, Pallas kernels for 45% -> 50%
where the time goes in v5:
time: 60 us; the launch traced here: 59.9 us
  Pallas kernels  35.1 us (58%)
  starting transfers between devices  18.8 us (31%)
  waiting for transfers between devices  5.25 us (9%)
  between operations  0.75 us (1%)
    pallas_call x1, Pallas kernels, inner_call(): pl.pallas_call(inner_kernel, out_shape=(shape((8, 3, 2, ROWS, 128), F32),...  21.5 us
    ppermute x8, starting transfers between devices, shifted(): lax.ppermute(value, axis, [(k, (k + steps) % count) for k in range(count)])  18.8 us
    ppermute x8, waiting for transfers between devices, shifted(): lax.ppermute(value, axis, [(k, (k + steps) % count) for k in range(count)])  5.25 us
    pallas_call x4, Pallas kernels, small_call(): pl.pallas_call(kernel, out_shape=(row,) * count, in_specs=[vmem] * len(ar...  4.51 us
    pallas_call x1, Pallas kernels, face_call(): pl.pallas_call(face_kernel, out_shape=(face, face, jax.ShapeDtypeStruct((...  3.64 us
    pallas_call x2, Pallas kernels, outer_call(): pl.pallas_call(functools.partial(outer_kernel, mu), out_shape=(shape((8,...  3.56 us
    pallas_call x1, Pallas kernels, blocks_call(): pl.pallas_call(blocks_kernel, out_shape=jax.ShapeDtypeStruct((5, 8, 2 * R...  1.95 us
  transfers between devices with their start and end apart: 8, of which 2 were waited for; matrix products, arithmetic and copies ran while one was open for 0% of the time, Pallas kernels for 50%

profile of v5, /device:TPU:0, one launch (start us, length us, event | category | flops | bytes accessed | tf_op | source)
XLA Modules:
  0.0 59.9 jit_solution(7854928521177176330)
XLA Ops:
  0.6 0.0 copy-start
  0.6 3.6 %faces.1 = (bf16[784,384]{1,0:T(8,128)(2,1)S(1)}, bf16[784,384]{1,0:T(8,128)(2,1)S(1)}, f32[8,128]{1,0:T(8,128)S(1)}) custom-call(bf16[2,24,4,3,16,128]{5,4,3,2,1,0:T(8,128)(2,1)} %bitcast.7, f32[8,96]{1,0:T(8,128)} %bitcast.10), custom_call_target="tpu_custom_call" | custom-call | tf_op jit(solution)/shard_map/faces/pallas_call | solution.py:351
  4.3 3.4 %collective-permute-start = (bf16[784,384]{1,0:T(8,128)(2,1)S(1)}, bf16[784,384]{1,0:T(8,128)(2,1)S(1)}, u32[]{:S(2)}, u32[]{:S(2)}) collective-permute-start(bf16[784,384]{1,0:T(8,128)(2,1)S(1)} %get-tuple-element.18), channel_id=1, source_target_pairs={{0,120},{8,0},{16,8},{24,16},{32,24},{40,32},{48,40},{56,48},{64,5... | collective-permute-start | bytes 1806344 | tf_op jit(solution)/shard_map/ppermute | solution.py:575
  7.7 6.4 %collective-permute-start.1 = (bf16[784,384]{1,0:T(8,128)(2,1)S(1)}, bf16[784,384]{1,0:T(8,128)(2,1)S(1)}, u32[]{:S(2)}, u32[]{:S(2)}) collective-permute-start(bf16[784,384]{1,0:T(8,128)(2,1)S(1)} %get-tuple-element.23), channel_id=1, source_target_pairs={{0,7},{1,0},{2,1},{3,2},{4,3},{5,4},{6,5},{7,6},{8,15},{9,8},{10,9... | collective-permute-start | bytes 1806344 | tf_op jit(solution)/shard_map/ppermute | solution.py:575
  14.0 0.0 copy-done
  14.0 21.5 %inner.1 = (f32[8,3,2,48,128]{4,3,2,1,0:T(8,128)S(1)}, bf16[8,2,48,384]{3,2,1,0:T(8,128)(2,1)S(1)}, bf16[2,8,2,48,384]{4,3,2,1,0:T(8,128)(2,1)S(1)}, f32[8,24,128]{2,1,0:T(8,128)S(1)}, f32[8,24,128]{2,1,0:T(8,128)S(1)}) custom-call(bf16[2,24,4,3,16,128]{5,4,3,2,1,0:T(8,128)(2,1)S(1)} %bitcast.8, bf16[2,4,3,3,16,128]{5,4,3,2,1,0:T(8,128)(2,1)} %bitcast.12), custom_call_target="tpu_custom_call" | custom-call | flops 40000000000 | bytes 6000000 | tf_op jit(solution)/shard_map/inner/pallas_call | solution.py:273
  35.5 0.0 collective-permute-done.face.ft
  35.5 1.6 %outer_t.1 = (f32[8,2,48,128]{3,2,1,0:T(8,128)S(1)}, f32[8,128]{1,0:T(8,128)S(1)}) custom-call(bf16[784,384]{1,0:T(8,128)(2,1)S(1)} %collective-permute-done.face.ft, bf16[8,2,48,384]{3,2,1,0:T(8,128)(2,1)S(1)} %get-tuple-element.19.refs_0_, f32[8,24,128]{2,1,0:T(8,128)S(1)} %get-tuple-element.20.refs_1_, f32[8,128]{1,0:T(8,128)S(1)} %get-tuple-element.21.refs_2_.vec), custom_call_target="tpu_custom_call" | custom-call | tf_op jit(solution)/shard_map/outer_t/pallas_call | solution.py:409
  37.1 0.0 collective-permute-start.2
  37.2 0.0 collective-permute-done.1.face.fz
  37.2 1.9 %outer_z.1 = (f32[8,2,48,128]{3,2,1,0:T(8,128)S(1)}, f32[8,128]{1,0:T(8,128)S(1)}) custom-call(bf16[784,384]{1,0:T(8,128)(2,1)S(1)} %collective-permute-done.1.face.fz, bf16[2,8,2,48,384]{4,3,2,1,0:T(8,128)(2,1)S(1)} %get-tuple-element.24.refs_0_, f32[8,24,128]{2,1,0:T(8,128)S(1)} %get-tuple-element.25.refs_1_, f32[8,128]{1,0:T(8,128)S(1)} %get-tuple-element.21.refs_2_.vec), custom_call_target="tpu_custom_call" | custom-call | tf_op jit(solution)/shard_map/outer_z/pallas_call | solution.py:409
  39.1 0.0 collective-permute-start.3
  39.1 2.0 %first.1.part = f32[8,128]{1,0:T(8,128)S(1)} custom-call(f32[8,3,2,48,128]{4,3,2,1,0:T(8,128)S(1)} %get-tuple-element.17.inner, f32[8,2,48,128]{3,2,1,0:T(8,128)S(1)} %get-tuple-element.22.outer_t, f32[8,2,48,128]{3,2,1,0:T(8,128)S(1)} %get-tuple-element.26.outer_z, f32[8,128]{1,0:T(8,128)S(1)} %get-tuple-element.21.refs_2_.vec, ...), custom_call_target="tpu_custom_call" | custom-call | tf_op jit(solution)/shard_map/first/pallas_call | solution.py:550
  41.1 1.2 %collective-permute-done.2.rt = f32[8,128]{1,0:T(8,128)S(1)} collective-permute-done((f32[8,128]{1,0:T(8,128)S(1)}, f32[8,128]{1,0:T(8,128)S(1)}, u32[]{:S(2)}, u32[]{:S(2)}) %collective-permute-start.2) | collective-permute-done | bytes 4128 | tf_op jit(solution)/shard_map/ppermute | solution.py:575
  42.3 4.1 %collective-permute-done.3.rz = f32[8,128]{1,0:T(8,128)S(1)} collective-permute-done((f32[8,128]{1,0:T(8,128)S(1)}, f32[8,128]{1,0:T(8,128)S(1)}, u32[]{:S(2)}, u32[]{:S(2)}) %collective-permute-start.3) | collective-permute-done | bytes 4128 | tf_op jit(solution)/shard_map/ppermute | solution.py:575
  46.3 0.6 back.1
  46.9 0.1 collective-permute-start.4
  47.0 0.1 collective-permute-start.5
  47.1 5.6 %collective-permute-start.7 = (f32[8,128]{1,0:T(8,128)S(1)}, f32[8,128]{1,0:T(8,128)S(1)}, u32[]{:S(2)}, u32[]{:S(2)}) collective-permute-start(f32[8,128]{1,0:T(8,128)S(1)} %get-tuple-element.29.vec), channel_id=1, source_target_pairs={{0,7},{1,0},{2,1},{3,2},{4,3},{5,4},{6,5},{7,6},{8,15},{9,8},{10,9... | collective-permute-start | bytes 12296 | tf_op jit(solution)/shard_map/ppermute | solution.py:575
  52.7 3.2 %collective-permute-start.6 = (f32[8,128]{1,0:T(8,128)S(1)}, f32[8,128]{1,0:T(8,128)S(1)}, u32[]{:S(2)}, u32[]{:S(2)}) collective-permute-start(f32[8,128]{1,0:T(8,128)S(1)} %get-tuple-element.29.vec), channel_id=1, source_target_pairs={{0,120},{8,0},{16,8},{24,16},{32,24},{40,32},{48,40},{56,48},{64,5... | collective-permute-start | bytes 12296 | tf_op jit(solution)/shard_map/ppermute | solution.py:575
  55.9 1.9 %blocks.1 = f32[5,8,4608]{2,1,0:T(8,128)} custom-call(f32[8,3,2,48,128]{4,3,2,1,0:T(8,128)S(1)} %get-tuple-element.17.inner, f32[8,2,48,128]{3,2,1,0:T(8,128)S(1)} %get-tuple-element.22.outer_t, f32[8,2,48,128]{3,2,1,0:T(8,128)S(1)} %get-tuple-element.26.outer_z), custom_call_target="tpu_custom_call" | custom-call | bytes 6000000 | tf_op jit(solution)/shard_map/blocks/pallas_call | solution.py:562
  57.9 0.9 %local.1.part = f32[8,128]{1,0:T(8,128)S(1)} custom-call(f32[8,3,2,48,128]{4,3,2,1,0:T(8,128)S(1)} %get-tuple-element.17.inner, f32[8,128]{1,0:T(8,128)S(1)} %get-tuple-element.29.vec), custom_call_target="tpu_custom_call" | custom-call | tf_op jit(solution)/shard_map/local/pallas_call | solution.py:550
  58.8 0.0 collective-permute-done.4.rt
  58.8 0.0 collective-permute-done.5.rz
  58.8 0.0 collective-permute-done.7.vz
  58.8 0.0 collective-permute-done.6.vt
  58.8 1.1 %last.1 = f32[8,96]{1,0:T(8,128)} custom-call(f32[8,2,48,128]{3,2,1,0:T(8,128)S(1)} %get-tuple-element.22.outer_t, f32[8,2,48,128]{3,2,1,0:T(8,128)S(1)} %get-tuple-element.26.outer_z, f32[8,128]{1,0:T(8,128)S(1)} %local.1.part, f32[8,128]{1,0:T(8,128)S(1)} %collective-permute-done.4.rt, f32[8,128]{1,0:T(8,128)S(1)} %collective-permute-done.5.rz, ...), custom_call_target="tpu_custom_call" | custom-call | tf_op jit(solution)/shard_map/last/pallas_call | solution.py:550
Async XLA Ops:
  0.6 13.4 %copy-start = (bf16[2,24,4,3,4,4,128]{6,5,4,3,2,1,0:T(4,128)(2,1)S(1)}, bf16[2,24,4,3,4,4,128]{6,5,4,3,2,1,0:T(4,128)(2,1)}, u32[]{:S(2)}) copy-start(bf16[2,24,4,3,4,4,128]{6,5,4,3,2,1,0:T(4,128)(2,1)} %param.3) | copy-start | bytes 7077892
  4.3 31.2 %collective-permute-start = (bf16[784,384]{1,0:T(8,128)(2,1)S(1)}, bf16[784,384]{1,0:T(8,128)(2,1)S(1)}, u32[]{:S(2)}, u32[]{:S(2)}) collective-permute-start(bf16[784,384]{1,0:T(8,128)(2,1)S(1)} %get-tuple-element.18), channel_id=1, source_target_pairs={{0,120},{8,0},{16,8},{24,16},{32,24},{40,32},{48,40},{56,48},{64,5... | collective-permute-start | bytes 1806344 | tf_op jit(solution)/shard_map/ppermute | solution.py:575
  7.7 29.5 %collective-permute-start.1 = (bf16[784,384]{1,0:T(8,128)(2,1)S(1)}, bf16[784,384]{1,0:T(8,128)(2,1)S(1)}, u32[]{:S(2)}, u32[]{:S(2)}) collective-permute-start(bf16[784,384]{1,0:T(8,128)(2,1)S(1)} %get-tuple-element.23), channel_id=1, source_target_pairs={{0,7},{1,0},{2,1},{3,2},{4,3},{5,4},{6,5},{7,6},{8,15},{9,8},{10,9... | collective-permute-start | bytes 1806344 | tf_op jit(solution)/shard_map/ppermute | solution.py:575
  37.1 5.1 %collective-permute-start.2 = (f32[8,128]{1,0:T(8,128)S(1)}, f32[8,128]{1,0:T(8,128)S(1)}, u32[]{:S(2)}, u32[]{:S(2)}) collective-permute-start(f32[8,128]{1,0:T(8,128)S(1)} %get-tuple-element.27), channel_id=1, source_target_pairs={{0,8},{8,16},{16,24},{24,32},{32,40},{40,48},{48,56},{56,64},{64,7... | collective-permute-start | bytes 12296 | tf_op jit(solution)/shard_map/ppermute | solution.py:575
  39.1 7.2 %collective-permute-start.3 = (f32[8,128]{1,0:T(8,128)S(1)}, f32[8,128]{1,0:T(8,128)S(1)}, u32[]{:S(2)}, u32[]{:S(2)}) collective-permute-start(f32[8,128]{1,0:T(8,128)S(1)} %get-tuple-element.28), channel_id=1, source_target_pairs={{0,1},{1,2},{2,3},{3,4},{4,5},{5,6},{6,7},{7,0},{8,9},{9,10},{10,1... | collective-permute-start | bytes 12296 | tf_op jit(solution)/shard_map/ppermute | solution.py:575
  46.9 11.8 %collective-permute-start.4 = (f32[8,128]{1,0:T(8,128)S(1)}, f32[8,128]{1,0:T(8,128)S(1)}, u32[]{:S(2)}, u32[]{:S(2)}) collective-permute-start(f32[8,128]{1,0:T(8,128)S(1)} %get-tuple-element.30), channel_id=1, source_target_pairs={{0,8},{8,16},{16,24},{24,32},{32,40},{40,48},{48,56},{56,64},{64,7... | collective-permute-start | bytes 12296 | tf_op jit(solution)/shard_map/ppermute | solution.py:575
  47.0 11.8 %collective-permute-start.5 = (f32[8,128]{1,0:T(8,128)S(1)}, f32[8,128]{1,0:T(8,128)S(1)}, u32[]{:S(2)}, u32[]{:S(2)}) collective-permute-start(f32[8,128]{1,0:T(8,128)S(1)} %get-tuple-element.31), channel_id=1, source_target_pairs={{0,1},{1,2},{2,3},{3,4},{4,5},{5,6},{6,7},{7,0},{8,9},{9,10},{10,1... | collective-permute-start | bytes 12296 | tf_op jit(solution)/shard_map/ppermute | solution.py:575
  47.1 11.7 %collective-permute-start.7 = (f32[8,128]{1,0:T(8,128)S(1)}, f32[8,128]{1,0:T(8,128)S(1)}, u32[]{:S(2)}, u32[]{:S(2)}) collective-permute-start(f32[8,128]{1,0:T(8,128)S(1)} %get-tuple-element.29.vec), channel_id=1, source_target_pairs={{0,7},{1,0},{2,1},{3,2},{4,3},{5,4},{6,5},{7,6},{8,15},{9,8},{10,9... | collective-permute-start | bytes 12296 | tf_op jit(solution)/shard_map/ppermute | solution.py:575
  52.7 6.1 %collective-permute-start.6 = (f32[8,128]{1,0:T(8,128)S(1)}, f32[8,128]{1,0:T(8,128)S(1)}, u32[]{:S(2)}, u32[]{:S(2)}) collective-permute-start(f32[8,128]{1,0:T(8,128)S(1)} %get-tuple-element.29.vec), channel_id=1, source_target_pairs={{0,120},{8,0},{16,8},{24,16},{32,24},{40,32},{48,40},{56,48},{64,5... | collective-permute-start | bytes 12296 | tf_op jit(solution)/shard_map/ppermute | solution.py:575

commit v6 on v5

--- a/solution.py
+++ b/solution.py
@@ -25,6 +25,20 @@
     step = 4 << bit
     chosen = (lane_ids(low.shape[0]) & step) != 0
     return jnp.where(chosen, roll(high, step), low), jnp.where(chosen, high, roll(low, -step))
+
+
+def exchange_twice(sets):
+    for bit in range(2):
+        for planes in sets:
+            for low in range(4):
+                if not low >> bit & 1:
+                    high = low | 1 << bit
+                    planes[low], planes[high] = exchange_bit(planes[low], planes[high], bit)
+    out = []
+    for planes in sets:
+        pairs = [exchange_bit(plane, plane, 2) for plane in planes]
+        out.append([pair[0] for pair in pairs] + [pair[1] for pair in pairs])
+    return out
 
 
 def exchange(sets):
@@ -56,7 +70,7 @@
 
 
 def inner_kernel(
-    v_ref, u_hbm, out_ref, lt_ref, lz_ref, ut_ref, uz_ref, vm, uf, cm, flat, kept, u_ref, sem
+    v_ref, u_hbm, own_ref, out_ref, lt_ref, lz_ref, ut_ref, uz_ref, vm, uf, cm, flat, kept, u_ref, sem
 ):
     fetch = pltpu.make_async_copy(u_hbm, u_ref, sem)
     fetch.start()
@@ -75,14 +89,19 @@
             return flat[sb, pl.ds(first, ROWS, stride=16), :].astype(BF16)
 
         second = (lane_ids(ROWS) & 16) != 0
-        for group in ((0, 1), (2, 3), (4,)):
-            done = exchange([[load(t, plane) for plane in range(8)] for t in group])
+        for group in ((0,), (1, 2), (3, 4)):
+            if group == (0,):
+                rows = [pl.ds(pl.multiple_of((a * 2 + chi) * ROWS, ROWS), ROWS) for a in range(8)]
+                column = pl.ds(pl.multiple_of(c * 128, 128), 128)
+                done = [[own_ref[part, column] for part in rows]]
+            else:
+                done = exchange([[load(t, plane) for plane in range(8)] for t in group])
             turned = [[jnp.where(second, -value, value) for value in values] for values in done]
-            if group != (4,):
-                swapped = [
-                    [jnp.where(second, roll(value, 16), roll(value, -16)) for value in values]
-                    for values in done
-                ]
+            swapped = [
+                [jnp.where(second, roll(value, 16), roll(value, -16)) for value in values]
+                for t, values in zip(group, done)
+                if t < 4
+            ]
             for k, t in enumerate(group):
                 for a in range(8):
                     if t == 4:
@@ -114,19 +133,18 @@
                     flat[0, pl.ds(row, 16), :] = 0.5 * u_ref[ri, mu, c, d].astype(F32)
 
         drop = ((lane_ids(24) & 12) == 12) & (mu == 1)
-
-        def load(t, plane):
-            first = plane % 4 * 4 + 3 if t == 4 else t * 4 + plane % 4
-            return flat[0, pl.ds(first, 24, stride=16), :]
-
-        for group in ((0, 1), (2, 3), (4,)):
-            done = exchange([[load(t, plane) for plane in range(8)] for t in group])
+        sets = [[flat[0, pl.ds(t * 4 + z, 24, stride=16), :] for z in range(4)] for t in range(4)]
+        for group in ((0, 1), (2, 3)):
+            done = exchange_twice([sets[t] for t in group])
             for t, values in zip(group, done):
                 for a, value in enumerate(values):
-                    uf[a, mu, t] = value if t == 4 else jnp.where(drop, 0.0, value)
-
-    for a in range(8):
-        uz_ref[a] = uf[a, 1, 4]
+                    uf[a, mu, t] = jnp.where(drop, 0.0, value)
+
+        @pl.when(mu == 1)
+        def _():
+            last = [flat[0, pl.ds(t * 4 + 3, 24, stride=16), :] for t in range(4)]
+            for a, value in enumerate(exchange_twice([last])[0]):
+                uz_ref[a] = value
 
     for a in range(8):
         ut_ref[a] = uf[a, 0, 3]
@@ -267,7 +285,7 @@
     return jnp.concatenate(rows, 0)
 
 
-def inner_call(vectors, links):
+def inner_call(vectors, links, own):
     shape = jax.ShapeDtypeStruct
     vmem = pl.BlockSpec(memory_space=pltpu.VMEM)
     return pl.pallas_call(
@@ -279,11 +297,11 @@
             shape((8, 24, 128), F32),
             shape((8, 24, 128), F32),
         ),
-        in_specs=[vmem, pl.BlockSpec(memory_space=pltpu.HBM)],
+        in_specs=[vmem, pl.BlockSpec(memory_space=pltpu.HBM), vmem],
         out_specs=(vmem,) * 5,
         scratch_shapes=[
             pltpu.VMEM((4, 8, 2, ROWS, 1536), BF16),
-            pltpu.VMEM((8, 4, 5, 24, 128), F32),
+            pltpu.VMEM((8, 4, 4, 24, 128), F32),
             pltpu.VMEM((2, 3, 96, 1536), BF16),
             pltpu.VMEM((2, 768, 128), F32),
             pltpu.VMEM((384, 128), F32),
@@ -295,7 +313,7 @@
             flops=40_000_000_000, bytes_accessed=6_000_000, transcendentals=0
         ),
         name="inner",
-    )(vectors, pltpu.with_memory_space_constraint(links, pltpu.HBM))
+    )(vectors, pltpu.with_memory_space_constraint(links, pltpu.HBM), own)
 
 
 def face_kernel(v_hbm, phi_hbm, t_ref, z_ref, vec_ref, flat, v_ref, phi_ref, sem):
@@ -579,8 +597,9 @@
     vectors = null_vectors.reshape(2, NV, 4, 3, 16, 128)
     links = gauge_links.reshape(2, 4, 3, 3, 16, 128)
     face_t, face_z, vec = face_call(vectors, coarse_in.reshape(8, 2 * ROWS))
+    own_t = face_t
     face_t, face_z = shifted(face_t, "ta", -1), shifted(face_z, "sa", -1)
-    inner, left_t, left_z, link_t, link_z = inner_call(vectors, links)
+    inner, left_t, left_z, link_t, link_z = inner_call(vectors, links, own_t)
     outer_t, bt = outer_call(0, "outer_t", face_t, left_t, link_t, vec)
     outer_z, bz = outer_call(1, "outer_z", face_z, left_z, link_z, vec)
     rt, rz = shifted(bt, "ta", 1), shifted(bz, "sa", 1)

time: 60 us -> 57.9 us (0.965)
  Pallas kernels: 35.1 us -> 33.9 us
  starting transfers between devices: 18.8 us -> 17.9 us
    pallas_call x1, Pallas kernels: 21.5 us -> 20.3 us  [inner_call(): pl.pallas_call(inner_kernel, out_shape=(shape((8, 3, 2, ROWS, 128), F32),...]
    ppermute x8, starting transfers between devices: 18.8 us -> 17.9 us  [shifted(): lax.ppermute(value, axis, [(k, (k + steps) % count) for k in range(count)])]
where the time goes in v6:
time: 57.9 us; the launch traced here: 57.8 us
  Pallas kernels  33.9 us (59%)
  starting transfers between devices  17.9 us (31%)
  waiting for transfers between devices  5.24 us (9%)
  between operations  0.75 us (1%)
    pallas_call x1, Pallas kernels, inner_call(): pl.pallas_call(inner_kernel, out_shape=(shape((8, 3, 2, ROWS, 128), F32),...  20.3 us
    ppermute x8, starting transfers between devices, shifted(): lax.ppermute(value, axis, [(k, (k + steps) % count) for k in range(count)])  17.9 us
    ppermute x8, waiting for transfers between devices, shifted(): lax.ppermute(value, axis, [(k, (k + steps) % count) for k in range(count)])  5.24 us
    pallas_call x4, Pallas kernels, small_call(): pl.pallas_call(kernel, out_shape=(row,) * count, in_specs=[vmem] * len(ar...  4.52 us
    pallas_call x1, Pallas kernels, face_call(): pl.pallas_call(face_kernel, out_shape=(face, face, jax.ShapeDtypeStruct((...  3.64 us
    pallas_call x2, Pallas kernels, outer_call(): pl.pallas_call(functools.partial(outer_kernel, mu), out_shape=(shape((8,...  3.56 us
    pallas_call x1, Pallas kernels, blocks_call(): pl.pallas_call(blocks_kernel, out_shape=jax.ShapeDtypeStruct((5, 8, 2 * R...  1.95 us
  transfers between devices with their start and end apart: 8, of which 2 were waited for; matrix products, arithmetic and copies ran while one was open for 0% of the time, Pallas kernels for 50%

profile of v6, /device:TPU:0, one launch (start us, length us, event | category | flops | bytes accessed | tf_op | source)
XLA Modules:
  0.0 57.8 jit_solution(743499943746188430)
XLA Ops:
  0.6 0.0 copy-start
  0.6 3.6 %faces.1 = (bf16[784,384]{1,0:T(8,128)(2,1)S(1)}, bf16[784,384]{1,0:T(8,128)(2,1)S(1)}, f32[8,128]{1,0:T(8,128)S(1)}) custom-call(bf16[2,24,4,3,16,128]{5,4,3,2,1,0:T(8,128)(2,1)} %bitcast.7, f32[8,96]{1,0:T(8,128)} %bitcast.10), custom_call_target="tpu_custom_call" | custom-call | tf_op jit(solution)/shard_map/faces/pallas_call | solution.py:369
  4.3 6.8 %collective-permute-start.1 = (bf16[784,384]{1,0:T(8,128)(2,1)S(1)}, bf16[784,384]{1,0:T(8,128)(2,1)S(1)}, u32[]{:S(2)}, u32[]{:S(2)}) collective-permute-start(bf16[784,384]{1,0:T(8,128)(2,1)S(1)} %get-tuple-element.23), channel_id=1, source_target_pairs={{0,7},{1,0},{2,1},{3,2},{4,3},{5,4},{6,5},{7,6},{8,15},{9,8},{10,9... | collective-permute-start | bytes 1806344 | tf_op jit(solution)/shard_map/ppermute | solution.py:593
  11.1 2.0 %collective-permute-start = (bf16[784,384]{1,0:T(8,128)(2,1)S(1)}, bf16[784,384]{1,0:T(8,128)(2,1)S(1)}, u32[]{:S(2)}, u32[]{:S(2)}) collective-permute-start(bf16[784,384]{1,0:T(8,128)(2,1)S(1)} %get-tuple-element.17.own_ref), channel_id=1, source_target_pairs={{0,120},{8,0},{16,8},{24,16},{32,24},{40,32},{48,40},{56,48},{64,5... | collective-permute-start | bytes 1806344 | tf_op jit(solution)/shard_map/ppermute | solution.py:593
  13.1 0.0 copy-done
  13.1 20.3 %inner.1 = (f32[8,3,2,48,128]{4,3,2,1,0:T(8,128)S(1)}, bf16[8,2,48,384]{3,2,1,0:T(8,128)(2,1)S(1)}, bf16[2,8,2,48,384]{4,3,2,1,0:T(8,128)(2,1)S(1)}, f32[8,24,128]{2,1,0:T(8,128)S(1)}, f32[8,24,128]{2,1,0:T(8,128)S(1)}) custom-call(bf16[2,24,4,3,16,128]{5,4,3,2,1,0:T(8,128)(2,1)S(1)} %bitcast.8, bf16[2,4,3,3,16,128]{5,4,3,2,1,0:T(8,128)(2,1)} %bitcast.12, ...), custom_call_target="tpu_custom_call" | custom-call | flops 40000000000 | bytes 6000000 | tf_op jit(solution)/shard_map/inner/pallas_call | solution.py:291
  33.4 0.0 collective-permute-done.face.ft
  33.4 1.6 %outer_t.1 = (f32[8,2,48,128]{3,2,1,0:T(8,128)S(1)}, f32[8,128]{1,0:T(8,128)S(1)}) custom-call(bf16[784,384]{1,0:T(8,128)(2,1)S(1)} %collective-permute-done.face.ft, bf16[8,2,48,384]{3,2,1,0:T(8,128)(2,1)S(1)} %get-tuple-element.19.refs_0_, f32[8,24,128]{2,1,0:T(8,128)S(1)} %get-tuple-element.20.refs_1_, f32[8,128]{1,0:T(8,128)S(1)} %get-tuple-element.21.refs_2_.vec), custom_call_target="tpu_custom_call" | custom-call | tf_op jit(solution)/shard_map/outer_t/pallas_call | solution.py:427
  35.0 0.0 collective-permute-start.2
  35.1 0.0 collective-permute-done.1.face.fz
  35.1 1.9 %outer_z.1 = (f32[8,2,48,128]{3,2,1,0:T(8,128)S(1)}, f32[8,128]{1,0:T(8,128)S(1)}) custom-call(bf16[784,384]{1,0:T(8,128)(2,1)S(1)} %collective-permute-done.1.face.fz, bf16[2,8,2,48,384]{4,3,2,1,0:T(8,128)(2,1)S(1)} %get-tuple-element.24.refs_0_, f32[8,24,128]{2,1,0:T(8,128)S(1)} %get-tuple-element.25.refs_1_, f32[8,128]{1,0:T(8,128)S(1)} %get-tuple-element.21.refs_2_.vec), custom_call_target="tpu_custom_call" | custom-call | tf_op jit(solution)/shard_map/outer_z/pallas_call | solution.py:427
  37.0 0.0 collective-permute-start.3
  37.0 2.0 %first.1.part = f32[8,128]{1,0:T(8,128)S(1)} custom-call(f32[8,3,2,48,128]{4,3,2,1,0:T(8,128)S(1)} %get-tuple-element.18.inner, f32[8,2,48,128]{3,2,1,0:T(8,128)S(1)} %get-tuple-element.22.outer_t, f32[8,2,48,128]{3,2,1,0:T(8,128)S(1)} %get-tuple-element.26.outer_z, f32[8,128]{1,0:T(8,128)S(1)} %get-tuple-element.21.refs_2_.vec, ...), custom_call_target="tpu_custom_call" | custom-call | tf_op jit(solution)/shard_map/first/pallas_call | solution.py:568
  39.0 1.2 %collective-permute-done.2.rt = f32[8,128]{1,0:T(8,128)S(1)} collective-permute-done((f32[8,128]{1,0:T(8,128)S(1)}, f32[8,128]{1,0:T(8,128)S(1)}, u32[]{:S(2)}, u32[]{:S(2)}) %collective-permute-start.2) | collective-permute-done | bytes 4128 | tf_op jit(solution)/shard_map/ppermute | solution.py:593
  40.2 4.1 %collective-permute-done.3.rz = f32[8,128]{1,0:T(8,128)S(1)} collective-permute-done((f32[8,128]{1,0:T(8,128)S(1)}, f32[8,128]{1,0:T(8,128)S(1)}, u32[]{:S(2)}, u32[]{:S(2)}) %collective-permute-start.3) | collective-permute-done | bytes 4128 | tf_op jit(solution)/shard_map/ppermute | solution.py:593
  44.2 0.6 back.1
  44.8 0.1 collective-permute-start.4
  44.9 0.1 collective-permute-start.5
  45.0 5.6 %collective-permute-start.7 = (f32[8,128]{1,0:T(8,128)S(1)}, f32[8,128]{1,0:T(8,128)S(1)}, u32[]{:S(2)}, u32[]{:S(2)}) collective-permute-start(f32[8,128]{1,0:T(8,128)S(1)} %get-tuple-element.29.vec), channel_id=1, source_target_pairs={{0,7},{1,0},{2,1},{3,2},{4,3},{5,4},{6,5},{7,6},{8,15},{9,8},{10,9... | collective-permute-start | bytes 12296 | tf_op jit(solution)/shard_map/ppermute | solution.py:593
  50.6 3.2 %collective-permute-start.6 = (f32[8,128]{1,0:T(8,128)S(1)}, f32[8,128]{1,0:T(8,128)S(1)}, u32[]{:S(2)}, u32[]{:S(2)}) collective-permute-start(f32[8,128]{1,0:T(8,128)S(1)} %get-tuple-element.29.vec), channel_id=1, source_target_pairs={{0,120},{8,0},{16,8},{24,16},{32,24},{40,32},{48,40},{56,48},{64,5... | collective-permute-start | bytes 12296 | tf_op jit(solution)/shard_map/ppermute | solution.py:593
  53.8 1.9 %blocks.1 = f32[5,8,4608]{2,1,0:T(8,128)} custom-call(f32[8,3,2,48,128]{4,3,2,1,0:T(8,128)S(1)} %get-tuple-element.18.inner, f32[8,2,48,128]{3,2,1,0:T(8,128)S(1)} %get-tuple-element.22.outer_t, f32[8,2,48,128]{3,2,1,0:T(8,128)S(1)} %get-tuple-element.26.outer_z), custom_call_target="tpu_custom_call" | custom-call | bytes 6000000 | tf_op jit(solution)/shard_map/blocks/pallas_call | solution.py:580
  55.8 0.9 %local.1.part = f32[8,128]{1,0:T(8,128)S(1)} custom-call(f32[8,3,2,48,128]{4,3,2,1,0:T(8,128)S(1)} %get-tuple-element.18.inner, f32[8,128]{1,0:T(8,128)S(1)} %get-tuple-element.29.vec), custom_call_target="tpu_custom_call" | custom-call | tf_op jit(solution)/shard_map/local/pallas_call | solution.py:568
  56.7 0.0 collective-permute-done.4.rt
  56.7 0.0 collective-permute-done.5.rz
  56.7 0.0 collective-permute-done.7.vz
  56.7 0.0 collective-permute-done.6.vt
  56.7 1.1 %last.1 = f32[8,96]{1,0:T(8,128)} custom-call(f32[8,2,48,128]{3,2,1,0:T(8,128)S(1)} %get-tuple-element.22.outer_t, f32[8,2,48,128]{3,2,1,0:T(8,128)S(1)} %get-tuple-element.26.outer_z, f32[8,128]{1,0:T(8,128)S(1)} %local.1.part, f32[8,128]{1,0:T(8,128)S(1)} %collective-permute-done.4.rt, f32[8,128]{1,0:T(8,128)S(1)} %collective-permute-done.5.rz, ...), custom_call_target="tpu_custom_call" | custom-call | tf_op jit(solution)/shard_map/last/pallas_call | solution.py:568
Async XLA Ops:
  0.6 12.5 %copy-start = (bf16[2,24,4,3,4,4,128]{6,5,4,3,2,1,0:T(4,128)(2,1)S(1)}, bf16[2,24,4,3,4,4,128]{6,5,4,3,2,1,0:T(4,128)(2,1)}, u32[]{:S(2)}) copy-start(bf16[2,24,4,3,4,4,128]{6,5,4,3,2,1,0:T(4,128)(2,1)} %param.3) | copy-start | bytes 7077892
  4.3 30.8 %collective-permute-start.1 = (bf16[784,384]{1,0:T(8,128)(2,1)S(1)}, bf16[784,384]{1,0:T(8,128)(2,1)S(1)}, u32[]{:S(2)}, u32[]{:S(2)}) collective-permute-start(bf16[784,384]{1,0:T(8,128)(2,1)S(1)} %get-tuple-element.23), channel_id=1, source_target_pairs={{0,7},{1,0},{2,1},{3,2},{4,3},{5,4},{6,5},{7,6},{8,15},{9,8},{10,9... | collective-permute-start | bytes 1806344 | tf_op jit(solution)/shard_map/ppermute | solution.py:593
  11.1 22.3 %collective-permute-start = (bf16[784,384]{1,0:T(8,128)(2,1)S(1)}, bf16[784,384]{1,0:T(8,128)(2,1)S(1)}, u32[]{:S(2)}, u32[]{:S(2)}) collective-permute-start(bf16[784,384]{1,0:T(8,128)(2,1)S(1)} %get-tuple-element.17.own_ref), channel_id=1, source_target_pairs={{0,120},{8,0},{16,8},{24,16},{32,24},{40,32},{48,40},{56,48},{64,5... | collective-permute-start | bytes 1806344 | tf_op jit(solution)/shard_map/ppermute | solution.py:593
  35.0 5.1 %collective-permute-start.2 = (f32[8,128]{1,0:T(8,128)S(1)}, f32[8,128]{1,0:T(8,128)S(1)}, u32[]{:S(2)}, u32[]{:S(2)}) collective-permute-start(f32[8,128]{1,0:T(8,128)S(1)} %get-tuple-element.27), channel_id=1, source_target_pairs={{0,8},{8,16},{16,24},{24,32},{32,40},{40,48},{48,56},{56,64},{64,7... | collective-permute-start | bytes 12296 | tf_op jit(solution)/shard_map/ppermute | solution.py:593
  37.0 7.2 %collective-permute-start.3 = (f32[8,128]{1,0:T(8,128)S(1)}, f32[8,128]{1,0:T(8,128)S(1)}, u32[]{:S(2)}, u32[]{:S(2)}) collective-permute-start(f32[8,128]{1,0:T(8,128)S(1)} %get-tuple-element.28), channel_id=1, source_target_pairs={{0,1},{1,2},{2,3},{3,4},{4,5},{5,6},{6,7},{7,0},{8,9},{9,10},{10,1... | collective-permute-start | bytes 12296 | tf_op jit(solution)/shard_map/ppermute | solution.py:593
  44.8 11.9 %collective-permute-start.4 = (f32[8,128]{1,0:T(8,128)S(1)}, f32[8,128]{1,0:T(8,128)S(1)}, u32[]{:S(2)}, u32[]{:S(2)}) collective-permute-start(f32[8,128]{1,0:T(8,128)S(1)} %get-tuple-element.30), channel_id=1, source_target_pairs={{0,8},{8,16},{16,24},{24,32},{32,40},{40,48},{48,56},{56,64},{64,7... | collective-permute-start | bytes 12296 | tf_op jit(solution)/shard_map/ppermute | solution.py:593
  44.9 11.8 %collective-permute-start.5 = (f32[8,128]{1,0:T(8,128)S(1)}, f32[8,128]{1,0:T(8,128)S(1)}, u32[]{:S(2)}, u32[]{:S(2)}) collective-permute-start(f32[8,128]{1,0:T(8,128)S(1)} %get-tuple-element.31), channel_id=1, source_target_pairs={{0,1},{1,2},{2,3},{3,4},{4,5},{5,6},{6,7},{7,0},{8,9},{9,10},{10,1... | collective-permute-start | bytes 12296 | tf_op jit(solution)/shard_map/ppermute | solution.py:593
  45.0 11.7 %collective-permute-start.7 = (f32[8,128]{1,0:T(8,128)S(1)}, f32[8,128]{1,0:T(8,128)S(1)}, u32[]{:S(2)}, u32[]{:S(2)}) collective-permute-start(f32[8,128]{1,0:T(8,128)S(1)} %get-tuple-element.29.vec), channel_id=1, source_target_pairs={{0,7},{1,0},{2,1},{3,2},{4,3},{5,4},{6,5},{7,6},{8,15},{9,8},{10,9... | collective-permute-start | bytes 12296 | tf_op jit(solution)/shard_map/ppermute | solution.py:593
  50.6 6.1 %collective-permute-start.6 = (f32[8,128]{1,0:T(8,128)S(1)}, f32[8,128]{1,0:T(8,128)S(1)}, u32[]{:S(2)}, u32[]{:S(2)}) collective-permute-start(f32[8,128]{1,0:T(8,128)S(1)} %get-tuple-element.29.vec), channel_id=1, source_target_pairs={{0,120},{8,0},{16,8},{24,16},{32,24},{40,32},{48,40},{56,48},{64,5... | collective-permute-start | bytes 12296 | tf_op jit(solution)/shard_map/ppermute | solution.py:593

commit v7 on v6

--- a/solution.py
+++ b/solution.py
@@ -70,7 +70,7 @@
 
 
 def inner_kernel(
-    v_ref, u_hbm, own_ref, out_ref, lt_ref, lz_ref, ut_ref, uz_ref, vm, uf, cm, flat, kept, u_ref, sem
+    v_ref, u_hbm, own_ref, out_ref, lt_ref, lz_ref, ut_ref, uz_ref, vm, uf, cm, flat, sites, kept, u_ref, sem
 ):
     fetch = pltpu.make_async_copy(u_hbm, u_ref, sem)
     fetch.start()
@@ -79,14 +79,13 @@
     def _(step):
         chi, c = step // 3, step % 3
         for sb in range(2):
-            for ri in range(2):
-                block = v_ref[ri, :, 2 * chi + sb, c].astype(F32)
-                flat[sb, pl.ds(ri * 384, 384), :] = block.reshape(384, 128)
+            parts = [v_ref[ri, :, 2 * chi + sb, c] for ri in range(2)]
+            sites[sb] = jnp.swapaxes(jnp.concatenate(parts, 0), 0, 1)
 
         def load(t, plane):
             sb, q = plane // 4, plane % 4
             first = q * 4 + 3 if t == 4 else t * 4 + q
-            return flat[sb, pl.ds(first, ROWS, stride=16), :].astype(BF16)
+            return sites[sb, first]
 
         second = (lane_ids(ROWS) & 16) != 0
         for group in ((0,), (1, 2), (3, 4)):
@@ -130,10 +129,10 @@
             for d in range(3):
                 for ri in range(2):
                     row = ((c * 3 + d) * 2 + ri) * 16
-                    flat[0, pl.ds(row, 16), :] = 0.5 * u_ref[ri, mu, c, d].astype(F32)
+                    flat[pl.ds(row, 16), :] = 0.5 * u_ref[ri, mu, c, d].astype(F32)
 
         drop = ((lane_ids(24) & 12) == 12) & (mu == 1)
-        sets = [[flat[0, pl.ds(t * 4 + z, 24, stride=16), :] for z in range(4)] for t in range(4)]
+        sets = [[flat[pl.ds(t * 4 + z, 24, stride=16), :] for z in range(4)] for t in range(4)]
         for group in ((0, 1), (2, 3)):
             done = exchange_twice([sets[t] for t in group])
             for t, values in zip(group, done):
@@ -142,7 +141,7 @@
 
         @pl.when(mu == 1)
         def _():
-            last = [flat[0, pl.ds(t * 4 + 3, 24, stride=16), :] for t in range(4)]
+            last = [flat[pl.ds(t * 4 + 3, 24, stride=16), :] for t in range(4)]
             for a, value in enumerate(exchange_twice([last])[0]):
                 uz_ref[a] = value
 
@@ -151,9 +150,9 @@
 
     def fill(a, chi):
         ahead = lax.rem(a + 1, 8)
-        x_last = (lane_ids(NV) & 3) == 3
+        x_last = jnp.where((lane_ids(NV) & 3) == 3, -1.0, 0.0).astype(F32)
         x_last_pair = (lane_ids(ROWS) & 3) == 3
-        y_last = lane_ids(NV) >= 96
+        y_last = jnp.where(lane_ids(NV) >= 96, -1.0, 0.0).astype(F32)
 
         def hop(t, mu):
             link = [uf[a, mu, t, pl.ds(k, 1), :] for k in range(18)]
@@ -180,7 +179,7 @@
                 else:
                     last = y_last if slot == 1 else x_last
                     one = hop(t, slot + 1)
-                    two = [[jnp.where(last, -part, 0.0) for part in pair] for pair in one]
+                    two = [[part * last for part in pair] for pair in one]
                 for c in range(3):
                     column = slice((t * 3 + c) * 128, (t * 3 + c + 1) * 128)
                     for ri in range(2):
@@ -234,8 +233,8 @@
     return product[:NV] + sides(half) * other_side(product[NV:], half)
 
 
-def times_i(value, half):
-    return -sides(half) * other_side(value, half)
+def complex_i(product, half):
+    return product[NV:] - sides(half) * other_side(product[:NV], half)
 
 
 def combine_inner(blocks, a, out_ref):
@@ -248,40 +247,39 @@
         phase = 1.0 if chi == 0 else -1.0
         z_tz, z_y, z_x = (complex_of(value[:ROWS], 48) for value in (tz, y, x))
         cross_t = complex_of(tz[48:96], 48)
-        cross_z = phase * times_i(complex_of(tz[96:144], 48), 48)
+        cross_z = phase * complex_i(tz[96:144], 48)
         cross_y = phase * complex_of(y[48:96], 48)
-        cross_x = phase * times_i(complex_of(x[48:96], 48), 48)
-        same = -(z_tz + z_y + z_x)
+        cross_x = phase * complex_i(x[48:96], 48)
+        upper[chi, chi] = -(z_tz + z_y + z_x), z_y, z_x
         cross = jnp.where(second, cross_z, cross_t) + cross_y + cross_x
-        same = same + roll(same, -NV)
-        cross = cross + roll(cross, -NV)
-        upper[chi, chi] = same, roll(z_y, -NV), roll(z_x, -NV)
-        upper[1 - chi, chi] = cross, -roll(cross_y, -NV), -roll(cross_x, -NV)
+        upper[1 - chi, chi] = cross, -cross_y, -cross_x
         grams[chi][chi] = complex_of(gram, NV)
         grams[chi][1 - chi] = zero
 
-    def whole(item, ri):
-        return placed([[upper[row, col][item] for col in range(2)] for row in range(2)], 48 * ri)
+    def whole(item, starts):
+        return placed([[upper[row, col][item] for col in range(2)] for row in range(2)], *starts)
 
     first_rows = lax.broadcasted_iota(jnp.int32, (ROWS, 128), 0) < NV
     cols = lane_ids(ROWS)
     flip = jnp.where(first_rows == (cols < NV), 1.0, -1.0).astype(F32)
     for ri in range(2):
-        out_ref[a, 1, ri] = whole(1, ri)
-        out_ref[a, 2, ri] = whole(2, ri)
-        inner = whole(0, ri)
+        first, behind = 48 * ri, 48 * ri + NV
+        out_ref[a, 1, ri] = whole(1, (behind,))
+        out_ref[a, 2, ri] = whole(2, (behind,))
+        inner = whole(0, (first, behind))
         turned = jnp.concatenate([inner, jnp.zeros((80, 128), F32)], 0).T[:ROWS]
         turned = flip * turned if ri == 0 else -flip * turned
         out_ref[a, 0, ri] = placed(grams, NV * ri) + inner + turned
 
 
-def placed(parts, start):
+def placed(parts, *starts):
     lanes = lane_ids(NV)
     left, right = lanes < NV, (lanes >= NV) & (lanes < 2 * NV)
     rows = []
     for row in range(2):
-        second = jnp.where(right, roll(parts[row][1], NV - start), 0.0)
-        rows.append(jnp.where(left, roll(parts[row][0], -start), second))
+        ahead = sum(roll(parts[row][1], NV - start) for start in starts)
+        here = sum(roll(parts[row][0], -start) for start in starts)
+        rows.append(jnp.where(left, here, jnp.where(right, ahead, 0.0)))
     return jnp.concatenate(rows, 0)
 
 
@@ -303,7 +301,8 @@
             pltpu.VMEM((4, 8, 2, ROWS, 1536), BF16),
             pltpu.VMEM((8, 4, 4, 24, 128), F32),
             pltpu.VMEM((2, 3, 96, 1536), BF16),
-            pltpu.VMEM((2, 768, 128), F32),
+            pltpu.VMEM((384, 128), F32),
+            pltpu.VMEM((2, 16, ROWS, 128), BF16),
             pltpu.VMEM((384, 128), F32),
             pltpu.VMEM((2, 4, 3, 3, 16, 128), BF16),
             pltpu.SemaphoreType.DMA,
@@ -407,9 +406,10 @@
             else:
                 near, far = lefts[0][0, a, chi], lefts[0][1, a, 1 - chi]
             product = widened(nt(jnp.concatenate([near, far], 0), cm[a, chi]))
-            cross = complex_of(product[ROWS:], NV)
-            if mu == 1:
-                cross = (1.0 if chi == 0 else -1.0) * times_i(cross, NV)
+            if mu == 0:
+                cross = complex_of(product[ROWS:], NV)
+            else:
+                cross = (1.0 if chi == 0 else -1.0) * complex_i(product[ROWS:], NV)
             parts[chi][chi] = -complex_of(product[:ROWS], NV)
             parts[1 - chi][chi] = cross
         pr, pi = split(vec_ref[pl.ds(a, 1), :])

time: 57.9 us -> 55.5 us (0.959)
  Pallas kernels: 33.9 us -> 31.5 us
    pallas_call x1, Pallas kernels: 20.3 us -> 18.2 us  [inner_call(): pl.pallas_call(inner_kernel, out_shape=(shape((8, 3, 2, ROWS, 128), F32),...]
  transfers between devices with their start and end apart: 8 -> 8, of which waited for: 2 -> 2; matrix products, arithmetic and copies ran while one was open for 0% -> 0% of each run, Pallas kernels for 50% -> 47%
where the time goes in v7:
time: 55.5 us; the launch traced here: 55.4 us
  Pallas kernels  31.5 us (57%)
  starting transfers between devices  17.9 us (32%)
  waiting for transfers between devices  5.24 us (9%)
  between operations  0.74 us (1%)
    pallas_call x1, Pallas kernels, inner_call(): pl.pallas_call(inner_kernel, out_shape=(shape((8, 3, 2, ROWS, 128), F32),...  18.2 us
    ppermute x8, starting transfers between devices, shifted(): lax.ppermute(value, axis, [(k, (k + steps) % count) for k in range(count)])  17.9 us
    ppermute x8, waiting for transfers between devices, shifted(): lax.ppermute(value, axis, [(k, (k + steps) % count) for k in range(count)])  5.24 us
    pallas_call x4, Pallas kernels, small_call(): pl.pallas_call(kernel, out_shape=(row,) * count, in_specs=[vmem] * len(ar...  4.52 us
    pallas_call x1, Pallas kernels, face_call(): pl.pallas_call(face_kernel, out_shape=(face, face, jax.ShapeDtypeStruct((...  3.64 us
    pallas_call x2, Pallas kernels, outer_call(): pl.pallas_call(functools.partial(outer_kernel, mu), out_shape=(shape((8,...  3.26 us
    pallas_call x1, Pallas kernels, blocks_call(): pl.pallas_call(blocks_kernel, out_shape=jax.ShapeDtypeStruct((5, 8, 2 * R...  1.95 us
  transfers between devices with their start and end apart: 8, of which 2 were waited for; matrix products, arithmetic and copies ran while one was open for 0% of the time, Pallas kernels for 47%

profile of v7, /device:TPU:0, one launch (start us, length us, event | category | flops | bytes accessed | tf_op | source)
XLA Modules:
  0.0 55.4 jit_solution(14084850315073585984)
XLA Ops:
  0.6 0.0 copy-start
  0.6 3.6 %faces.1 = (bf16[784,384]{1,0:T(8,128)(2,1)S(1)}, bf16[784,384]{1,0:T(8,128)(2,1)S(1)}, f32[8,128]{1,0:T(8,128)S(1)}) custom-call(bf16[2,24,4,3,16,128]{5,4,3,2,1,0:T(8,128)(2,1)} %bitcast.7, f32[8,96]{1,0:T(8,128)} %bitcast.10), custom_call_target="tpu_custom_call" | custom-call | tf_op jit(solution)/shard_map/faces/pallas_call | solution.py:368
  4.3 6.8 %collective-permute-start.1 = (bf16[784,384]{1,0:T(8,128)(2,1)S(1)}, bf16[784,384]{1,0:T(8,128)(2,1)S(1)}, u32[]{:S(2)}, u32[]{:S(2)}) collective-permute-start(bf16[784,384]{1,0:T(8,128)(2,1)S(1)} %get-tuple-element.23), channel_id=1, source_target_pairs={{0,7},{1,0},{2,1},{3,2},{4,3},{5,4},{6,5},{7,6},{8,15},{9,8},{10,9... | collective-permute-start | bytes 1806344 | tf_op jit(solution)/shard_map/ppermute | solution.py:593
  11.1 2.0 %collective-permute-start = (bf16[784,384]{1,0:T(8,128)(2,1)S(1)}, bf16[784,384]{1,0:T(8,128)(2,1)S(1)}, u32[]{:S(2)}, u32[]{:S(2)}) collective-permute-start(bf16[784,384]{1,0:T(8,128)(2,1)S(1)} %get-tuple-element.17.own_ref), channel_id=1, source_target_pairs={{0,120},{8,0},{16,8},{24,16},{32,24},{40,32},{48,40},{56,48},{64,5... | collective-permute-start | bytes 1806344 | tf_op jit(solution)/shard_map/ppermute | solution.py:593
  13.1 0.0 copy-done
  13.1 18.2 %inner.1 = (f32[8,3,2,48,128]{4,3,2,1,0:T(8,128)S(1)}, bf16[8,2,48,384]{3,2,1,0:T(8,128)(2,1)S(1)}, bf16[2,8,2,48,384]{4,3,2,1,0:T(8,128)(2,1)S(1)}, f32[8,24,128]{2,1,0:T(8,128)S(1)}, f32[8,24,128]{2,1,0:T(8,128)S(1)}) custom-call(bf16[2,24,4,3,16,128]{5,4,3,2,1,0:T(8,128)(2,1)S(1)} %bitcast.8, bf16[2,4,3,3,16,128]{5,4,3,2,1,0:T(8,128)(2,1)} %bitcast.12, ...), custom_call_target="tpu_custom_call" | custom-call | flops 40000000000 | bytes 6000000 | tf_op jit(solution)/shard_map/inner/pallas_call | solution.py:289
  31.3 0.0 collective-permute-done.face.ft
  31.3 1.6 %outer_t.1 = (f32[8,2,48,128]{3,2,1,0:T(8,128)S(1)}, f32[8,128]{1,0:T(8,128)S(1)}) custom-call(bf16[784,384]{1,0:T(8,128)(2,1)S(1)} %collective-permute-done.face.ft, bf16[8,2,48,384]{3,2,1,0:T(8,128)(2,1)S(1)} %get-tuple-element.19.refs_0_, f32[8,24,128]{2,1,0:T(8,128)S(1)} %get-tuple-element.20.refs_1_, f32[8,128]{1,0:T(8,128)S(1)} %get-tuple-element.21.refs_2_.vec), custom_call_target="tpu_custom_call" | custom-call | tf_op jit(solution)/shard_map/outer_t/pallas_call | solution.py:427
  33.0 0.0 collective-permute-start.2
  33.0 0.0 collective-permute-done.1.face.fz
  33.0 1.6 %outer_z.1 = (f32[8,2,48,128]{3,2,1,0:T(8,128)S(1)}, f32[8,128]{1,0:T(8,128)S(1)}) custom-call(bf16[784,384]{1,0:T(8,128)(2,1)S(1)} %collective-permute-done.1.face.fz, bf16[2,8,2,48,384]{4,3,2,1,0:T(8,128)(2,1)S(1)} %get-tuple-element.24.refs_0_, f32[8,24,128]{2,1,0:T(8,128)S(1)} %get-tuple-element.25.refs_1_, f32[8,128]{1,0:T(8,128)S(1)} %get-tuple-element.21.refs_2_.vec), custom_call_target="tpu_custom_call" | custom-call | tf_op jit(solution)/shard_map/outer_z/pallas_call | solution.py:427
  34.6 0.0 collective-permute-start.3
  34.6 2.0 %first.1.part = f32[8,128]{1,0:T(8,128)S(1)} custom-call(f32[8,3,2,48,128]{4,3,2,1,0:T(8,128)S(1)} %get-tuple-element.18.inner, f32[8,2,48,128]{3,2,1,0:T(8,128)S(1)} %get-tuple-element.22.outer_t, f32[8,2,48,128]{3,2,1,0:T(8,128)S(1)} %get-tuple-element.26.outer_z, f32[8,128]{1,0:T(8,128)S(1)} %get-tuple-element.21.refs_2_.vec, ...), custom_call_target="tpu_custom_call" | custom-call | tf_op jit(solution)/shard_map/first/pallas_call | solution.py:568
  36.6 1.5 %collective-permute-done.2.rt = f32[8,128]{1,0:T(8,128)S(1)} collective-permute-done((f32[8,128]{1,0:T(8,128)S(1)}, f32[8,128]{1,0:T(8,128)S(1)}, u32[]{:S(2)}, u32[]{:S(2)}) %collective-permute-start.2) | collective-permute-done | bytes 4128 | tf_op jit(solution)/shard_map/ppermute | solution.py:593
  38.1 3.8 %collective-permute-done.3.rz = f32[8,128]{1,0:T(8,128)S(1)} collective-permute-done((f32[8,128]{1,0:T(8,128)S(1)}, f32[8,128]{1,0:T(8,128)S(1)}, u32[]{:S(2)}, u32[]{:S(2)}) %collective-permute-start.3) | collective-permute-done | bytes 4128 | tf_op jit(solution)/shard_map/ppermute | solution.py:593
  41.9 0.6 %back.1 = (f32[8,128]{1,0:T(8,128)S(1)}, f32[8,128]{1,0:T(8,128)S(1)}, f32[8,128]{1,0:T(8,128)S(1)}) custom-call(f32[8,2,48,128]{3,2,1,0:T(8,128)S(1)} %get-tuple-element.22.outer_t, f32[8,2,48,128]{3,2,1,0:T(8,128)S(1)} %get-tuple-element.26.outer_z, f32[8,128]{1,0:T(8,128)S(1)} %first.1.part, f32[8,128]{1,0:T(8,128)S(1)} %collective-permute-done.2.rt, ...), custom_call_target="tpu_custom_call" | custom-call | tf_op jit(solution)/shard_map/back/pallas_call | solution.py:568
  42.4 0.1 collective-permute-start.4
  42.5 0.1 collective-permute-start.5
  42.6 5.6 %collective-permute-start.7 = (f32[8,128]{1,0:T(8,128)S(1)}, f32[8,128]{1,0:T(8,128)S(1)}, u32[]{:S(2)}, u32[]{:S(2)}) collective-permute-start(f32[8,128]{1,0:T(8,128)S(1)} %get-tuple-element.29.vec), channel_id=1, source_target_pairs={{0,7},{1,0},{2,1},{3,2},{4,3},{5,4},{6,5},{7,6},{8,15},{9,8},{10,9... | collective-permute-start | bytes 12296 | tf_op jit(solution)/shard_map/ppermute | solution.py:593
  48.2 3.2 %collective-permute-start.6 = (f32[8,128]{1,0:T(8,128)S(1)}, f32[8,128]{1,0:T(8,128)S(1)}, u32[]{:S(2)}, u32[]{:S(2)}) collective-permute-start(f32[8,128]{1,0:T(8,128)S(1)} %get-tuple-element.29.vec), channel_id=1, source_target_pairs={{0,120},{8,0},{16,8},{24,16},{32,24},{40,32},{48,40},{56,48},{64,5... | collective-permute-start | bytes 12296 | tf_op jit(solution)/shard_map/ppermute | solution.py:593
  51.4 1.9 %blocks.1 = f32[5,8,4608]{2,1,0:T(8,128)} custom-call(f32[8,3,2,48,128]{4,3,2,1,0:T(8,128)S(1)} %get-tuple-element.18.inner, f32[8,2,48,128]{3,2,1,0:T(8,128)S(1)} %get-tuple-element.22.outer_t, f32[8,2,48,128]{3,2,1,0:T(8,128)S(1)} %get-tuple-element.26.outer_z), custom_call_target="tpu_custom_call" | custom-call | bytes 6000000 | tf_op jit(solution)/shard_map/blocks/pallas_call | solution.py:580
  53.4 0.9 %local.1.part = f32[8,128]{1,0:T(8,128)S(1)} custom-call(f32[8,3,2,48,128]{4,3,2,1,0:T(8,128)S(1)} %get-tuple-element.18.inner, f32[8,128]{1,0:T(8,128)S(1)} %get-tuple-element.29.vec), custom_call_target="tpu_custom_call" | custom-call | tf_op jit(solution)/shard_map/local/pallas_call | solution.py:568
  54.3 0.0 collective-permute-done.4.rt
  54.3 0.0 collective-permute-done.5.rz
  54.3 0.0 collective-permute-done.7.vz
  54.3 0.0 collective-permute-done.6.vt
  54.3 1.1 %last.1 = f32[8,96]{1,0:T(8,128)} custom-call(f32[8,2,48,128]{3,2,1,0:T(8,128)S(1)} %get-tuple-element.22.outer_t, f32[8,2,48,128]{3,2,1,0:T(8,128)S(1)} %get-tuple-element.26.outer_z, f32[8,128]{1,0:T(8,128)S(1)} %local.1.part, f32[8,128]{1,0:T(8,128)S(1)} %collective-permute-done.4.rt, f32[8,128]{1,0:T(8,128)S(1)} %collective-permute-done.5.rz, ...), custom_call_target="tpu_custom_call" | custom-call | tf_op jit(solution)/shard_map/last/pallas_call | solution.py:568
Async XLA Ops:
  0.6 12.5 %copy-start = (bf16[2,24,4,3,4,4,128]{6,5,4,3,2,1,0:T(4,128)(2,1)S(1)}, bf16[2,24,4,3,4,4,128]{6,5,4,3,2,1,0:T(4,128)(2,1)}, u32[]{:S(2)}) copy-start(bf16[2,24,4,3,4,4,128]{6,5,4,3,2,1,0:T(4,128)(2,1)} %param.3) | copy-start | bytes 7077892
  4.3 28.7 %collective-permute-start.1 = (bf16[784,384]{1,0:T(8,128)(2,1)S(1)}, bf16[784,384]{1,0:T(8,128)(2,1)S(1)}, u32[]{:S(2)}, u32[]{:S(2)}) collective-permute-start(bf16[784,384]{1,0:T(8,128)(2,1)S(1)} %get-tuple-element.23), channel_id=1, source_target_pairs={{0,7},{1,0},{2,1},{3,2},{4,3},{5,4},{6,5},{7,6},{8,15},{9,8},{10,9... | collective-permute-start | bytes 1806344 | tf_op jit(solution)/shard_map/ppermute | solution.py:593
  11.1 20.2 %collective-permute-start = (bf16[784,384]{1,0:T(8,128)(2,1)S(1)}, bf16[784,384]{1,0:T(8,128)(2,1)S(1)}, u32[]{:S(2)}, u32[]{:S(2)}) collective-permute-start(bf16[784,384]{1,0:T(8,128)(2,1)S(1)} %get-tuple-element.17.own_ref), channel_id=1, source_target_pairs={{0,120},{8,0},{16,8},{24,16},{32,24},{40,32},{48,40},{56,48},{64,5... | collective-permute-start | bytes 1806344 | tf_op jit(solution)/shard_map/ppermute | solution.py:593
  33.0 5.1 %collective-permute-start.2 = (f32[8,128]{1,0:T(8,128)S(1)}, f32[8,128]{1,0:T(8,128)S(1)}, u32[]{:S(2)}, u32[]{:S(2)}) collective-permute-start(f32[8,128]{1,0:T(8,128)S(1)} %get-tuple-element.27), channel_id=1, source_target_pairs={{0,8},{8,16},{16,24},{24,32},{32,40},{40,48},{48,56},{56,64},{64,7... | collective-permute-start | bytes 12296 | tf_op jit(solution)/shard_map/ppermute | solution.py:593
  34.6 7.2 %collective-permute-start.3 = (f32[8,128]{1,0:T(8,128)S(1)}, f32[8,128]{1,0:T(8,128)S(1)}, u32[]{:S(2)}, u32[]{:S(2)}) collective-permute-start(f32[8,128]{1,0:T(8,128)S(1)} %get-tuple-element.28), channel_id=1, source_target_pairs={{0,1},{1,2},{2,3},{3,4},{4,5},{5,6},{6,7},{7,0},{8,9},{9,10},{10,1... | collective-permute-start | bytes 12296 | tf_op jit(solution)/shard_map/ppermute | solution.py:593
  42.4 11.9 %collective-permute-start.4 = (f32[8,128]{1,0:T(8,128)S(1)}, f32[8,128]{1,0:T(8,128)S(1)}, u32[]{:S(2)}, u32[]{:S(2)}) collective-permute-start(f32[8,128]{1,0:T(8,128)S(1)} %get-tuple-element.30), channel_id=1, source_target_pairs={{0,8},{8,16},{16,24},{24,32},{32,40},{40,48},{48,56},{56,64},{64,7... | collective-permute-start | bytes 12296 | tf_op jit(solution)/shard_map/ppermute | solution.py:593
  42.5 11.8 %collective-permute-start.5 = (f32[8,128]{1,0:T(8,128)S(1)}, f32[8,128]{1,0:T(8,128)S(1)}, u32[]{:S(2)}, u32[]{:S(2)}) collective-permute-start(f32[8,128]{1,0:T(8,128)S(1)} %get-tuple-element.31), channel_id=1, source_target_pairs={{0,1},{1,2},{2,3},{3,4},{4,5},{5,6},{6,7},{7,0},{8,9},{9,10},{10,1... | collective-permute-start | bytes 12296 | tf_op jit(solution)/shard_map/ppermute | solution.py:593
  42.6 11.7 %collective-permute-start.7 = (f32[8,128]{1,0:T(8,128)S(1)}, f32[8,128]{1,0:T(8,128)S(1)}, u32[]{:S(2)}, u32[]{:S(2)}) collective-permute-start(f32[8,128]{1,0:T(8,128)S(1)} %get-tuple-element.29.vec), channel_id=1, source_target_pairs={{0,7},{1,0},{2,1},{3,2},{4,3},{5,4},{6,5},{7,6},{8,15},{9,8},{10,9... | collective-permute-start | bytes 12296 | tf_op jit(solution)/shard_map/ppermute | solution.py:593
  48.2 6.1 %collective-permute-start.6 = (f32[8,128]{1,0:T(8,128)S(1)}, f32[8,128]{1,0:T(8,128)S(1)}, u32[]{:S(2)}, u32[]{:S(2)}) collective-permute-start(f32[8,128]{1,0:T(8,128)S(1)} %get-tuple-element.29.vec), channel_id=1, source_target_pairs={{0,120},{8,0},{16,8},{24,16},{32,24},{40,32},{48,40},{56,48},{64,5... | collective-permute-start | bytes 12296 | tf_op jit(solution)/shard_map/ppermute | solution.py:593

commit v8 on v7

--- a/solution.py
+++ b/solution.py
@@ -121,18 +121,13 @@
 
     fetch.wait()
 
-    flat[...] = jnp.zeros_like(flat)
-
     @pl.loop(0, 4)
     def _(mu):
-        for c in range(3):
-            for d in range(3):
-                for ri in range(2):
-                    row = ((c * 3 + d) * 2 + ri) * 16
-                    flat[pl.ds(row, 16), :] = 0.5 * u_ref[ri, mu, c, d].astype(F32)
-
+        parts = [u_ref[ri, mu, c, d] for c in range(3) for d in range(3) for ri in range(2)]
+        parts += [jnp.zeros((16, 128), BF16)] * 6
+        flat[...] = 0.5 * jnp.swapaxes(jnp.stack(parts).astype(F32), 0, 1)
         drop = ((lane_ids(24) & 12) == 12) & (mu == 1)
-        sets = [[flat[pl.ds(t * 4 + z, 24, stride=16), :] for z in range(4)] for t in range(4)]
+        sets = [[flat[t * 4 + z] for z in range(4)] for t in range(4)]
         for group in ((0, 1), (2, 3)):
             done = exchange_twice([sets[t] for t in group])
             for t, values in zip(group, done):
@@ -141,14 +136,14 @@
 
         @pl.when(mu == 1)
         def _():
-            last = [flat[pl.ds(t * 4 + 3, 24, stride=16), :] for t in range(4)]
+            last = [flat[t * 4 + 3] for t in range(4)]
             for a, value in enumerate(exchange_twice([last])[0]):
                 uz_ref[a] = value
 
     for a in range(8):
         ut_ref[a] = uf[a, 0, 3]
 
-    def fill(a, chi):
+    def fill(a, chi, times=range(4)):
         ahead = lax.rem(a + 1, 8)
         x_last = jnp.where((lane_ids(NV) & 3) == 3, -1.0, 0.0).astype(F32)
         x_last_pair = (lane_ids(ROWS) & 3) == 3
@@ -172,7 +167,7 @@
             return colour(link, vector)
 
         nothing = [(jnp.zeros((NV, 128), F32),) * 2] * 3
-        for t in range(4):
+        for t in times:
             for slot in range(3):
                 if slot == 0:
                     one, two = hop(t, 0) if t < 3 else nothing, hop(t, 1)
@@ -186,22 +181,29 @@
                         both = jnp.concatenate([one[c][ri], two[c][ri]], 0).astype(BF16)
                         cm[chi, slot, ri * ROWS : ri * ROWS + ROWS, column] = both
 
-    def multiply(a, chi):
+    def multiply(a, chi, beside=None):
         near, far = vm[0, a, chi], vm[0, a, 1 - chi]
-        return (
-            nt(jnp.concatenate([near, far, vm[1, a, 1 - chi]], 0), cm[chi, 0]),
-            nt(jnp.concatenate([near, vm[3, a, 1 - chi]], 0), cm[chi, 1]),
-            nt(jnp.concatenate([near, vm[2, a, 1 - chi]], 0), cm[chi, 2]),
-            nt(near, near),
+        lefts = (
+            lambda: jnp.concatenate([near, far, vm[1, a, 1 - chi]], 0),
+            lambda: jnp.concatenate([near, vm[3, a, 1 - chi]], 0),
+            lambda: jnp.concatenate([near, vm[2, a, 1 - chi]], 0),
+            lambda: near,
         )
+        blocks = []
+        for k, left in enumerate(lefts):
+            blocks.append(nt(left(), cm[chi, k] if k < 3 else near))
+            if beside is not None:
+                beside(k)
+        return blocks
 
     def keep(blocks):
         for value, (start, rows) in zip(blocks, ((0, 144), (144, 96), (240, 96), (336, 48))):
             kept[start : start + rows, : value.shape[1]] = value
 
-    def finish(a):
+    def finish(a, beside=None):
+        second = multiply(a, 1, beside)
         first = (kept[0:144, :96], kept[144:240, :96], kept[240:336, :96], kept[336:384, :ROWS])
-        combine_inner([first, multiply(a, 1)], a, out_ref)
+        combine_inner([first, second], a, out_ref)
 
     fill(0, 0)
     keep(multiply(0, 0))
@@ -209,10 +211,8 @@
 
     @pl.loop(1, 8)
     def _(a):
-        finish(a - 1)
-        fill(a, 0)
-        keep(multiply(a, 0))
-        fill(a, 1)
+        finish(a - 1, lambda k: fill(a, 0, (k,)))
+        keep(multiply(a, 0, lambda k: fill(a, 1, (k,))))
 
     finish(7)
 
@@ -301,7 +301,7 @@
             pltpu.VMEM((4, 8, 2, ROWS, 1536), BF16),
             pltpu.VMEM((8, 4, 4, 24, 128), F32),
             pltpu.VMEM((2, 3, 96, 1536), BF16),
-            pltpu.VMEM((384, 128), F32),
+            pltpu.VMEM((16, 24, 128), F32),
             pltpu.VMEM((2, 16, ROWS, 128), BF16),
             pltpu.VMEM((384, 128), F32),
             pltpu.VMEM((2, 4, 3, 3, 16, 128), BF16),
@@ -384,12 +384,11 @@
 def outer_kernel(mu, face, *refs):
     lefts, (links, vec_ref, out_ref, back_ref, cm) = refs[:-5], refs[-5:]
 
-    @pl.loop(0, 8)
-    def _(a):
+    for a in range(8):
         for chi in range(2):
             link = [links[a, pl.ds(k, 1), :] for k in range(18)]
             vector = []
-            rows = pl.ds(pl.multiple_of((a * 2 + chi) * ROWS, ROWS), ROWS)
+            rows = pl.ds((a * 2 + chi) * ROWS, ROWS)
             for d in range(3):
                 value = face[rows, d * 128 : (d + 1) * 128].astype(F32)
                 vector += [value[:NV], value[NV:]]

time: 55.5 us -> 55 us (level)
  Pallas kernels: 31.5 us -> 30.6 us
  transfers between devices with their start and end apart: 8 -> 8, of which waited for: 2 -> 2; matrix products, arithmetic and copies ran while one was open for 0% -> 0% of each run, Pallas kernels for 47% -> 46%
where the time goes in v8:
time: 55 us; the launch traced here: 54.9 us
  Pallas kernels  30.6 us (56%)
  starting transfers between devices  18.3 us (33%)
  waiting for transfers between devices  5.24 us (10%)
  between operations  0.74 us (1%)
    ppermute x8, starting transfers between devices, shifted(): lax.ppermute(value, axis, [(k, (k + steps) % count) for k in range(count)])  18.3 us
    pallas_call x1, Pallas kernels, inner_call(): pl.pallas_call(inner_kernel, out_shape=(shape((8, 3, 2, ROWS, 128), F32),...  17.7 us
    ppermute x8, waiting for transfers between devices, shifted(): lax.ppermute(value, axis, [(k, (k + steps) % count) for k in range(count)])  5.24 us
    pallas_call x4, Pallas kernels, small_call(): pl.pallas_call(kernel, out_shape=(row,) * count, in_specs=[vmem] * len(ar...  4.52 us
    pallas_call x1, Pallas kernels, face_call(): pl.pallas_call(face_kernel, out_shape=(face, face, jax.ShapeDtypeStruct((...  3.64 us
    pallas_call x2, Pallas kernels, outer_call(): pl.pallas_call(functools.partial(outer_kernel, mu), out_shape=(shape((8,...  2.74 us
    pallas_call x1, Pallas kernels, blocks_call(): pl.pallas_call(blocks_kernel, out_shape=jax.ShapeDtypeStruct((5, 8, 2 * R...  1.95 us
  transfers between devices with their start and end apart: 8, of which 2 were waited for; matrix products, arithmetic and copies ran while one was open for 0% of the time, Pallas kernels for 46%

profile of v8, /device:TPU:0, one launch (start us, length us, event | category | flops | bytes accessed | tf_op | source)
XLA Modules:
  0.0 54.9 jit_solution(16305764011195285846)
XLA Ops:
  0.6 0.0 copy-start
  0.6 3.6 %faces.1 = (bf16[784,384]{1,0:T(8,128)(2,1)S(1)}, bf16[784,384]{1,0:T(8,128)(2,1)S(1)}, f32[8,128]{1,0:T(8,128)S(1)}) custom-call(bf16[2,24,4,3,16,128]{5,4,3,2,1,0:T(8,128)(2,1)} %bitcast.7, f32[8,96]{1,0:T(8,128)} %bitcast.10), custom_call_target="tpu_custom_call" | custom-call | tf_op jit(solution)/shard_map/faces/pallas_call | solution.py:368
  4.3 6.8 %collective-permute-start.1 = (bf16[784,384]{1,0:T(8,128)(2,1)S(1)}, bf16[784,384]{1,0:T(8,128)(2,1)S(1)}, u32[]{:S(2)}, u32[]{:S(2)}) collective-permute-start(bf16[784,384]{1,0:T(8,128)(2,1)S(1)} %get-tuple-element.23), channel_id=1, source_target_pairs={{0,7},{1,0},{2,1},{3,2},{4,3},{5,4},{6,5},{7,6},{8,15},{9,8},{10,9... | collective-permute-start | bytes 1806344 | tf_op jit(solution)/shard_map/ppermute | solution.py:592
  11.1 2.0 %collective-permute-start = (bf16[784,384]{1,0:T(8,128)(2,1)S(1)}, bf16[784,384]{1,0:T(8,128)(2,1)S(1)}, u32[]{:S(2)}, u32[]{:S(2)}) collective-permute-start(bf16[784,384]{1,0:T(8,128)(2,1)S(1)} %get-tuple-element.17.own_ref), channel_id=1, source_target_pairs={{0,120},{8,0},{16,8},{24,16},{32,24},{40,32},{48,40},{56,48},{64,5... | collective-permute-start | bytes 1806344 | tf_op jit(solution)/shard_map/ppermute | solution.py:592
  13.1 0.0 copy-done
  13.1 17.7 %inner.1 = (f32[8,3,2,48,128]{4,3,2,1,0:T(8,128)S(1)}, bf16[8,2,48,384]{3,2,1,0:T(8,128)(2,1)S(1)}, bf16[2,8,2,48,384]{4,3,2,1,0:T(8,128)(2,1)S(1)}, f32[8,24,128]{2,1,0:T(8,128)S(1)}, f32[8,24,128]{2,1,0:T(8,128)S(1)}) custom-call(bf16[2,24,4,3,16,128]{5,4,3,2,1,0:T(8,128)(2,1)S(1)} %bitcast.8, bf16[2,4,3,3,16,128]{5,4,3,2,1,0:T(8,128)(2,1)} %bitcast.12, ...), custom_call_target="tpu_custom_call" | custom-call | flops 40000000000 | bytes 6000000 | tf_op jit(solution)/shard_map/inner/pallas_call | solution.py:289
  30.9 0.0 collective-permute-done.face.ft
  30.9 1.4 %outer_t.1 = (f32[8,2,48,128]{3,2,1,0:T(8,128)S(1)}, f32[8,128]{1,0:T(8,128)S(1)}) custom-call(bf16[784,384]{1,0:T(8,128)(2,1)S(1)} %collective-permute-done.face.ft, bf16[8,2,48,384]{3,2,1,0:T(8,128)(2,1)S(1)} %get-tuple-element.19.refs_0_, f32[8,24,128]{2,1,0:T(8,128)S(1)} %get-tuple-element.20.refs_1_, f32[8,128]{1,0:T(8,128)S(1)} %get-tuple-element.21.refs_2_.vec), custom_call_target="tpu_custom_call" | custom-call | tf_op jit(solution)/shard_map/outer_t/pallas_call | solution.py:426
  32.2 0.5 collective-permute-start.2
  32.7 0.0 collective-permute-done.1.face.fz
  32.7 1.4 %outer_z.1 = (f32[8,2,48,128]{3,2,1,0:T(8,128)S(1)}, f32[8,128]{1,0:T(8,128)S(1)}) custom-call(bf16[784,384]{1,0:T(8,128)(2,1)S(1)} %collective-permute-done.1.face.fz, bf16[2,8,2,48,384]{4,3,2,1,0:T(8,128)(2,1)S(1)} %get-tuple-element.24.refs_0_, f32[8,24,128]{2,1,0:T(8,128)S(1)} %get-tuple-element.25.refs_1_, f32[8,128]{1,0:T(8,128)S(1)} %get-tuple-element.21.refs_2_.vec), custom_call_target="tpu_custom_call" | custom-call | tf_op jit(solution)/shard_map/outer_z/pallas_call | solution.py:426
  34.1 0.0 collective-permute-start.3
  34.1 2.0 %first.1.part = f32[8,128]{1,0:T(8,128)S(1)} custom-call(f32[8,3,2,48,128]{4,3,2,1,0:T(8,128)S(1)} %get-tuple-element.18.inner, f32[8,2,48,128]{3,2,1,0:T(8,128)S(1)} %get-tuple-element.22.outer_t, f32[8,2,48,128]{3,2,1,0:T(8,128)S(1)} %get-tuple-element.26.outer_z, f32[8,128]{1,0:T(8,128)S(1)} %get-tuple-element.21.refs_2_.vec, ...), custom_call_target="tpu_custom_call" | custom-call | tf_op jit(solution)/shard_map/first/pallas_call | solution.py:567
  36.1 1.3 %collective-permute-done.2.rt = f32[8,128]{1,0:T(8,128)S(1)} collective-permute-done((f32[8,128]{1,0:T(8,128)S(1)}, f32[8,128]{1,0:T(8,128)S(1)}, u32[]{:S(2)}, u32[]{:S(2)}) %collective-permute-start.2) | collective-permute-done | bytes 4128 | tf_op jit(solution)/shard_map/ppermute | solution.py:592
  37.4 3.9 %collective-permute-done.3.rz = f32[8,128]{1,0:T(8,128)S(1)} collective-permute-done((f32[8,128]{1,0:T(8,128)S(1)}, f32[8,128]{1,0:T(8,128)S(1)}, u32[]{:S(2)}, u32[]{:S(2)}) %collective-permute-start.3) | collective-permute-done | bytes 4128 | tf_op jit(solution)/shard_map/ppermute | solution.py:592
  41.3 0.6 %back.1 = (f32[8,128]{1,0:T(8,128)S(1)}, f32[8,128]{1,0:T(8,128)S(1)}, f32[8,128]{1,0:T(8,128)S(1)}) custom-call(f32[8,2,48,128]{3,2,1,0:T(8,128)S(1)} %get-tuple-element.22.outer_t, f32[8,2,48,128]{3,2,1,0:T(8,128)S(1)} %get-tuple-element.26.outer_z, f32[8,128]{1,0:T(8,128)S(1)} %first.1.part, f32[8,128]{1,0:T(8,128)S(1)} %collective-permute-done.2.rt, ...), custom_call_target="tpu_custom_call" | custom-call | tf_op jit(solution)/shard_map/back/pallas_call | solution.py:567
  41.9 0.1 collective-permute-start.4
  42.0 0.1 collective-permute-start.5
  42.1 5.6 %collective-permute-start.7 = (f32[8,128]{1,0:T(8,128)S(1)}, f32[8,128]{1,0:T(8,128)S(1)}, u32[]{:S(2)}, u32[]{:S(2)}) collective-permute-start(f32[8,128]{1,0:T(8,128)S(1)} %get-tuple-element.29.vec), channel_id=1, source_target_pairs={{0,7},{1,0},{2,1},{3,2},{4,3},{5,4},{6,5},{7,6},{8,15},{9,8},{10,9... | collective-permute-start | bytes 12296 | tf_op jit(solution)/shard_map/ppermute | solution.py:592
  47.7 3.2 %collective-permute-start.6 = (f32[8,128]{1,0:T(8,128)S(1)}, f32[8,128]{1,0:T(8,128)S(1)}, u32[]{:S(2)}, u32[]{:S(2)}) collective-permute-start(f32[8,128]{1,0:T(8,128)S(1)} %get-tuple-element.29.vec), channel_id=1, source_target_pairs={{0,120},{8,0},{16,8},{24,16},{32,24},{40,32},{48,40},{56,48},{64,5... | collective-permute-start | bytes 12296 | tf_op jit(solution)/shard_map/ppermute | solution.py:592
  50.9 1.9 %blocks.1 = f32[5,8,4608]{2,1,0:T(8,128)} custom-call(f32[8,3,2,48,128]{4,3,2,1,0:T(8,128)S(1)} %get-tuple-element.18.inner, f32[8,2,48,128]{3,2,1,0:T(8,128)S(1)} %get-tuple-element.22.outer_t, f32[8,2,48,128]{3,2,1,0:T(8,128)S(1)} %get-tuple-element.26.outer_z), custom_call_target="tpu_custom_call" | custom-call | bytes 6000000 | tf_op jit(solution)/shard_map/blocks/pallas_call | solution.py:579
  52.9 0.9 %local.1.part = f32[8,128]{1,0:T(8,128)S(1)} custom-call(f32[8,3,2,48,128]{4,3,2,1,0:T(8,128)S(1)} %get-tuple-element.18.inner, f32[8,128]{1,0:T(8,128)S(1)} %get-tuple-element.29.vec), custom_call_target="tpu_custom_call" | custom-call | tf_op jit(solution)/shard_map/local/pallas_call | solution.py:567
  53.8 0.0 collective-permute-done.4.rt
  53.8 0.0 collective-permute-done.5.rz
  53.8 0.0 collective-permute-done.7.vz
  53.8 0.0 collective-permute-done.6.vt
  53.8 1.1 %last.1 = f32[8,96]{1,0:T(8,128)} custom-call(f32[8,2,48,128]{3,2,1,0:T(8,128)S(1)} %get-tuple-element.22.outer_t, f32[8,2,48,128]{3,2,1,0:T(8,128)S(1)} %get-tuple-element.26.outer_z, f32[8,128]{1,0:T(8,128)S(1)} %local.1.part, f32[8,128]{1,0:T(8,128)S(1)} %collective-permute-done.4.rt, f32[8,128]{1,0:T(8,128)S(1)} %collective-permute-done.5.rz, ...), custom_call_target="tpu_custom_call" | custom-call | tf_op jit(solution)/shard_map/last/pallas_call | solution.py:567
Async XLA Ops:
  0.6 12.5 %copy-start = (bf16[2,24,4,3,4,4,128]{6,5,4,3,2,1,0:T(4,128)(2,1)S(1)}, bf16[2,24,4,3,4,4,128]{6,5,4,3,2,1,0:T(4,128)(2,1)}, u32[]{:S(2)}) copy-start(bf16[2,24,4,3,4,4,128]{6,5,4,3,2,1,0:T(4,128)(2,1)} %param.3) | copy-start | bytes 7077892
  4.3 28.5 %collective-permute-start.1 = (bf16[784,384]{1,0:T(8,128)(2,1)S(1)}, bf16[784,384]{1,0:T(8,128)(2,1)S(1)}, u32[]{:S(2)}, u32[]{:S(2)}) collective-permute-start(bf16[784,384]{1,0:T(8,128)(2,1)S(1)} %get-tuple-element.23), channel_id=1, source_target_pairs={{0,7},{1,0},{2,1},{3,2},{4,3},{5,4},{6,5},{7,6},{8,15},{9,8},{10,9... | collective-permute-start | bytes 1806344 | tf_op jit(solution)/shard_map/ppermute | solution.py:592
  11.1 19.8 %collective-permute-start = (bf16[784,384]{1,0:T(8,128)(2,1)S(1)}, bf16[784,384]{1,0:T(8,128)(2,1)S(1)}, u32[]{:S(2)}, u32[]{:S(2)}) collective-permute-start(bf16[784,384]{1,0:T(8,128)(2,1)S(1)} %get-tuple-element.17.own_ref), channel_id=1, source_target_pairs={{0,120},{8,0},{16,8},{24,16},{32,24},{40,32},{48,40},{56,48},{64,5... | collective-permute-start | bytes 1806344 | tf_op jit(solution)/shard_map/ppermute | solution.py:592
  32.2 5.1 %collective-permute-start.2 = (f32[8,128]{1,0:T(8,128)S(1)}, f32[8,128]{1,0:T(8,128)S(1)}, u32[]{:S(2)}, u32[]{:S(2)}) collective-permute-start(f32[8,128]{1,0:T(8,128)S(1)} %get-tuple-element.27), channel_id=1, source_target_pairs={{0,8},{8,16},{16,24},{24,32},{32,40},{40,48},{48,56},{56,64},{64,7... | collective-permute-start | bytes 12296 | tf_op jit(solution)/shard_map/ppermute | solution.py:592
  34.1 7.2 %collective-permute-start.3 = (f32[8,128]{1,0:T(8,128)S(1)}, f32[8,128]{1,0:T(8,128)S(1)}, u32[]{:S(2)}, u32[]{:S(2)}) collective-permute-start(f32[8,128]{1,0:T(8,128)S(1)} %get-tuple-element.28), channel_id=1, source_target_pairs={{0,1},{1,2},{2,3},{3,4},{4,5},{5,6},{6,7},{7,0},{8,9},{9,10},{10,1... | collective-permute-start | bytes 12296 | tf_op jit(solution)/shard_map/ppermute | solution.py:592
  41.9 11.9 %collective-permute-start.4 = (f32[8,128]{1,0:T(8,128)S(1)}, f32[8,128]{1,0:T(8,128)S(1)}, u32[]{:S(2)}, u32[]{:S(2)}) collective-permute-start(f32[8,128]{1,0:T(8,128)S(1)} %get-tuple-element.30), channel_id=1, source_target_pairs={{0,8},{8,16},{16,24},{24,32},{32,40},{40,48},{48,56},{56,64},{64,7... | collective-permute-start | bytes 12296 | tf_op jit(solution)/shard_map/ppermute | solution.py:592
  42.0 11.8 %collective-permute-start.5 = (f32[8,128]{1,0:T(8,128)S(1)}, f32[8,128]{1,0:T(8,128)S(1)}, u32[]{:S(2)}, u32[]{:S(2)}) collective-permute-start(f32[8,128]{1,0:T(8,128)S(1)} %get-tuple-element.31), channel_id=1, source_target_pairs={{0,1},{1,2},{2,3},{3,4},{4,5},{5,6},{6,7},{7,0},{8,9},{9,10},{10,1... | collective-permute-start | bytes 12296 | tf_op jit(solution)/shard_map/ppermute | solution.py:592
  42.1 11.7 %collective-permute-start.7 = (f32[8,128]{1,0:T(8,128)S(1)}, f32[8,128]{1,0:T(8,128)S(1)}, u32[]{:S(2)}, u32[]{:S(2)}) collective-permute-start(f32[8,128]{1,0:T(8,128)S(1)} %get-tuple-element.29.vec), channel_id=1, source_target_pairs={{0,7},{1,0},{2,1},{3,2},{4,3},{5,4},{6,5},{7,6},{8,15},{9,8},{10,9... | collective-permute-start | bytes 12296 | tf_op jit(solution)/shard_map/ppermute | solution.py:592
  47.7 6.1 %collective-permute-start.6 = (f32[8,128]{1,0:T(8,128)S(1)}, f32[8,128]{1,0:T(8,128)S(1)}, u32[]{:S(2)}, u32[]{:S(2)}) collective-permute-start(f32[8,128]{1,0:T(8,128)S(1)} %get-tuple-element.29.vec), channel_id=1, source_target_pairs={{0,120},{8,0},{16,8},{24,16},{32,24},{40,32},{48,40},{56,48},{64,5... | collective-permute-start | bytes 12296 | tf_op jit(solution)/shard_map/ppermute | solution.py:592

commit v9 on v8

--- a/solution.py
+++ b/solution.py
@@ -315,7 +315,7 @@
     )(vectors, pltpu.with_memory_space_constraint(links, pltpu.HBM), own)
 
 
-def face_kernel(v_hbm, phi_hbm, t_ref, z_ref, vec_ref, flat, v_ref, phi_ref, sem):
+def face_kernel(stride, v_hbm, phi_hbm, out, vec_ref, flat, v_ref, phi_ref, sem):
     def fetch(chi, c, k):
         part = (slice(None), slice(None), pl.ds(2 * chi, 2), c)
         return pltpu.make_async_copy(v_hbm.at[part], v_ref.at[part], sem.at[k])
@@ -325,24 +325,26 @@
     small = pltpu.make_async_copy(phi_hbm, phi_ref, sem.at[6])
     small.start()
 
-    @pl.loop(0, 6)
-    def _(step):
-        chi, c = step // 3, step % 3
-        fetch(chi, c, step).wait()
-        for sb in range(2):
-            for ri in range(2):
-                block = v_ref[ri, :, 2 * chi + sb, c].astype(F32)
-                flat[sb, pl.ds(ri * 384, 384), :] = block.reshape(384, 128)
-        column = pl.multiple_of(c * 128, 128)
+    for pair in range(3):
+        steps = [(pair * 2 + k) for k in range(2)]
+        for k, step in enumerate(steps):
+            chi, c = step // 3, step % 3
+            fetch(chi, c, step).wait()
+            for sb in range(2):
+                for ri in range(2):
+                    block = v_ref[ri, :, 2 * chi + sb, c].astype(F32)
+                    flat[k, sb, ri * 384 : ri * 384 + 384, :] = block.reshape(384, 128)
 
         def load(k, plane):
-            return flat[plane // 4, pl.ds(plane % 4 * (1, 4)[k], ROWS, stride=16), :].astype(BF16)
+            first = plane % 4 * stride
+            return flat[k, plane // 4, pl.ds(first, ROWS, stride=16), :].astype(BF16)
 
         done = exchange([[load(k, plane) for plane in range(8)] for k in range(2)])
-        for out, values in zip((t_ref, z_ref), done):
+        for step, values in zip(steps, done):
+            chi, c = step // 3, step % 3
             for a, value in enumerate(values):
-                rows = pl.ds(pl.multiple_of((a * 2 + chi) * ROWS, ROWS), ROWS)
-                out[rows, pl.ds(column, 128)] = value
+                row = (a * 2 + chi) * ROWS
+                out[row : row + ROWS, c * 128 : c * 128 + 128] = value
 
     small.wait()
     vec = jnp.concatenate([phi_ref[...], jnp.zeros((8, 32), F32)], 1)
@@ -354,30 +356,29 @@
         pieces.append(piece.astype(F32))
     rider = jnp.concatenate(pieces, 1)
     rider = jnp.concatenate([rider, jnp.zeros((8, 384), F32)], 0).astype(BF16)
-    for ref in (t_ref, z_ref):
-        ref[768:784, :] = rider
+    out[768:784, :] = rider
 
 
 def ridden(face):
     return sum(face[768:784, 128 * k : 128 * k + 128].astype(F32)[:8] for k in range(3))
 
 
-def face_call(vectors, phi):
+def face_call(stride, name, vectors, phi):
     face = jax.ShapeDtypeStruct((784, 384), BF16)
     vmem = pl.BlockSpec(memory_space=pltpu.VMEM)
     return pl.pallas_call(
-        face_kernel,
-        out_shape=(face, face, jax.ShapeDtypeStruct((8, 128), F32)),
+        functools.partial(face_kernel, stride),
+        out_shape=(face, jax.ShapeDtypeStruct((8, 128), F32)),
         in_specs=[pl.BlockSpec(memory_space=pltpu.HBM)] * 2,
-        out_specs=(vmem,) * 3,
+        out_specs=(vmem,) * 2,
         scratch_shapes=[
-            pltpu.VMEM((2, 768, 128), F32),
+            pltpu.VMEM((2, 2, 768, 128), F32),
             pltpu.VMEM((2, NV, 4, 3, 16, 128), BF16),
             pltpu.VMEM((8, 2 * ROWS), F32),
             pltpu.SemaphoreType.DMA((7,)),
         ],
         compiler_params=pltpu.CompilerParams(vmem_limit_bytes=12 * 1024 * 1024),
-        name="faces",
+        name=name,
     )(*(pltpu.with_memory_space_constraint(x, pltpu.HBM) for x in (vectors, phi)))
 
 
@@ -595,9 +596,11 @@
 def per_device(null_vectors, gauge_links, coarse_in):
     vectors = null_vectors.reshape(2, NV, 4, 3, 16, 128)
     links = gauge_links.reshape(2, 4, 3, 3, 16, 128)
-    face_t, face_z, vec = face_call(vectors, coarse_in.reshape(8, 2 * ROWS))
-    own_t = face_t
-    face_t, face_z = shifted(face_t, "ta", -1), shifted(face_z, "sa", -1)
+    phi = coarse_in.reshape(8, 2 * ROWS)
+    face_z, vec = face_call(4, "face_z", vectors, phi)
+    own_t, _ = face_call(1, "face_t", vectors, phi)
+    face_z = shifted(face_z, "sa", -1)
+    face_t = shifted(own_t, "ta", -1)
     inner, left_t, left_z, link_t, link_z = inner_call(vectors, links, own_t)
     outer_t, bt = outer_call(0, "outer_t", face_t, left_t, link_t, vec)
     outer_z, bz = outer_call(1, "outer_z", face_z, left_z, link_z, vec)

time: 55 us -> 58.4 us (1.062)
  Pallas kernels: 30.6 us -> 32.5 us
  starting transfers between devices: 18.3 us -> 19.7 us
    pallas_call x1 -> x2, Pallas kernels: 3.64 us -> 5.57 us  [face_call(): pl.pallas_call(functools.partial(face_kernel, stride), out_shape=(face, j...]
    ppermute x8, starting transfers between devices: 18.3 us -> 19.7 us  [shifted(): lax.ppermute(value, axis, [(k, (k + steps) % count) for k in range(count)])]
  transfers between devices with their start and end apart: 8 -> 8, of which waited for: 2 -> 2; matrix products, arithmetic and copies ran while one was open for 0% -> 0% of each run, Pallas kernels for 46% -> 48%
where the time goes in v9:
time: 58.4 us; the launch traced here: 58.2 us
  Pallas kernels  32.5 us (56%)
  starting transfers between devices  19.7 us (34%)
  waiting for transfers between devices  5.24 us (9%)
  between operations  0.76 us (1%)
    ppermute x8, starting transfers between devices, shifted(): lax.ppermute(value, axis, [(k, (k + steps) % count) for k in range(count)])  19.7 us
    pallas_call x1, Pallas kernels, inner_call(): pl.pallas_call(inner_kernel, out_shape=(shape((8, 3, 2, ROWS, 128), F32),...  17.7 us
    pallas_call x2, Pallas kernels, face_call(): pl.pallas_call(functools.partial(face_kernel, stride), out_shape=(face, j...  5.57 us
    ppermute x8, waiting for transfers between devices, shifted(): lax.ppermute(value, axis, [(k, (k + steps) % count) for k in range(count)])  5.24 us
    pallas_call x4, Pallas kernels, small_call(): pl.pallas_call(kernel, out_shape=(row,) * count, in_specs=[vmem] * len(ar...  4.52 us
    pallas_call x2, Pallas kernels, outer_call(): pl.pallas_call(functools.partial(outer_kernel, mu), out_shape=(shape((8,...  2.74 us
    pallas_call x1, Pallas kernels, blocks_call(): pl.pallas_call(blocks_kernel, out_shape=jax.ShapeDtypeStruct((5, 8, 2 * R...  1.95 us
  transfers between devices with their start and end apart: 8, of which 2 were waited for; matrix products, arithmetic and copies ran while one was open for 0% of the time, Pallas kernels for 48%

profile of v9, /device:TPU:0, one launch (start us, length us, event | category | flops | bytes accessed | tf_op | source)
XLA Modules:
  0.0 58.2 jit_solution(610028647280767118)
XLA Ops:
  0.6 3.0 %face_t.1 = (bf16[784,384]{1,0:T(8,128)(2,1)S(1)}, f32[8,128]{1,0:T(8,128)}) custom-call(bf16[2,24,4,3,16,128]{5,4,3,2,1,0:T(8,128)(2,1)} %bitcast.7, f32[8,96]{1,0:T(8,128)} %bitcast.11), custom_call_target="tpu_custom_call" | custom-call | tf_op jit(solution)/shard_map/face_t/pallas_call | solution.py:369
  3.7 0.0 copy-start
  3.7 3.4 %collective-permute-start = (bf16[784,384]{1,0:T(8,128)(2,1)S(1)}, bf16[784,384]{1,0:T(8,128)(2,1)S(1)}, u32[]{:S(2)}, u32[]{:S(2)}) collective-permute-start(bf16[784,384]{1,0:T(8,128)(2,1)S(1)} %get-tuple-element.17.own_ref), channel_id=1, source_target_pairs={{0,120},{8,0},{16,8},{24,16},{32,24},{40,32},{48,40},{56,48},{64,5... | collective-permute-start | bytes 1806344 | tf_op jit(solution)/shard_map/ppermute | solution.py:593
  7.0 2.5 %face_z.1 = (bf16[784,384]{1,0:T(8,128)(2,1)S(1)}, f32[8,128]{1,0:T(8,128)S(1)}) custom-call(bf16[2,24,4,3,16,128]{5,4,3,2,1,0:T(8,128)(2,1)} %bitcast.8, f32[8,96]{1,0:T(8,128)} %bitcast.12), custom_call_target="tpu_custom_call" | custom-call | tf_op jit(solution)/shard_map/face_z/pallas_call | solution.py:369
  9.6 6.4 %collective-permute-start.1 = (bf16[784,384]{1,0:T(8,128)(2,1)S(1)}, bf16[784,384]{1,0:T(8,128)(2,1)S(1)}, u32[]{:S(2)}, u32[]{:S(2)}) collective-permute-start(bf16[784,384]{1,0:T(8,128)(2,1)S(1)} %get-tuple-element.23), channel_id=1, source_target_pairs={{0,7},{1,0},{2,1},{3,2},{4,3},{5,4},{6,5},{7,6},{8,15},{9,8},{10,9... | collective-permute-start | bytes 1806344 | tf_op jit(solution)/shard_map/ppermute | solution.py:593
  16.0 0.0 copy-done
  16.0 17.7 %inner.1 = (f32[8,3,2,48,128]{4,3,2,1,0:T(8,128)S(1)}, bf16[8,2,48,384]{3,2,1,0:T(8,128)(2,1)S(1)}, bf16[2,8,2,48,384]{4,3,2,1,0:T(8,128)(2,1)S(1)}, f32[8,24,128]{2,1,0:T(8,128)S(1)}, f32[8,24,128]{2,1,0:T(8,128)S(1)}) custom-call(bf16[2,24,4,3,16,128]{5,4,3,2,1,0:T(8,128)(2,1)S(1)} %bitcast.9, bf16[2,4,3,3,16,128]{5,4,3,2,1,0:T(8,128)(2,1)} %bitcast.14, ...), custom_call_target="tpu_custom_call" | custom-call | flops 40000000000 | bytes 6000000 | tf_op jit(solution)/shard_map/inner/pallas_call | solution.py:289
  33.8 0.0 collective-permute-done.face.ft
  33.8 1.4 %outer_t.1 = (f32[8,2,48,128]{3,2,1,0:T(8,128)S(1)}, f32[8,128]{1,0:T(8,128)S(1)}) custom-call(bf16[784,384]{1,0:T(8,128)(2,1)S(1)} %collective-permute-done.face.ft, bf16[8,2,48,384]{3,2,1,0:T(8,128)(2,1)S(1)} %get-tuple-element.19.refs_0_, f32[8,24,128]{2,1,0:T(8,128)S(1)} %get-tuple-element.20.refs_1_, f32[8,128]{1,0:T(8,128)S(1)} %get-tuple-element.21.refs_2_.vec), custom_call_target="tpu_custom_call" | custom-call | tf_op jit(solution)/shard_map/outer_t/pallas_call | solution.py:427
  35.1 0.0 collective-permute-start.2
  35.2 0.0 collective-permute-done.1.face.fz
  35.2 1.4 %outer_z.1 = (f32[8,2,48,128]{3,2,1,0:T(8,128)S(1)}, f32[8,128]{1,0:T(8,128)S(1)}) custom-call(bf16[784,384]{1,0:T(8,128)(2,1)S(1)} %collective-permute-done.1.face.fz, bf16[2,8,2,48,384]{4,3,2,1,0:T(8,128)(2,1)S(1)} %get-tuple-element.24.refs_0_, f32[8,24,128]{2,1,0:T(8,128)S(1)} %get-tuple-element.25.refs_1_, f32[8,128]{1,0:T(8,128)S(1)} %get-tuple-element.21.refs_2_.vec), custom_call_target="tpu_custom_call" | custom-call | tf_op jit(solution)/shard_map/outer_z/pallas_call | solution.py:427
  36.5 0.0 collective-permute-start.3
  36.6 2.0 %first.1.part = f32[8,128]{1,0:T(8,128)S(1)} custom-call(f32[8,3,2,48,128]{4,3,2,1,0:T(8,128)S(1)} %get-tuple-element.18.inner, f32[8,2,48,128]{3,2,1,0:T(8,128)S(1)} %get-tuple-element.22.outer_t, f32[8,2,48,128]{3,2,1,0:T(8,128)S(1)} %get-tuple-element.26.outer_z, f32[8,128]{1,0:T(8,128)S(1)} %get-tuple-element.21.refs_2_.vec, ...), custom_call_target="tpu_custom_call" | custom-call | tf_op jit(solution)/shard_map/first/pallas_call | solution.py:568
  38.5 1.7 %collective-permute-done.2.rt = f32[8,128]{1,0:T(8,128)S(1)} collective-permute-done((f32[8,128]{1,0:T(8,128)S(1)}, f32[8,128]{1,0:T(8,128)S(1)}, u32[]{:S(2)}, u32[]{:S(2)}) %collective-permute-start.2) | collective-permute-done | bytes 4128 | tf_op jit(solution)/shard_map/ppermute | solution.py:593
  40.3 3.5 %collective-permute-done.3.rz = f32[8,128]{1,0:T(8,128)S(1)} collective-permute-done((f32[8,128]{1,0:T(8,128)S(1)}, f32[8,128]{1,0:T(8,128)S(1)}, u32[]{:S(2)}, u32[]{:S(2)}) %collective-permute-start.3) | collective-permute-done | bytes 4128 | tf_op jit(solution)/shard_map/ppermute | solution.py:593
  43.8 0.6 back.1
  44.3 0.1 collective-permute-start.4
  44.4 0.1 collective-permute-start.5
  44.5 3.8 %collective-permute-start.6 = (f32[8,128]{1,0:T(8,128)S(1)}, f32[8,128]{1,0:T(8,128)S(1)}, u32[]{:S(2)}, u32[]{:S(2)}) collective-permute-start(f32[8,128]{1,0:T(8,128)S(1)} %get-tuple-element.29.vec), channel_id=1, source_target_pairs={{0,120},{8,0},{16,8},{24,16},{32,24},{40,32},{48,40},{56,48},{64,5... | collective-permute-start | bytes 12296 | tf_op jit(solution)/shard_map/ppermute | solution.py:593
  48.3 6.0 %collective-permute-start.7 = (f32[8,128]{1,0:T(8,128)S(1)}, f32[8,128]{1,0:T(8,128)S(1)}, u32[]{:S(2)}, u32[]{:S(2)}) collective-permute-start(f32[8,128]{1,0:T(8,128)S(1)} %get-tuple-element.29.vec), channel_id=1, source_target_pairs={{0,7},{1,0},{2,1},{3,2},{4,3},{5,4},{6,5},{7,6},{8,15},{9,8},{10,9... | collective-permute-start | bytes 12296 | tf_op jit(solution)/shard_map/ppermute | solution.py:593
  54.2 1.9 %blocks.1 = f32[5,8,4608]{2,1,0:T(8,128)} custom-call(f32[8,3,2,48,128]{4,3,2,1,0:T(8,128)S(1)} %get-tuple-element.18.inner, f32[8,2,48,128]{3,2,1,0:T(8,128)S(1)} %get-tuple-element.22.outer_t, f32[8,2,48,128]{3,2,1,0:T(8,128)S(1)} %get-tuple-element.26.outer_z), custom_call_target="tpu_custom_call" | custom-call | bytes 6000000 | tf_op jit(solution)/shard_map/blocks/pallas_call | solution.py:580
  56.2 0.9 %local.1.part = f32[8,128]{1,0:T(8,128)S(1)} custom-call(f32[8,3,2,48,128]{4,3,2,1,0:T(8,128)S(1)} %get-tuple-element.18.inner, f32[8,128]{1,0:T(8,128)S(1)} %get-tuple-element.29.vec), custom_call_target="tpu_custom_call" | custom-call | tf_op jit(solution)/shard_map/local/pallas_call | solution.py:568
  57.1 0.0 collective-permute-done.4.rt
  57.1 0.0 collective-permute-done.5.rz
  57.1 0.0 collective-permute-done.6.vt
  57.1 0.0 collective-permute-done.7.vz
  57.1 1.1 %last.1 = f32[8,96]{1,0:T(8,128)} custom-call(f32[8,2,48,128]{3,2,1,0:T(8,128)S(1)} %get-tuple-element.22.outer_t, f32[8,2,48,128]{3,2,1,0:T(8,128)S(1)} %get-tuple-element.26.outer_z, f32[8,128]{1,0:T(8,128)S(1)} %local.1.part, f32[8,128]{1,0:T(8,128)S(1)} %collective-permute-done.4.rt, f32[8,128]{1,0:T(8,128)S(1)} %collective-permute-done.5.rz, ...), custom_call_target="tpu_custom_call" | custom-call | tf_op jit(solution)/shard_map/last/pallas_call | solution.py:568
Async XLA Ops:
  3.7 12.4 %copy-start = (bf16[2,24,4,3,4,4,128]{6,5,4,3,2,1,0:T(4,128)(2,1)S(1)}, bf16[2,24,4,3,4,4,128]{6,5,4,3,2,1,0:T(4,128)(2,1)}, u32[]{:S(2)}) copy-start(bf16[2,24,4,3,4,4,128]{6,5,4,3,2,1,0:T(4,128)(2,1)} %param.3) | copy-start | bytes 7077892
  3.7 30.1 %collective-permute-start = (bf16[784,384]{1,0:T(8,128)(2,1)S(1)}, bf16[784,384]{1,0:T(8,128)(2,1)S(1)}, u32[]{:S(2)}, u32[]{:S(2)}) collective-permute-start(bf16[784,384]{1,0:T(8,128)(2,1)S(1)} %get-tuple-element.17.own_ref), channel_id=1, source_target_pairs={{0,120},{8,0},{16,8},{24,16},{32,24},{40,32},{48,40},{56,48},{64,5... | collective-permute-start | bytes 1806344 | tf_op jit(solution)/shard_map/ppermute | solution.py:593
  9.6 25.6 %collective-permute-start.1 = (bf16[784,384]{1,0:T(8,128)(2,1)S(1)}, bf16[784,384]{1,0:T(8,128)(2,1)S(1)}, u32[]{:S(2)}, u32[]{:S(2)}) collective-permute-start(bf16[784,384]{1,0:T(8,128)(2,1)S(1)} %get-tuple-element.23), channel_id=1, source_target_pairs={{0,7},{1,0},{2,1},{3,2},{4,3},{5,4},{6,5},{7,6},{8,15},{9,8},{10,9... | collective-permute-start | bytes 1806344 | tf_op jit(solution)/shard_map/ppermute | solution.py:593
  35.1 5.1 %collective-permute-start.2 = (f32[8,128]{1,0:T(8,128)S(1)}, f32[8,128]{1,0:T(8,128)S(1)}, u32[]{:S(2)}, u32[]{:S(2)}) collective-permute-start(f32[8,128]{1,0:T(8,128)S(1)} %get-tuple-element.27), channel_id=1, source_target_pairs={{0,8},{8,16},{16,24},{24,32},{32,40},{40,48},{48,56},{56,64},{64,7... | collective-permute-start | bytes 12296 | tf_op jit(solution)/shard_map/ppermute | solution.py:593
  36.5 7.2 %collective-permute-start.3 = (f32[8,128]{1,0:T(8,128)S(1)}, f32[8,128]{1,0:T(8,128)S(1)}, u32[]{:S(2)}, u32[]{:S(2)}) collective-permute-start(f32[8,128]{1,0:T(8,128)S(1)} %get-tuple-element.28), channel_id=1, source_target_pairs={{0,1},{1,2},{2,3},{3,4},{4,5},{5,6},{6,7},{7,0},{8,9},{9,10},{10,1... | collective-permute-start | bytes 12296 | tf_op jit(solution)/shard_map/ppermute | solution.py:593
  44.3 12.7 %collective-permute-start.4 = (f32[8,128]{1,0:T(8,128)S(1)}, f32[8,128]{1,0:T(8,128)S(1)}, u32[]{:S(2)}, u32[]{:S(2)}) collective-permute-start(f32[8,128]{1,0:T(8,128)S(1)} %get-tuple-element.30), channel_id=1, source_target_pairs={{0,8},{8,16},{16,24},{24,32},{32,40},{40,48},{48,56},{56,64},{64,7... | collective-permute-start | bytes 12296 | tf_op jit(solution)/shard_map/ppermute | solution.py:593
  44.4 12.7 %collective-permute-start.5 = (f32[8,128]{1,0:T(8,128)S(1)}, f32[8,128]{1,0:T(8,128)S(1)}, u32[]{:S(2)}, u32[]{:S(2)}) collective-permute-start(f32[8,128]{1,0:T(8,128)S(1)} %get-tuple-element.31), channel_id=1, source_target_pairs={{0,1},{1,2},{2,3},{3,4},{4,5},{5,6},{6,7},{7,0},{8,9},{9,10},{10,1... | collective-permute-start | bytes 12296 | tf_op jit(solution)/shard_map/ppermute | solution.py:593
  44.5 12.6 %collective-permute-start.6 = (f32[8,128]{1,0:T(8,128)S(1)}, f32[8,128]{1,0:T(8,128)S(1)}, u32[]{:S(2)}, u32[]{:S(2)}) collective-permute-start(f32[8,128]{1,0:T(8,128)S(1)} %get-tuple-element.29.vec), channel_id=1, source_target_pairs={{0,120},{8,0},{16,8},{24,16},{32,24},{40,32},{48,40},{56,48},{64,5... | collective-permute-start | bytes 12296 | tf_op jit(solution)/shard_map/ppermute | solution.py:593
  48.3 8.8 %collective-permute-start.7 = (f32[8,128]{1,0:T(8,128)S(1)}, f32[8,128]{1,0:T(8,128)S(1)}, u32[]{:S(2)}, u32[]{:S(2)}) collective-permute-start(f32[8,128]{1,0:T(8,128)S(1)} %get-tuple-element.29.vec), channel_id=1, source_target_pairs={{0,7},{1,0},{2,1},{3,2},{4,3},{5,4},{6,5},{7,6},{8,15},{9,8},{10,9... | collective-permute-start | bytes 12296 | tf_op jit(solution)/shard_map/ppermute | solution.py:593
